TPU v7x, 32 devices: a whole 2x2x4 slice. The times are simulated.
32 devices in a mesh: cell: 8 (over z, x), spec: 4 (over y, core).
Axes of the slice: x: 2, y: 2, z: 4, core: 2. Of those that a mesh axis runs over, the one named last changes fastest.
Arguments:
- fields: bfloat16 [4, 256, 384], P('spec', 'cell'), may hold values from -6 to 6
- tensors: bfloat16 [16, 384, 384, 384], P('spec', 'cell'), may hold values from -0.0078125 to 0.0078125
- pair_table: int32 [4, 4], replicated, may hold values from 0 to 15, as said below
- plus_flux: float32 [4, 384, 384], P('spec'), may hold values from -0.3125 to 0.3125
- minus_flux: float32 [4, 384, 384], P('spec'), may hold values from -0.3125 to 0.3125
- face_limiter: int32 [4, 256], P('spec', 'cell'), may hold values from 0 to 2
Outputs:
- new_field: float32 [4, 256, 384], P('spec', 'cell')
- collision: float32 [4, 256, 384], P('spec', 'cell')
Inputs may be any that keep to these rules, and one draw needn't show every extreme that they name: Row s of pair_table names each of the tensors s * 4 to s * 4 + 3 exactly once. `face_limiter`: 0 first order, 1 minmod slope, 2 monotonized central slope.
All inputs are finite; a program needn't handle non-finite values.
Results may differ from a plain program's by a relative error of at most 0.0004.
Values may be sent and summed in bfloat16 or wider, within the bound.
No kernel may reach another device: no remote copies, remote signals or barrier semaphores. Data moves between devices by JAX's collectives and lax.ppermute only.
A program may use at most 128 MiB of HBM per device.

v0:
```python
import jax
import jax.numpy as jnp
from jax import lax
from jax.sharding import PartitionSpec as P


def shifted(x, axis, by):
    size = lax.axis_size(axis)
    return lax.ppermute(x, axis, [(i, (i + by) % size) for i in range(size)])


def minmod_two(first, second):
    return jnp.where(
        first * second > 0, jnp.sign(first) * jnp.minimum(jnp.abs(first), jnp.abs(second)), 0.0
    )


def minmod_three(first, second, third):
    same = (first * second > 0) & (second * third > 0)
    least = jnp.minimum(jnp.minimum(jnp.abs(first), jnp.abs(second)), jnp.abs(third))
    return jnp.where(same, jnp.sign(first) * least, 0.0)


def local(fields, tensors, pair_table, plus_flux, minus_flux, face_limiter):
    cells = fields.shape[1]
    species = lax.axis_size("spec")
    owner = lax.axis_index("spec")
    position = lax.axis_index("cell")
    total_cells = cells * lax.axis_size("cell")
    out_modes = tensors.shape[1]
    table_row = lax.dynamic_index_in_dim(pair_table, owner, 0, keepdims=False)
    all_species = lax.all_gather(fields, "spec", axis=0, tiled=True)
    gathered = lax.all_gather(all_species, "cell", axis=1, tiled=True)
    own_rows = lax.dynamic_index_in_dim(gathered, owner, 0, keepdims=True)
    own_wide = own_rows[0].astype(jnp.float32)
    collision_part = jnp.zeros((total_cells, out_modes), jnp.float32)
    for partner in range(species):
        partner_rows = gathered[partner]
        local_pair = table_row[partner] - owner * species
        tensor = lax.dynamic_index_in_dim(tensors, local_pair, 0, keepdims=False)
        inner = jnp.einsum("cj,kij->cki", partner_rows, tensor, preferred_element_type=jnp.float32)
        collision_part = collision_part + jnp.einsum(
            "cki,ci->ck",
            inner,
            own_wide,
            precision=lax.Precision.HIGHEST,
            preferred_element_type=jnp.float32,
        )
    collision = lax.all_to_all(collision_part, "cell", split_axis=0, concat_axis=1, tiled=True)
    padded = jnp.concatenate([own_rows[:, -2:], own_rows, own_rows[:, :2]], axis=1)
    extended = lax.dynamic_slice_in_dim(padded, position * cells, cells + 4, 1)
    wide = extended[0].astype(jnp.float32)
    prior_flag = shifted(face_limiter[:, -1:], "cell", 1)
    flags = jnp.concatenate([prior_flag, face_limiter], axis=1)[0][:, None]
    lower = wide[1:-1] - wide[:-2]
    upper = wide[2:] - wide[1:-1]
    slope_one = minmod_two(lower, upper)
    slope_two = minmod_three(2.0 * lower, 0.5 * (lower + upper), 2.0 * upper)
    zero = jnp.zeros((cells + 1, wide.shape[1]), jnp.float32)
    here = jnp.where(flags == 1, slope_one[:-1], jnp.where(flags == 2, slope_two[:-1], zero))
    there = jnp.where(flags == 1, slope_one[1:], jnp.where(flags == 2, slope_two[1:], zero))
    left_state = wide[1 : cells + 2] + 0.5 * here
    right_state = wide[2 : cells + 3] - 0.5 * there
    flux = jnp.dot(
        left_state,
        plus_flux[0],
        precision=lax.Precision.HIGHEST,
        preferred_element_type=jnp.float32,
    )
    flux = flux + jnp.dot(
        right_state,
        minus_flux[0],
        precision=lax.Precision.HIGHEST,
        preferred_element_type=jnp.float32,
    )
    center = wide[2 : cells + 2]
    new_field = center + 0.4 * (flux[:-1] - flux[1:]) + 0.5 * collision
    return (new_field[None], collision[None])


def solution(mesh):
    placed = (
        P("spec", "cell", None),
        P("spec", "cell", None, None),
        P(),
        P("spec", None, None),
        P("spec", None, None),
        P("spec", "cell"),
    )
    return jax.shard_map(
        local,
        mesh=mesh,
        in_specs=placed,
        out_specs=(P("spec", "cell", None), P("spec", "cell", None)),
        check_vma=False,
    )
```

profile of v0, /device:TPU:0, one launch (start us, length us, event | category | flops | bytes accessed | tf_op | source)
XLA Modules:
  0.0 95.2 jit_solution(4871820601077643029)
XLA Ops:
  0.6 1.4 %slice.92 = s32[1,1]{1,0:T(1,128)} slice(s32[1,32]{1,0:T(1,128)} %param.11), slice={[0:1], [31:32]} | slice | bytes 8 | tf_op jit(solution)/shard_map/slice | solution.py:53
  2.0 2.9 %collective-permute-start = (s32[1,1]{1,0:T(1,128)}, s32[1,1]{1,0:T(1,128)}, u32[]{:S(2)}, u32[]{:S(2)}) collective-permute-start(s32[1,1]{1,0:T(1,128)} %slice.92), channel_id=1, source_target_pairs={{0,4},{4,8},{8,12},{12,16},{16,20},{20,24},{24,28},{28,0},{1,5},{5... | collective-permute-start | bytes 20 | tf_op jit(solution)/shard_map/ppermute | solution.py:9
  5.0 0.7 constant_dynamic-slice_fusion.2
  5.6 0.6 fusion.61
  8.8 5.5 %all_gather.6 = bf16[4,32,384]{2,1,0:T(8,128)(2,1)S(1)} all-gather(bf16[1,32,384]{2,1,0:T(8,128)(2,1)} %param.6), channel_id=1, replica_groups=mesh['cell'=8,'spec'=4] {'spec'}, dimensions={0}, use_global_device_ids=true | all-gather | bytes 122880 | tf_op jit(solution)/shard_map/all_gather | solution.py:32
  14.4 32.5 %all_gather.7 = bf16[4,256,384]{2,1,0:T(8,128)(2,1)S(1)} all-gather(bf16[4,32,384]{2,1,0:T(8,128)(2,1)S(1)} %all_gather.6), channel_id=1, replica_groups=mesh['cell'=8,'spec'=4] {'cell'}, dimensions={1}, use_global_device_ids=true | all-gather | bytes 884736 | tf_op jit(solution)/shard_map/all_gather | solution.py:33
  47.0 0.2 copy.39
  47.1 8.3 %fusion.2 = f32[256,48]{0,1:T(8,128)S(1)} fusion(f32[256,384]{0,1:T(8,128)S(1)} %copy.39, bf16[4,48,384,384]{3,2,1,0:T(8,128)(2,1)} %param.7, s32[]{:T(128)S(6)} %select_n.51, bf16[4,256,384]{2,1,0:T(8,128)(2,1)S(1)} %all_gather.7), kind=kOutput, calls=%fused_computation.5 | convolution fusion | flops 3633303552 | bytes 14794756 | tf_op jit(solution)/shard_map/cj,kij->cki/dot_general | solution.py:41
  55.5 8.4 %fusion.3 = f32[256,48]{0,1:T(8,128)S(1)} fusion(f32[256,384]{0,1:T(8,128)S(1)} %copy.39, bf16[4,48,384,384]{3,2,1,0:T(8,128)(2,1)} %param.7, s32[]{:T(128)S(6)} %select_n.50, bf16[4,256,384]{2,1,0:T(8,128)(2,1)S(1)} %all_gather.7), kind=kOutput, calls=%fused_computation.7 | convolution fusion | flops 3633303552 | bytes 14794756 | tf_op jit(solution)/shard_map/cj,kij->cki/dot_general | solution.py:41
  63.9 8.3 %fusion.1 = f32[256,48]{0,1:T(8,128)S(1)} fusion(f32[256,384]{0,1:T(8,128)S(1)} %copy.39, bf16[4,48,384,384]{3,2,1,0:T(8,128)(2,1)} %param.7, s32[]{:T(128)S(6)} %select_n.52, bf16[4,256,384]{2,1,0:T(8,128)(2,1)S(1)} %all_gather.7), kind=kOutput, calls=%fused_computation.3 | convolution fusion | flops 3633303552 | bytes 14794756 | tf_op jit(solution)/shard_map/cj,kij->cki/dot_general | solution.py:41
  72.3 8.4 %fusion = f32[256,48]{0,1:T(8,128)S(1)} fusion(f32[256,384]{0,1:T(8,128)S(1)} %copy.39, bf16[4,48,384,384]{3,2,1,0:T(8,128)(2,1)} %param.7, s32[]{:T(128)S(6)} %select_n.53, bf16[4,256,384]{2,1,0:T(8,128)(2,1)S(1)} %all_gather.7), kind=kOutput, calls=%fused_computation.1 | convolution fusion | flops 3633303552 | bytes 14794756 | tf_op jit(solution)/shard_map/cj,kij->cki/dot_general | solution.py:41
  80.7 0.1 copy.38
  80.8 0.8 reshape.94
  81.6 3.8 %all-to-all-start = ((f32[8,1,1536]{2,1,0:T(1,128)}), f32[8,1,1536]{2,1,0:T(1,128)S(1)}, u32[]{:S(2)}, u32[]{:S(2)}) async-start(f32[8,1,1536]{2,1,0:T(1,128)} %reshape.94), calls=%async_computation | async-start | bytes 98304 | tf_op jit(solution)/shard_map/all_to_all | solution.py:49
  85.6 0.6 compare_bitcast_fusion.1
  86.2 0.5 fusion.25
  86.7 0.5 convolution_add_fusion
  87.2 5.0 %all-to-all-done = f32[8,1,1536]{2,1,0:T(1,128)S(1)} async-done(((f32[8,1,1536]{2,1,0:T(1,128)}), f32[8,1,1536]{2,1,0:T(1,128)S(1)}, u32[]{:S(2)}, u32[]{:S(2)}) %all-to-all-start) | async-done | bytes 49184 | tf_op jit(solution)/shard_map/all_to_all | solution.py:49
  92.2 0.5 broadcast.69
  92.7 0.8 reduce.8
  93.5 0.1 reshape.95
  93.7 0.1 mul.87
  93.9 0.7 broadcast_in_dim.35
  94.6 0.6 fusion.41
  (15 shorter events, 0.4 us)
Async XLA Ops:
  0.6 85.6 %copy-start = (f32[1,384,384]{2,1,0:T(8,128)S(1)}, f32[1,384,384]{2,1,0:T(8,128)}, u32[]{:S(2)}) copy-start(f32[1,384,384]{2,1,0:T(8,128)} %param.9) | copy-start | bytes 1769476
  2.0 83.5 %collective-permute-start = (s32[1,1]{1,0:T(1,128)}, s32[1,1]{1,0:T(1,128)}, u32[]{:S(2)}, u32[]{:S(2)}) collective-permute-start(s32[1,1]{1,0:T(1,128)} %slice.92), channel_id=1, source_target_pairs={{0,4},{4,8},{8,12},{12,16},{16,20},{20,24},{24,28},{28,0},{1,5},{5... | collective-permute-start | bytes 20 | tf_op jit(solution)/shard_map/ppermute | solution.py:9
  72.2 13.3 %copy-start.2 = (s32[1,32]{1,0:T(1,128)S(1)}, s32[1,32]{1,0:T(1,128)}, u32[]{:S(2)}) copy-start(s32[1,32]{1,0:T(1,128)} %param.11) | copy-start | bytes 388
  72.2 14.4 %copy-start.1 = (f32[1,384,384]{2,1,0:T(8,128)S(1)}, f32[1,384,384]{2,1,0:T(8,128)}, u32[]{:S(2)}) copy-start(f32[1,384,384]{2,1,0:T(8,128)} %param.10) | copy-start | bytes 1769476
  81.6 10.6 %all-to-all-start = ((f32[8,1,1536]{2,1,0:T(1,128)}), f32[8,1,1536]{2,1,0:T(1,128)S(1)}, u32[]{:S(2)}, u32[]{:S(2)}) async-start(f32[8,1,1536]{2,1,0:T(1,128)} %reshape.94), calls=%async_computation | async-start | bytes 98304 | tf_op jit(solution)/shard_map/all_to_all | solution.py:49
where the time goes:
time: 95.5 us; the launch traced here: 95.2 us
  blocking collectives  38.1 us (40%)
  matrix products  34.4 us (36%)
  starting transfers between devices  6.76 us (7%)
  local copies, waits for them, and re-layouts  5.34 us (6%)
  waiting for transfers between devices  5.03 us (5%)
  between operations  3.4 us (4%)
  other arithmetic  2.24 us (2%)
    dot_general x4, matrix products, local(): jnp.einsum('cj,kij->cki', partner_rows, tensor, preferred_element_type=jn...  33.5 us
    all_gather x1, blocking collectives, local(): gathered = lax.all_gather(all_species, 'cell', axis=1, tiled=True)  32.5 us
    all_gather x1, blocking collectives, local(): all_species = lax.all_gather(fields, 'spec', axis=0, tiled=True)  5.55 us
    all_to_all x1, waiting for transfers between devices, local(): lax.all_to_all(collision_part, 'cell', split_axis=0, concat_axis=1, tiled...  5.03 us
    all_to_all x1, starting transfers between devices, local(): lax.all_to_all(collision_part, 'cell', split_axis=0, concat_axis=1, tiled...  3.82 us
    ppermute x1, starting transfers between devices, shifted(): return lax.ppermute(x, axis, [(i, (i + by) % size) for i in range(size)])  2.94 us
  transfers between devices with their start and end apart: 2, of which 1 were waited for; matrix products, arithmetic and copies ran while one was open for 39% of the time, Pallas kernels for 0%

commit v1 on v0

v1 whole, which is shorter than its diff:
```python
import functools

import jax
import jax.numpy as jnp
from jax import lax
from jax.experimental import pallas as pl
from jax.experimental.pallas import tpu as pltpu
from jax.sharding import PartitionSpec as P

LANES = 128
MIB = 1 << 20


def minmod_two(first, second):
    least = jnp.minimum(jnp.abs(first), jnp.abs(second))
    return jnp.where(first * second > 0, jnp.where(first > 0, least, -least), 0.0)


def minmod_three(first, second, third):
    same = (first * second > 0) & (second * third > 0)
    least = jnp.minimum(jnp.minimum(jnp.abs(first), jnp.abs(second)), jnp.abs(third))
    return jnp.where(same, jnp.where(first > 0, least, -least), 0.0)


def column(row):
    n = row.shape[1]
    down = lax.broadcasted_iota(jnp.int32, (n, n), 0)
    across = lax.broadcasted_iota(jnp.int32, (n, n), 1)
    return jnp.sum(jnp.where(down == across, row, 0), axis=1, keepdims=True)


def fold_of(cells, out_modes):
    fold = 1
    while cells % (2 * fold) == 0 and 2 * fold * out_modes < LANES:
        fold *= 2
    return fold


def collide_kernel(place, order, gathered, tensors, limiter, out, other, own, total):
    step = pl.program_id(0)
    groups, species, cells, modes = gathered.shape
    block = tensors.shape[1]

    @pl.when(step == 0)
    def _():
        for p in range(species):
            rows = gathered[:, pl.ds(order[p], 1)].reshape(groups * cells, modes)
            other[p * modes : (p + 1) * modes, :] = rows.astype(jnp.float32).T.astype(other.dtype)
        rows = gathered[:, pl.ds(place[1], 1)].reshape(groups * cells, modes)
        own[...] = rows.astype(jnp.float32).T

    for k in range(block):
        left = jnp.concatenate([tensors[p, k] for p in range(species)], axis=1)
        inner = jnp.dot(left, other[...], preferred_element_type=jnp.float32)
        total[pl.ds(step * block + k, 1), :] = jnp.sum(inner * own[...], axis=0, keepdims=True)

    @pl.when(step == pl.num_programs(0) - 1)
    def _():
        whole = total[...].T
        out_modes = whole.shape[1]
        fold = fold_of(cells, out_modes)
        rows = cells // fold
        flag = limiter[:, cells - 1 :].astype(jnp.float32)
        spare = jnp.broadcast_to(flag, (rows, LANES - fold * out_modes))
        for d in range(groups):
            first = d * cells
            parts = [whole[first + f * rows : first + (f + 1) * rows] for f in range(fold)]
            out[d] = jnp.concatenate(parts + [spare], axis=1)


def collide(place, order, gathered, tensors, limiter):
    groups, species, cells, modes = gathered.shape
    out_modes = tensors.shape[1]
    rows = cells // fold_of(cells, out_modes)
    block = 2 if out_modes % 2 == 0 else 1
    return pl.pallas_call(
        collide_kernel,
        grid_spec=pltpu.PrefetchScalarGridSpec(
            num_scalar_prefetch=2,
            grid=(out_modes // block,),
            in_specs=[
                pl.BlockSpec(memory_space=pltpu.VMEM),
                pl.BlockSpec((species, block, modes, modes), lambda step, *_: (0, step, 0, 0)),
                pl.BlockSpec(memory_space=pltpu.VMEM),
            ],
            out_specs=pl.BlockSpec(memory_space=pltpu.VMEM),
            scratch_shapes=[
                pltpu.VMEM((species * modes, groups * cells), jnp.bfloat16),
                pltpu.VMEM((modes, groups * cells), jnp.float32),
                pltpu.VMEM((out_modes, groups * cells), jnp.float32),
            ],
        ),
        out_shape=jax.ShapeDtypeStruct((groups, rows, LANES), jnp.float32),
        compiler_params=pltpu.CompilerParams(vmem_limit_bytes=32 * MIB),
        name="collide",
    )(place, order, gathered, tensors, limiter)


def flux_kernel(place, gathered, limiter, plus, minus, flux):
    groups, species, cells, modes = gathered.shape
    here, owner = place[0], place[1]
    before = lax.rem(here + groups - 1, groups)
    after = lax.rem(here + 1, groups)
    wide = jnp.concatenate(
        [gathered[g, owner].astype(jnp.float32) for g in (before, here, after)], axis=0
    )
    wide = wide[cells - 2 : 2 * cells + 2]
    lower = wide[1:-1] - wide[:-2]
    upper = wide[2:] - wide[1:-1]
    one = minmod_two(lower, upper)
    two = minmod_three(2.0 * lower, 0.5 * (lower + upper), 2.0 * upper)
    flags = column(limiter[...])
    ahead = lax.broadcasted_iota(jnp.int32, (3, 1), 0)

    def chosen(first, second, flag):
        return jnp.where(flag == 1, first, jnp.where(flag == 2, second, 0.0))

    def stack(shift):
        base = wide[1 + shift :]
        faces = base[1 : cells + 1]
        faces = faces + (0.5 - shift) * chosen(
            one[1 + shift : 1 + shift + cells], two[1 + shift : 1 + shift + cells], flags
        )
        edge = base[:1] + (0.5 - shift) * chosen(
            one[shift : shift + 1], two[shift : shift + 1], ahead
        )
        pad = jnp.zeros((flux.shape[0] - cells - 3, modes), jnp.float32)
        return jnp.concatenate([faces, edge, pad], axis=0)

    total = jnp.dot(
        stack(0), plus[0], precision=lax.Precision.HIGHEST, preferred_element_type=jnp.float32
    )
    total = total + jnp.dot(
        stack(1), minus[0], precision=lax.Precision.HIGHEST, preferred_element_type=jnp.float32
    )
    flux[...] = total


def transport(place, gathered, limiter, plus, minus):
    groups, species, cells, modes = gathered.shape
    vmem = pl.BlockSpec(memory_space=pltpu.VMEM)
    return pl.pallas_call(
        flux_kernel,
        in_specs=[pl.BlockSpec(memory_space=pltpu.SMEM), vmem, vmem, vmem, vmem],
        out_specs=vmem,
        out_shape=jax.ShapeDtypeStruct((cells + 8, modes), jnp.float32),
        compiler_params=pltpu.CompilerParams(vmem_limit_bytes=16 * MIB),
        name="transport",
    )(place, gathered, limiter, plus, minus)


def finish_kernel(out_modes, place, received, flux, fields, new_field, collision):
    groups, rows, _ = received.shape
    cells = fields.shape[1]
    fold = cells // rows
    parts = []
    for f in range(fold):
        pieces = [received[g][:, f * out_modes : (f + 1) * out_modes] for g in range(groups)]
        parts.append(jnp.concatenate(pieces, axis=1))
    term = jnp.concatenate(parts, axis=0)
    collision[0] = term
    before = lax.rem(place[0] + groups - 1, groups)
    flag = received[before][:1, fold * out_modes : fold * out_modes + 1]
    behind = flux[cells : cells + 3]
    edge = jnp.where(flag == 1.0, behind[1:2], jnp.where(flag == 2.0, behind[2:3], behind[:1]))
    faces = flux[:cells]
    ahead = jnp.concatenate([edge, faces[:-1]], axis=0)
    new_field[0] = fields[0].astype(jnp.float32) + 0.4 * (ahead - faces) + 0.5 * term


def finish(place, received, flux, fields, out_modes):
    vmem = pl.BlockSpec(memory_space=pltpu.VMEM)
    shape = jax.ShapeDtypeStruct(fields.shape, jnp.float32)
    return pl.pallas_call(
        functools.partial(finish_kernel, out_modes),
        in_specs=[pl.BlockSpec(memory_space=pltpu.SMEM), vmem, vmem, vmem],
        out_specs=(vmem, vmem),
        out_shape=(shape, shape),
        compiler_params=pltpu.CompilerParams(vmem_limit_bytes=16 * MIB),
        name="finish",
    )(place, received, flux, fields)


def local(fields, tensors, pair_table, plus_flux, minus_flux, face_limiter):
    species = lax.axis_size("spec")
    owner = lax.axis_index("spec")
    position = lax.axis_index("cell")
    place = jnp.stack([position, owner]).astype(jnp.int32)
    row = lax.dynamic_index_in_dim(pair_table, owner, 0, keepdims=False) - owner * species
    order = jnp.sum(
        jnp.where(row[None, :] == jnp.arange(species)[:, None], jnp.arange(species)[None, :], 0),
        axis=1,
        dtype=jnp.int32,
    )
    everyone = lax.all_gather(fields[0], ("cell", "spec"), axis=0, tiled=False)
    gathered = everyone.reshape((lax.axis_size("cell"), species) + fields.shape[1:])
    block = collide(place, order, gathered, tensors, face_limiter)
    received = lax.all_to_all(block, "cell", split_axis=0, concat_axis=0, tiled=False)
    flux = transport(place, gathered, face_limiter, plus_flux, minus_flux)
    return finish(place, received, flux, fields, tensors.shape[1])


def solution(mesh):
    placed = (
        P("spec", "cell", None),
        P("spec", "cell", None, None),
        P(),
        P("spec", None, None),
        P("spec", None, None),
        P("spec", "cell"),
    )
    return jax.shard_map(
        local,
        mesh=mesh,
        in_specs=placed,
        out_specs=(P("spec", "cell", None), P("spec", "cell", None)),
        check_vma=False,
    )
```

time: 95.5 us -> 93.6 us (0.980)
  Pallas kernels: 0 us -> 36.2 us
  matrix products: 34.4 us -> 0 us
  blocking collectives: 38.1 us -> 45.6 us
  local copies, waits for them, and re-layouts: 5.34 us -> 0.67 us
  starting transfers between devices: 6.76 us -> 3.35 us
  between operations: 3.4 us -> 0.7 us
  other arithmetic: 2.24 us -> 0.98 us
    pallas_call x0 -> x3, Pallas kernels: none -> 36.2 us  [the longest x1 33.6 us: collide(): pl.pallas_call(collide_kernel, grid_spec=pltpu.PrefetchScalarGridSpec(num...]
    dot_general x6 -> x0, matrix products: 34.4 us -> none  [the longest x4 33.5 us: local(): jnp.einsum('cj,kij->cki', partner_rows, tensor, preferred_element_type=jn...]
    all_gather x2 -> x1, blocking collectives: 38.1 us -> 45.6 us  [local(): everyone = lax.all_gather(fields[0], ('cell', 'spec'), axis=0, tiled=False)]
    ppermute x1 -> x0, starting transfers between devices: 2.94 us -> none  [shifted(): return lax.ppermute(x, axis, [(i, (i + by) % size) for i in range(size)])]
    slice x3 -> x0, local copies, waits for them, and re-layouts: 2 us -> none  [the longest x1 1.38 us: local(): prior_flag = shifted(face_limiter[:, -1:], 'cell', 1)]
  transfers between devices with their start and end apart: 2 -> 1, of which waited for: 1 -> 1; matrix products, arithmetic and copies ran while one was open for 39% -> 0% of each run, Pallas kernels for 0% -> 1%
where the time goes in v1:
time: 93.6 us; the launch traced here: 93 us
  blocking collectives  45.6 us (49%)
  Pallas kernels  36.2 us (39%)
  waiting for transfers between devices  5.47 us (6%)
  starting transfers between devices  3.35 us (4%)
  other arithmetic  0.98 us (1%)
    all_gather x1, blocking collectives, local(): everyone = lax.all_gather(fields[0], ('cell', 'spec'), axis=0, tiled=False)  45.6 us
    pallas_call x1, Pallas kernels, collide(): pl.pallas_call(collide_kernel, grid_spec=pltpu.PrefetchScalarGridSpec(num...  33.6 us
    all_to_all x1, waiting for transfers between devices, local(): lax.all_to_all(block, 'cell', split_axis=0, concat_axis=0, tiled=False)  5.47 us
    all_to_all x1, starting transfers between devices, local(): lax.all_to_all(block, 'cell', split_axis=0, concat_axis=0, tiled=False)  3.35 us
  transfers between devices with their start and end apart: 1, of which 1 were waited for; matrix products, arithmetic and copies ran while one was open for 0% of the time, Pallas kernels for 1%

profile of v1, /device:TPU:0, one launch (start us, length us, event | category | flops | bytes accessed | tf_op | source)
XLA Modules:
  0.0 93.0 jit_solution(6767003758449215373)
XLA Ops:
  0.6 0.0 copy-start.2
  0.6 0.0 copy-start.1
  0.7 0.0 copy-start
  0.7 0.8 subtract_bitcast_fusion
  1.5 0.1 select_reduce_fusion.order
  1.6 45.6 %all_gather.3 = bf16[32,32,384]{2,1,0:T(8,128)(2,1)S(1)} all-gather(bf16[1,32,384]{2,1,0:T(8,128)(2,1)} %fields.1), channel_id=1, replica_groups=mesh['cell'=8,'spec'=4] {'cell','spec'}, dimensions={0}, use_global_device_ids=true | all-gather | bytes 811008 | tf_op jit(solution)/shard_map/all_gather | solution.py:195
  47.2 0.1 pad_add_fusion.place
  47.2 0.0 copy-start.3
  47.3 0.7 copy-done.3
  47.9 0.0 copy-start.4
  47.9 33.6 %collide.1 = f32[8,16,128]{2,1,0:T(8,128)} custom-call(s32[2]{0:T(128)S(1)} %pad_add_fusion.place, s32[4]{0:T(128)S(1)} %select_reduce_fusion.order, bf16[8,4,32,384]{3,2,1,0:T(8,128)(2,1)S(1)} %bitcast.5, bf16[4,48,384,384]{3,2,1,0:T(8,128)(2,1)} %tensors.1, s32[1,32]{1,0:T(1,128)S(1)} %copy-done.3), custom_call_target="tpu_custom_call" | custom-call | tf_op jit(solution)/shard_map/collide/pallas_call | solution.py:76
  81.5 3.3 %all-to-all-start = ((f32[8,16,128]{2,1,0:T(8,128)}), f32[8,16,128]{2,1,0:T(8,128)S(1)}, u32[]{:S(2)}, u32[]{:S(2)}) async-start(f32[8,16,128]{2,1,0:T(8,128)} %collide.1), calls=%async_computation | async-start | bytes 131072 | tf_op jit(solution)/shard_map/all_to_all | solution.py:198
  84.9 0.0 copy-done.1
  84.9 0.0 copy-done
  84.9 0.0 copy-done.4
  84.9 1.3 %transport.1.flux = f32[40,384]{1,0:T(8,128)S(1)} custom-call(s32[2]{0:T(128)S(1)} %pad_add_fusion.place, bf16[8,4,32,384]{3,2,1,0:T(8,128)(2,1)S(1)} %bitcast.6, s32[1,32]{1,0:T(1,128)S(1)} %copy-done.4, f32[1,384,384]{2,1,0:T(8,128)S(1)} %copy-done, f32[1,384,384]{2,1,0:T(8,128)S(1)} %copy-done.1), custom_call_target="tpu_custom_call" | custom-call | tf_op jit(solution)/shard_map/transport/pallas_call | solution.py:142
  86.2 5.5 %all-to-all-done.received = f32[8,16,128]{2,1,0:T(8,128)S(1)} async-done(((f32[8,16,128]{2,1,0:T(8,128)}), f32[8,16,128]{2,1,0:T(8,128)S(1)}, u32[]{:S(2)}, u32[]{:S(2)}) %all-to-all-start) | async-done | bytes 65568 | tf_op jit(solution)/shard_map/all_to_all | solution.py:198
  91.7 0.0 copy-done.2
  91.7 1.3 %finish.1 = (f32[1,32,384]{2,1,0:T(8,128)}, f32[1,32,384]{2,1,0:T(8,128)}) custom-call(s32[2]{0:T(128)S(1)} %pad_add_fusion.place, f32[8,16,128]{2,1,0:T(8,128)S(1)} %all-to-all-done.received, f32[40,384]{1,0:T(8,128)S(1)} %transport.1.flux, bf16[1,32,384]{2,1,0:T(8,128)(2,1)S(1)} %copy-done.2), custom_call_target="tpu_custom_call" | custom-call | tf_op jit(solution)/shard_map/finish/pallas_call | solution.py:174
Async XLA Ops:
  0.6 91.1 %copy-start.2 = (bf16[1,32,384]{2,1,0:T(8,128)(2,1)S(1)}, bf16[1,32,384]{2,1,0:T(8,128)(2,1)}, u32[]{:S(2)}) copy-start(bf16[1,32,384]{2,1,0:T(8,128)(2,1)} %fields.1) | copy-start | bytes 73732
  0.6 84.2 %copy-start.1 = (f32[1,384,384]{2,1,0:T(8,128)S(1)}, f32[1,384,384]{2,1,0:T(8,128)}, u32[]{:S(2)}) copy-start(f32[1,384,384]{2,1,0:T(8,128)} %minus.1) | copy-start | bytes 1769476
  0.7 84.2 %copy-start = (f32[1,384,384]{2,1,0:T(8,128)S(1)}, f32[1,384,384]{2,1,0:T(8,128)}, u32[]{:S(2)}) copy-start(f32[1,384,384]{2,1,0:T(8,128)} %plus.1) | copy-start | bytes 1769476
  47.2 0.7 copy-start.3
  47.9 37.0 %copy-start.4 = (s32[1,32]{1,0:T(1,128)S(1)}, s32[1,32]{1,0:T(1,128)}, u32[]{:S(2)}) copy-start(s32[1,32]{1,0:T(1,128)} %limiter.3) | copy-start | bytes 388
  81.5 10.2 %all-to-all-start = ((f32[8,16,128]{2,1,0:T(8,128)}), f32[8,16,128]{2,1,0:T(8,128)S(1)}, u32[]{:S(2)}, u32[]{:S(2)}) async-start(f32[8,16,128]{2,1,0:T(8,128)} %collide.1), calls=%async_computation | async-start | bytes 131072 | tf_op jit(solution)/shard_map/all_to_all | solution.py:198

commit v2 on v1

v2 whole, which is shorter than its diff:
```python
import functools

import jax
import jax.numpy as jnp
from jax import lax
from jax.experimental import pallas as pl
from jax.experimental.pallas import tpu as pltpu
from jax.sharding import PartitionSpec as P

LANES = 128
MIB = 1 << 20


def minmod_two(first, second):
    least = jnp.minimum(jnp.abs(first), jnp.abs(second))
    return jnp.where(first * second > 0, jnp.where(first > 0, least, -least), 0.0)


def minmod_three(first, second, third):
    same = (first * second > 0) & (second * third > 0)
    least = jnp.minimum(jnp.minimum(jnp.abs(first), jnp.abs(second)), jnp.abs(third))
    return jnp.where(same, jnp.where(first > 0, least, -least), 0.0)


def column(row):
    n = row.shape[1]
    down = lax.broadcasted_iota(jnp.int32, (n, n), 0)
    across = lax.broadcasted_iota(jnp.int32, (n, n), 1)
    return jnp.sum(jnp.where(down == across, row, 0), axis=1, keepdims=True)


def fold_of(cells, out_modes):
    fold = 1
    while cells % (2 * fold) == 0 and 2 * fold * out_modes < LANES:
        fold *= 2
    return fold


def collide_kernel(
    table, *refs, species
):
    spread = refs[:species]
    tensors, limiter, out, other, own, total = refs[species:]
    step = pl.program_id(0)
    groups, cells, modes = spread[0].shape
    block = tensors.shape[1]
    everyone = groups * cells
    width = 2 * LANES
    owner = lax.axis_index("spec")

    @pl.when(step == 0)
    def _():
        for q in range(species):
            p = table[owner, owner ^ q] - owner * species
            other[p] = spread[q][...].reshape(everyone, modes)
        own[...] = spread[0][...].reshape(everyone, modes).astype(jnp.float32).T

    def strip(ref, lead, rows, tile):
        parts = []
        for piece in range(2 * tile, 2 * tile + 2):
            p, lane = piece * LANES // modes, piece * LANES % modes
            parts.append(ref[(p,) + lead + (rows, slice(lane, lane + LANES))])
        return jnp.concatenate(parts, axis=1)

    tiles = species * modes // width
    units = [(k, n) for k in range(block) for n in range(everyone // width)]
    pending = []

    def drain():
        while pending:
            acc, k, n = pending.pop(0)
            columns = slice(n * width, (n + 1) * width)
            inner = pltpu.matmul_pop(acc)
            row = jnp.sum(inner * own[:, columns], axis=0, keepdims=True)
            total[pl.ds(step * block + k, 1), columns] = row

    def multiply(*sums):
        for at in range(0, len(units), 2):
            pair = units[at : at + 2]

            def push(tile):
                for unit, (k, n) in enumerate(pair):
                    rows = slice(n * width, (n + 1) * width)
                    pltpu.matmul_push_rhs(strip(other, (), rows, tile), tile % 2, unit, transpose=True)

            push(0)
            for tile in range(tiles):
                if tile + 1 < tiles:
                    push(tile + 1)
                for unit, (k, n) in enumerate(pair):
                    acc = sums[2 * unit + (at // 2) % 2]
                    pltpu.matmul_acc_lhs(acc, strip(tensors, (k,), slice(None), tile), tile % 2)
                if tile == 0:
                    drain()
            for unit, (k, n) in enumerate(pair):
                pending.append((sums[2 * unit + (at // 2) % 2], k, n))
        drain()

    pl.run_scoped(
        multiply, *[pltpu.ACC(unit)((modes, width), jnp.float32) for unit in (0, 0, 1, 1)]
    )

    @pl.when(step == pl.num_programs(0) - 1)
    def _():
        here = lax.axis_index("cell")
        whole = total[...].T
        out_modes = whole.shape[1]
        fold = fold_of(cells, out_modes)
        rows = cells // fold
        flag = limiter[:, cells - 1 :].astype(jnp.float32)
        spare = jnp.broadcast_to(flag, (rows, LANES - fold * out_modes))
        for d in range(groups):
            first = d * cells
            parts = [whole[first + f * rows : first + (f + 1) * rows] for f in range(fold)]
            out[lax.rem(here + groups - d, groups)] = jnp.concatenate(parts + [spare], axis=1)


def collide(table, spread, tensors, limiter):
    species = len(spread)
    groups, cells, modes = spread[0].shape
    out_modes = tensors.shape[1]
    rows = cells // fold_of(cells, out_modes)
    block = max(b for b in (1, 2, 4, 6, 8) if out_modes % b == 0)
    vmem = pl.BlockSpec(memory_space=pltpu.VMEM)
    return pl.pallas_call(
        functools.partial(collide_kernel, species=species),
        grid=(out_modes // block,),
        in_specs=[
            pl.BlockSpec(memory_space=pltpu.SMEM),
            *[vmem] * species,
            pl.BlockSpec((species, block, modes, modes), lambda step: (0, step, 0, 0)),
            vmem,
        ],
        out_specs=vmem,
        scratch_shapes=[
            pltpu.VMEM((species, groups * cells, modes), jnp.bfloat16),
            pltpu.VMEM((modes, groups * cells), jnp.float32),
            pltpu.VMEM((out_modes, groups * cells), jnp.float32),
        ],
        out_shape=jax.ShapeDtypeStruct((groups, rows, LANES), jnp.float32),
        compiler_params=pltpu.CompilerParams(vmem_limit_bytes=40 * MIB),
        name="collide",
    )(table, *spread, tensors, limiter)


def flux_kernel(mine, limiter, plus, minus, flux):
    groups, cells, modes = mine.shape
    wide = jnp.concatenate([mine[d].astype(jnp.float32) for d in (1, 0, groups - 1)], axis=0)
    wide = wide[cells - 2 : 2 * cells + 2]
    lower = wide[1:-1] - wide[:-2]
    upper = wide[2:] - wide[1:-1]
    one = minmod_two(lower, upper)
    two = minmod_three(2.0 * lower, 0.5 * (lower + upper), 2.0 * upper)
    flags = column(limiter[...])
    ahead = lax.broadcasted_iota(jnp.int32, (3, 1), 0)

    def chosen(first, second, flag):
        return jnp.where(flag == 1, first, jnp.where(flag == 2, second, 0.0))

    def stack(shift):
        base = wide[1 + shift :]
        faces = base[1 : cells + 1]
        faces = faces + (0.5 - shift) * chosen(
            one[1 + shift : 1 + shift + cells], two[1 + shift : 1 + shift + cells], flags
        )
        edge = base[:1] + (0.5 - shift) * chosen(
            one[shift : shift + 1], two[shift : shift + 1], ahead
        )
        pad = jnp.zeros((flux.shape[0] - cells - 3, modes), jnp.float32)
        return jnp.concatenate([faces, edge, pad], axis=0)

    total = jnp.dot(
        stack(0), plus[0], precision=lax.Precision.HIGHEST, preferred_element_type=jnp.float32
    )
    total = total + jnp.dot(
        stack(1), minus[0], precision=lax.Precision.HIGHEST, preferred_element_type=jnp.float32
    )
    flux[...] = total


def transport(mine, limiter, plus, minus):
    groups, cells, modes = mine.shape
    vmem = pl.BlockSpec(memory_space=pltpu.VMEM)
    return pl.pallas_call(
        flux_kernel,
        in_specs=[vmem, vmem, vmem, vmem],
        out_specs=vmem,
        out_shape=jax.ShapeDtypeStruct((cells + 8, modes), jnp.float32),
        compiler_params=pltpu.CompilerParams(vmem_limit_bytes=16 * MIB),
        name="transport",
    )(mine, limiter, plus, minus)


def finish_kernel(out_modes, received, flux, fields, new_field, collision):
    groups, rows, _ = received.shape
    cells = fields.shape[1]
    fold = cells // rows
    parts = []
    for f in range(fold):
        pieces = [received[g][:, f * out_modes : (f + 1) * out_modes] for g in range(groups)]
        parts.append(jnp.concatenate(pieces, axis=1))
    term = jnp.concatenate(parts, axis=0)
    collision[0] = term
    before = lax.rem(lax.axis_index("cell") + groups - 1, groups)
    flag = received[before][:1, fold * out_modes : fold * out_modes + 1]
    behind = flux[cells : cells + 3]
    edge = jnp.where(flag == 1.0, behind[1:2], jnp.where(flag == 2.0, behind[2:3], behind[:1]))
    faces = flux[:cells]
    ahead = jnp.concatenate([edge, faces[:-1]], axis=0)
    new_field[0] = fields[0].astype(jnp.float32) + 0.4 * (ahead - faces) + 0.5 * term


def finish(received, flux, fields, out_modes):
    vmem = pl.BlockSpec(memory_space=pltpu.VMEM)
    shape = jax.ShapeDtypeStruct(fields.shape, jnp.float32)
    return pl.pallas_call(
        functools.partial(finish_kernel, out_modes),
        in_specs=[vmem, vmem, vmem],
        out_specs=(vmem, vmem),
        out_shape=(shape, shape),
        compiler_params=pltpu.CompilerParams(vmem_limit_bytes=16 * MIB),
        name="finish",
    )(received, flux, fields)


def shifted(x, axis, by):
    size = lax.axis_size(axis)
    return lax.ppermute(x, axis, [(i, (i + by) % size) for i in range(size)])


def exchanged(x, axis, bit):
    return lax.ppermute(x, axis, [(i, i ^ bit) for i in range(lax.axis_size(axis))])


def local(fields, tensors, pair_table, plus_flux, minus_flux, face_limiter):
    groups, species = lax.axis_size("cell"), lax.axis_size("spec")
    mine = jnp.stack([fields[0]] + [shifted(fields[0], "cell", d) for d in range(1, groups)])
    spread = {0: mine}
    bit = species // 2
    while bit > 0:
        spread.update({q | bit: exchanged(x, "spec", bit) for q, x in spread.items()})
        bit //= 2
    spread = [spread[q] for q in range(species)]
    block = collide(pair_table, spread, tensors, face_limiter)
    received = lax.all_to_all(block, "cell", split_axis=0, concat_axis=0, tiled=False)
    flux = transport(mine, face_limiter, plus_flux, minus_flux)
    return finish(received, flux, fields, tensors.shape[1])


def solution(mesh):
    placed = (
        P("spec", "cell", None),
        P("spec", "cell", None, None),
        P(),
        P("spec", None, None),
        P("spec", None, None),
        P("spec", "cell"),
    )
    return jax.shard_map(
        local,
        mesh=mesh,
        in_specs=placed,
        out_specs=(P("spec", "cell", None), P("spec", "cell", None)),
        check_vma=False,
    )
```

time: 93.6 us -> 62.9 us (0.67)
  blocking collectives: 45.6 us -> 0 us
  starting transfers between devices: 3.35 us -> 20.7 us
  Pallas kernels: 36.2 us -> 24.7 us
  waiting for transfers between devices: 5.47 us -> 14.2 us
  local copies, waits for them, and re-layouts: 0.67 us -> 2.2 us
  other arithmetic: 0.98 us -> 0 us
    all_gather x1 -> x0, blocking collectives: 45.6 us -> none  [local(): everyone = lax.all_gather(fields[0], ('cell', 'spec'), axis=0, tiled=False)]
    ppermute x0 -> x10, starting transfers between devices: none -> 15.3 us  [the longest x7 13.8 us: shifted(): return lax.ppermute(x, axis, [(i, (i + by) % size) for i in range(size)])]
    pallas_call x3, Pallas kernels: 36.2 us -> 24.7 us  [the longest x1 23.1 us: collide(): pl.pallas_call(functools.partial(collide_kernel, species=species), grid=(...]
    ppermute x0 -> x10, waiting for transfers between devices: none -> 8.11 us  [the longest x3 5.59 us: exchanged(): lax.ppermute(x, axis, [(i, i ^ bit) for i in range(lax.axis_size(axis))])]
    all_to_all x1, starting transfers between devices: 3.35 us -> 5.4 us  [local(): lax.all_to_all(block, 'cell', split_axis=0, concat_axis=0, tiled=False)]
    unnamed x10 -> x19, local copies, waits for them, and re-layouts: 0.67 us -> 2.19 us
  transfers between devices with their start and end apart: 1 -> 11, of which waited for: 1 -> 5; matrix products, arithmetic and copies ran while one was open for 0% -> 1% of each run, Pallas kernels for 1% -> 1%
where the time goes in v2:
time: 62.9 us; the launch traced here: 62.5 us
  Pallas kernels  24.7 us (39%)
  starting transfers between devices  20.7 us (33%)
  waiting for transfers between devices  14.2 us (23%)
  local copies, waits for them, and re-layouts  2.2 us (3%)
  between operations  0.72 us (1%)
    pallas_call x1, Pallas kernels, collide(): pl.pallas_call(functools.partial(collide_kernel, species=species), grid=(...  23.1 us
    ppermute x7, starting transfers between devices, shifted(): return lax.ppermute(x, axis, [(i, (i + by) % size) for i in range(size)])  13.8 us
    all_to_all x1, waiting for transfers between devices, local(): lax.all_to_all(block, 'cell', split_axis=0, concat_axis=0, tiled=False)  6.09 us
    ppermute x3, waiting for transfers between devices, exchanged(): lax.ppermute(x, axis, [(i, i ^ bit) for i in range(lax.axis_size(axis))])  5.59 us
    all_to_all x1, starting transfers between devices, local(): lax.all_to_all(block, 'cell', split_axis=0, concat_axis=0, tiled=False)  5.4 us
    ppermute x7, waiting for transfers between devices, shifted(): return lax.ppermute(x, axis, [(i, (i + by) % size) for i in range(size)])  2.53 us
    unnamed x19, local copies, waits for them, and re-layouts  2.19 us
    ppermute x3, starting transfers between devices, exchanged(): lax.ppermute(x, axis, [(i, i ^ bit) for i in range(lax.axis_size(axis))])  1.52 us
  transfers between devices with their start and end apart: 11, of which 5 were waited for; matrix products, arithmetic and copies ran while one was open for 1% of the time, Pallas kernels for 1%

profile of v2, /device:TPU:0, one launch (start us, length us, event | category | flops | bytes accessed | tf_op | source)
XLA Modules:
  0.0 62.5 jit_solution(406633739060942644)
XLA Ops:
  0.6 0.0 copy-start.2
  0.7 3.0 %collective-permute-start = (bf16[32,384]{1,0:T(8,128)(2,1)}, bf16[32,384]{1,0:T(8,128)(2,1)S(1)}, u32[]{:S(2)}, u32[]{:S(2)}) collective-permute-start(bf16[32,384]{1,0:T(8,128)(2,1)} %bitcast.15), channel_id=1, source_target_pairs={{0,4},{4,8},{8,12},{12,16},{16,20},{20,24},{24,28},{28,0},{1,5},{5... | collective-permute-start | bytes 73736 | tf_op jit(solution)/shard_map/ppermute | solution.py:228
  3.7 1.6 %collective-permute-start.1 = (bf16[32,384]{1,0:T(8,128)(2,1)}, bf16[32,384]{1,0:T(8,128)(2,1)S(1)}, u32[]{:S(2)}, u32[]{:S(2)}) collective-permute-start(bf16[32,384]{1,0:T(8,128)(2,1)} %bitcast.16), channel_id=1, source_target_pairs={{0,8},{4,12},{8,16},{12,20},{16,24},{20,28},{24,0},{28,4},{1,9},{5... | collective-permute-start | bytes 73736 | tf_op jit(solution)/shard_map/ppermute | solution.py:228
  5.2 2.6 %collective-permute-start.2 = (bf16[32,384]{1,0:T(8,128)(2,1)}, bf16[32,384]{1,0:T(8,128)(2,1)S(1)}, u32[]{:S(2)}, u32[]{:S(2)}) collective-permute-start(bf16[32,384]{1,0:T(8,128)(2,1)} %bitcast.17), channel_id=1, source_target_pairs={{0,12},{4,16},{8,20},{12,24},{16,28},{20,0},{24,4},{28,8},{1,13},{... | collective-permute-start | bytes 73736 | tf_op jit(solution)/shard_map/ppermute | solution.py:228
  7.8 1.2 %collective-permute-start.3 = (bf16[32,384]{1,0:T(8,128)(2,1)}, bf16[32,384]{1,0:T(8,128)(2,1)S(1)}, u32[]{:S(2)}, u32[]{:S(2)}) collective-permute-start(bf16[32,384]{1,0:T(8,128)(2,1)} %bitcast.18), channel_id=1, source_target_pairs={{0,16},{4,20},{8,24},{12,28},{16,0},{20,4},{24,8},{28,12},{1,17},{... | collective-permute-start | bytes 73736 | tf_op jit(solution)/shard_map/ppermute | solution.py:228
  9.0 2.6 %collective-permute-start.4 = (bf16[32,384]{1,0:T(8,128)(2,1)}, bf16[32,384]{1,0:T(8,128)(2,1)S(1)}, u32[]{:S(2)}, u32[]{:S(2)}) collective-permute-start(bf16[32,384]{1,0:T(8,128)(2,1)} %bitcast.19), channel_id=1, source_target_pairs={{0,20},{4,24},{8,28},{12,0},{16,4},{20,8},{24,12},{28,16},{1,21},{... | collective-permute-start | bytes 73736 | tf_op jit(solution)/shard_map/ppermute | solution.py:228
  11.6 0.8 %constant_dynamic-update-slice_fusion = bf16[8,32,384]{2,1,0:T(8,128)(2,1)S(1)} fusion(bf16[1,32,384]{2,1,0:T(8,128)(2,1)} %fields.1), kind=kLoop, calls=%fused_computation.7 | loop fusion | bytes 49152
  12.4 0.0 collective-permute-done
  12.4 1.3 %collective-permute-start.5 = (bf16[32,384]{1,0:T(8,128)(2,1)}, bf16[32,384]{1,0:T(8,128)(2,1)S(1)}, u32[]{:S(2)}, u32[]{:S(2)}) collective-permute-start(bf16[32,384]{1,0:T(8,128)(2,1)} %bitcast.20), channel_id=1, source_target_pairs={{0,24},{4,28},{8,0},{12,4},{16,8},{20,12},{24,16},{28,20},{1,25},{... | collective-permute-start | bytes 73736 | tf_op jit(solution)/shard_map/ppermute | solution.py:228
  13.8 1.5 %collective-permute-start.6 = (bf16[32,384]{1,0:T(8,128)(2,1)}, bf16[32,384]{1,0:T(8,128)(2,1)S(1)}, u32[]{:S(2)}, u32[]{:S(2)}) collective-permute-start(bf16[32,384]{1,0:T(8,128)(2,1)} %bitcast.21), channel_id=1, source_target_pairs={{0,28},{4,0},{8,4},{12,8},{16,12},{20,16},{24,20},{28,24},{1,29},{... | collective-permute-start | bytes 73736 | tf_op jit(solution)/shard_map/ppermute | solution.py:228
  15.3 1.1 %collective-permute-done.5 = bf16[32,384]{1,0:T(8,128)(2,1)S(1)} collective-permute-done((bf16[32,384]{1,0:T(8,128)(2,1)}, bf16[32,384]{1,0:T(8,128)(2,1)S(1)}, u32[]{:S(2)}, u32[]{:S(2)}) %collective-permute-start.5) | collective-permute-done | bytes 24608 | tf_op jit(solution)/shard_map/ppermute | solution.py:228
  16.5 1.4 %collective-permute-done.6 = bf16[32,384]{1,0:T(8,128)(2,1)S(1)} collective-permute-done((bf16[32,384]{1,0:T(8,128)(2,1)}, bf16[32,384]{1,0:T(8,128)(2,1)S(1)}, u32[]{:S(2)}, u32[]{:S(2)}) %collective-permute-start.6) | collective-permute-done | bytes 24608 | tf_op jit(solution)/shard_map/ppermute | solution.py:228
  17.9 1.5 %collective-permute-start.8 = (bf16[8,32,384]{2,1,0:T(8,128)(2,1)S(1)}, bf16[8,32,384]{2,1,0:T(8,128)(2,1)S(1)}, u32[]{:S(2)}, u32[]{:S(2)}) collective-permute-start(bf16[8,32,384]{2,1,0:T(8,128)(2,1)S(1)} %bitcast_dynamic-update-slice_fusion.refs_0_.mine), channel_id=1, source_target_pairs={{0,2},{1,3},{2,0},{3,1},{4,6},{5,7},{6,4},{7,5},{8,10},{9,11},{10,... | collective-permute-start | bytes 589832 | tf_op jit(solution)/shard_map/ppermute | solution.py:232
  19.4 0.0 collective-permute-start.7
  19.4 4.1 %collective-permute-done.8.refs_2_ = bf16[8,32,384]{2,1,0:T(8,128)(2,1)S(1)} collective-permute-done((bf16[8,32,384]{2,1,0:T(8,128)(2,1)S(1)}, bf16[8,32,384]{2,1,0:T(8,128)(2,1)S(1)}, u32[]{:S(2)}, u32[]{:S(2)}) %collective-permute-start.8) | collective-permute-done | bytes 196640 | tf_op jit(solution)/shard_map/ppermute | solution.py:232
  23.6 0.0 collective-permute-start.9
  23.6 1.4 %collective-permute-done.9.refs_3_ = bf16[8,32,384]{2,1,0:T(8,128)(2,1)S(1)} collective-permute-done((bf16[8,32,384]{2,1,0:T(8,128)(2,1)S(1)}, bf16[8,32,384]{2,1,0:T(8,128)(2,1)S(1)}, u32[]{:S(2)}, u32[]{:S(2)}) %collective-permute-start.9) | collective-permute-done | bytes 196640 | tf_op jit(solution)/shard_map/ppermute | solution.py:232
  25.0 0.7 %copy-done.3 = s32[4,4]{1,0:T(4,128)S(1)} copy-done((s32[4,4]{1,0:T(4,128)S(1)}, s32[4,4]{1,0:T(4,128)}, u32[]{:S(2)}) %copy-start.3) | copy-done | bytes 88
  25.7 0.7 %copy-done.4 = s32[1,32]{1,0:T(1,128)S(1)} copy-done((s32[1,32]{1,0:T(1,128)S(1)}, s32[1,32]{1,0:T(1,128)}, u32[]{:S(2)}) %copy-start.4) | copy-done | bytes 152
  26.3 23.1 %collide.1 = f32[8,16,128]{2,1,0:T(8,128)} custom-call(s32[4,4]{1,0:T(4,128)S(1)} %copy-done.3, bf16[8,32,384]{2,1,0:T(8,128)(2,1)S(1)} %bitcast_dynamic-update-slice_fusion.refs_0_.mine, bf16[8,32,384]{2,1,0:T(8,128)(2,1)S(1)} %collective-permute-done.7.refs_1_, bf16[8,32,384]{2,1,0:T(8,128)(2,1)S(1)} %collective-permute-done.8.refs_2_, ...), custom_call_target="tpu_custom_call" | custom-call | tf_op jit(solution)/shard_map/collide/pallas_call | solution.py:125
  49.5 5.4 %all-to-all-start = ((f32[8,16,128]{2,1,0:T(8,128)}), f32[8,16,128]{2,1,0:T(8,128)S(1)}, u32[]{:S(2)}, u32[]{:S(2)}) async-start(f32[8,16,128]{2,1,0:T(8,128)} %collide.1), calls=%async_computation | async-start | bytes 131072 | tf_op jit(solution)/shard_map/all_to_all | solution.py:245
  54.9 0.8 %transport.1.flux = f32[40,384]{1,0:T(8,128)S(1)} custom-call(bf16[8,32,384]{2,1,0:T(8,128)(2,1)S(1)} %bitcast_dynamic-update-slice_fusion.refs_0_.mine, s32[1,32]{1,0:T(1,128)S(1)} %copy-done.5, f32[1,384,384]{2,1,0:T(8,128)S(1)} %copy-done, f32[1,384,384]{2,1,0:T(8,128)S(1)} %copy-done.1), custom_call_target="tpu_custom_call" | custom-call | tf_op jit(solution)/shard_map/transport/pallas_call | solution.py:184
  55.7 6.1 %all-to-all-done.received = f32[8,16,128]{2,1,0:T(8,128)S(1)} async-done(((f32[8,16,128]{2,1,0:T(8,128)}), f32[8,16,128]{2,1,0:T(8,128)S(1)}, u32[]{:S(2)}, u32[]{:S(2)}) %all-to-all-start) | async-done | bytes 65568 | tf_op jit(solution)/shard_map/all_to_all | solution.py:245
  61.8 0.7 %finish.1 = (f32[1,32,384]{2,1,0:T(8,128)}, f32[1,32,384]{2,1,0:T(8,128)}) custom-call(f32[8,16,128]{2,1,0:T(8,128)S(1)} %all-to-all-done.received, f32[40,384]{1,0:T(8,128)S(1)} %transport.1.flux, bf16[1,32,384]{2,1,0:T(8,128)(2,1)S(1)} %copy-done.2), custom_call_target="tpu_custom_call" | custom-call | tf_op jit(solution)/shard_map/finish/pallas_call | solution.py:216
  (21 shorter events, 0.1 us)
Async XLA Ops:
  0.6 61.2 %copy-start.2 = (bf16[1,32,384]{2,1,0:T(8,128)(2,1)S(1)}, bf16[1,32,384]{2,1,0:T(8,128)(2,1)}, u32[]{:S(2)}) copy-start(bf16[1,32,384]{2,1,0:T(8,128)(2,1)} %fields.1) | copy-start | bytes 73732
  0.6 54.2 %copy-start.1 = (f32[1,384,384]{2,1,0:T(8,128)S(1)}, f32[1,384,384]{2,1,0:T(8,128)}, u32[]{:S(2)}) copy-start(f32[1,384,384]{2,1,0:T(8,128)} %minus.1) | copy-start | bytes 1769476
  0.7 54.2 %copy-start = (f32[1,384,384]{2,1,0:T(8,128)S(1)}, f32[1,384,384]{2,1,0:T(8,128)}, u32[]{:S(2)}) copy-start(f32[1,384,384]{2,1,0:T(8,128)} %plus.1) | copy-start | bytes 1769476
  0.7 11.8 %collective-permute-start = (bf16[32,384]{1,0:T(8,128)(2,1)}, bf16[32,384]{1,0:T(8,128)(2,1)S(1)}, u32[]{:S(2)}, u32[]{:S(2)}) collective-permute-start(bf16[32,384]{1,0:T(8,128)(2,1)} %bitcast.15), channel_id=1, source_target_pairs={{0,4},{4,8},{8,12},{12,16},{16,20},{20,24},{24,28},{28,0},{1,5},{5... | collective-permute-start | bytes 73736 | tf_op jit(solution)/shard_map/ppermute | solution.py:228
  3.7 10.1 %collective-permute-start.1 = (bf16[32,384]{1,0:T(8,128)(2,1)}, bf16[32,384]{1,0:T(8,128)(2,1)S(1)}, u32[]{:S(2)}, u32[]{:S(2)}) collective-permute-start(bf16[32,384]{1,0:T(8,128)(2,1)} %bitcast.16), channel_id=1, source_target_pairs={{0,8},{4,12},{8,16},{12,20},{16,24},{20,28},{24,0},{28,4},{1,9},{5... | collective-permute-start | bytes 73736 | tf_op jit(solution)/shard_map/ppermute | solution.py:228
  5.2 10.1 %collective-permute-start.2 = (bf16[32,384]{1,0:T(8,128)(2,1)}, bf16[32,384]{1,0:T(8,128)(2,1)S(1)}, u32[]{:S(2)}, u32[]{:S(2)}) collective-permute-start(bf16[32,384]{1,0:T(8,128)(2,1)} %bitcast.17), channel_id=1, source_target_pairs={{0,12},{4,16},{8,20},{12,24},{16,28},{20,0},{24,4},{28,8},{1,13},{... | collective-permute-start | bytes 73736 | tf_op jit(solution)/shard_map/ppermute | solution.py:228
  7.8 7.5 %collective-permute-start.3 = (bf16[32,384]{1,0:T(8,128)(2,1)}, bf16[32,384]{1,0:T(8,128)(2,1)S(1)}, u32[]{:S(2)}, u32[]{:S(2)}) collective-permute-start(bf16[32,384]{1,0:T(8,128)(2,1)} %bitcast.18), channel_id=1, source_target_pairs={{0,16},{4,20},{8,24},{12,28},{16,0},{20,4},{24,8},{28,12},{1,17},{... | collective-permute-start | bytes 73736 | tf_op jit(solution)/shard_map/ppermute | solution.py:228
  9.0 6.3 %collective-permute-start.4 = (bf16[32,384]{1,0:T(8,128)(2,1)}, bf16[32,384]{1,0:T(8,128)(2,1)S(1)}, u32[]{:S(2)}, u32[]{:S(2)}) collective-permute-start(bf16[32,384]{1,0:T(8,128)(2,1)} %bitcast.19), channel_id=1, source_target_pairs={{0,20},{4,24},{8,28},{12,0},{16,4},{20,8},{24,12},{28,16},{1,21},{... | collective-permute-start | bytes 73736 | tf_op jit(solution)/shard_map/ppermute | solution.py:228
  12.4 4.0 %collective-permute-start.5 = (bf16[32,384]{1,0:T(8,128)(2,1)}, bf16[32,384]{1,0:T(8,128)(2,1)S(1)}, u32[]{:S(2)}, u32[]{:S(2)}) collective-permute-start(bf16[32,384]{1,0:T(8,128)(2,1)} %bitcast.20), channel_id=1, source_target_pairs={{0,24},{4,28},{8,0},{12,4},{16,8},{20,12},{24,16},{28,20},{1,25},{... | collective-permute-start | bytes 73736 | tf_op jit(solution)/shard_map/ppermute | solution.py:228
  13.8 4.1 %collective-permute-start.6 = (bf16[32,384]{1,0:T(8,128)(2,1)}, bf16[32,384]{1,0:T(8,128)(2,1)S(1)}, u32[]{:S(2)}, u32[]{:S(2)}) collective-permute-start(bf16[32,384]{1,0:T(8,128)(2,1)} %bitcast.21), channel_id=1, source_target_pairs={{0,28},{4,0},{8,4},{12,8},{16,12},{20,16},{24,20},{28,24},{1,29},{... | collective-permute-start | bytes 73736 | tf_op jit(solution)/shard_map/ppermute | solution.py:228
  17.9 5.7 %collective-permute-start.8 = (bf16[8,32,384]{2,1,0:T(8,128)(2,1)S(1)}, bf16[8,32,384]{2,1,0:T(8,128)(2,1)S(1)}, u32[]{:S(2)}, u32[]{:S(2)}) collective-permute-start(bf16[8,32,384]{2,1,0:T(8,128)(2,1)S(1)} %bitcast_dynamic-update-slice_fusion.refs_0_.mine), channel_id=1, source_target_pairs={{0,2},{1,3},{2,0},{3,1},{4,6},{5,7},{6,4},{7,5},{8,10},{9,11},{10,... | collective-permute-start | bytes 589832 | tf_op jit(solution)/shard_map/ppermute | solution.py:232
  19.4 4.2 %collective-permute-start.7 = (bf16[8,32,384]{2,1,0:T(8,128)(2,1)S(1)}, bf16[8,32,384]{2,1,0:T(8,128)(2,1)S(1)}, u32[]{:S(2)}, u32[]{:S(2)}) collective-permute-start(bf16[8,32,384]{2,1,0:T(8,128)(2,1)S(1)} %bitcast_dynamic-update-slice_fusion.refs_0_.mine), channel_id=1, source_target_pairs={{0,1},{1,0},{2,3},{3,2},{4,5},{5,4},{6,7},{7,6},{8,9},{9,8},{10,11... | collective-permute-start | bytes 589832 | tf_op jit(solution)/shard_map/ppermute | solution.py:232
  23.6 1.4 %collective-permute-start.9 = (bf16[8,32,384]{2,1,0:T(8,128)(2,1)S(1)}, bf16[8,32,384]{2,1,0:T(8,128)(2,1)S(1)}, u32[]{:S(2)}, u32[]{:S(2)}) collective-permute-start(bf16[8,32,384]{2,1,0:T(8,128)(2,1)S(1)} %collective-permute-done.8.refs_2_), channel_id=1, source_target_pairs={{0,1},{1,0},{2,3},{3,2},{4,5},{5,4},{6,7},{7,6},{8,9},{9,8},{10,11... | collective-permute-start | bytes 589832 | tf_op jit(solution)/shard_map/ppermute | solution.py:232
  25.0 0.7 %copy-start.3 = (s32[4,4]{1,0:T(4,128)S(1)}, s32[4,4]{1,0:T(4,128)}, u32[]{:S(2)}) copy-start(s32[4,4]{1,0:T(4,128)} %table.1) | copy-start | bytes 196
  25.7 0.7 %copy-start.4 = (s32[1,32]{1,0:T(1,128)S(1)}, s32[1,32]{1,0:T(1,128)}, u32[]{:S(2)}) copy-start(s32[1,32]{1,0:T(1,128)} %limiter.1) | copy-start | bytes 388
  26.3 28.6 %copy-start.5 = (s32[1,32]{1,0:T(1,128)S(1)}, s32[1,32]{1,0:T(1,128)}, u32[]{:S(2)}) copy-start(s32[1,32]{1,0:T(1,128)} %limiter.1) | copy-start | bytes 388
  49.5 12.3 %all-to-all-start = ((f32[8,16,128]{2,1,0:T(8,128)}), f32[8,16,128]{2,1,0:T(8,128)S(1)}, u32[]{:S(2)}, u32[]{:S(2)}) async-start(f32[8,16,128]{2,1,0:T(8,128)} %collide.1), calls=%async_computation | async-start | bytes 131072 | tf_op jit(solution)/shard_map/all_to_all | solution.py:245

commit v3 on v2

v3 whole, which is shorter than its diff:
```python
import functools

import jax
import jax.numpy as jnp
from jax import lax
from jax.experimental import pallas as pl
from jax.experimental.pallas import tpu as pltpu
from jax.sharding import PartitionSpec as P

LANES = 128
MIB = 1 << 20
WORK = 3 * MIB
PARTS = 4


def minmod_two(first, second):
    least = jnp.minimum(jnp.abs(first), jnp.abs(second))
    return jnp.where(first * second > 0, jnp.where(first > 0, least, -least), 0.0)


def minmod_three(first, second, third):
    same = (first * second > 0) & (second * third > 0)
    least = jnp.minimum(jnp.minimum(jnp.abs(first), jnp.abs(second)), jnp.abs(third))
    return jnp.where(same, jnp.where(first > 0, least, -least), 0.0)


def column(row):
    n = row.shape[1]
    down = lax.broadcasted_iota(jnp.int32, (n, n), 0)
    across = lax.broadcasted_iota(jnp.int32, (n, n), 1)
    return jnp.sum(jnp.where(down == across, row, 0), axis=1, keepdims=True)


def fold_of(cells, out_modes):
    fold = 1
    while cells % (2 * fold) == 0 and 2 * fold * out_modes < LANES:
        fold *= 2
    return fold


def reverse(number, count):
    out, bit = 0, 1
    while bit < count:
        out = out * 2 + number // bit % 2
        bit *= 2
    return out


def slot_of(here, there, groups):
    difference = here ^ there
    out, bit = 0, 0
    while (1 << bit) < groups:
        out = out * 2 + ((difference >> bit) & 1)
        bit += 1
    return out


def tensor_of(table, species, partner):
    owner = lax.axis_index("spec")
    return table[owner, owner ^ partner] - owner * species


def fetches(table, tensors, near, sems, first, partners, pieces):
    count = near.shape[1] // pieces
    copies = []
    for at, partner in enumerate(partners):
        p = tensor_of(table, tensors.shape[0], partner)
        for piece in range(pieces):
            copies.append(
                pltpu.make_async_copy(
                    tensors.at[p, pl.ds(first + piece * count, count)],
                    near.at[at, pl.ds(piece * count, count)],
                    sems.at[at * pieces + piece],
                )
            )
    return copies


def close(x):
    return pltpu.with_memory_space_constraint(x, pltpu.VMEM)


def fetch_kernel(table, after, tensors, near, token, sems, *, first, partners, pieces):
    copies = fetches(table, tensors, near, sems, first, partners, pieces)
    for copy in copies:
        copy.start()
    token[...] = jnp.zeros_like(token)
    for copy in copies:
        copy.wait()


def fetch(table, after, tensors, first, count, partners):
    pieces = max(d for d in (1, 2, 3, 4) if count % d == 0)
    shape = (len(partners), count) + tensors.shape[2:]
    anywhere = pl.BlockSpec(memory_space=pl.ANY)
    vmem = pl.BlockSpec(memory_space=pltpu.VMEM)
    return pl.pallas_call(
        functools.partial(fetch_kernel, first=first, partners=partners, pieces=pieces),
        in_specs=[pl.BlockSpec(memory_space=pltpu.SMEM), anywhere, anywhere],
        out_specs=(vmem, vmem),
        scratch_shapes=[pltpu.SemaphoreType.DMA((len(partners) * pieces,))],
        out_shape=(pltpu.VMEM(shape, tensors.dtype), pltpu.VMEM((8, LANES), jnp.float32)),
        compiler_params=pltpu.CompilerParams(vmem_limit_bytes=MIB),
        cost_estimate=pl.CostEstimate(
            flops=0, transcendentals=0, bytes_accessed=2 * shape[0] * count * shape[2] * shape[3]
        ),
        name="fetch",
    )(table, after, tensors)


def contract(parts, other, own, total, add):
    partners, groups, cells, modes = other.shape
    everyone = groups * cells
    width = 2 * LANES
    tiles = partners * modes // width
    spans = everyone // width

    def unit_of(pair, unit):
        at = 2 * pair + unit
        if spans == 1:
            return at, 0
        return at // spans, at % spans

    def columns_of(span):
        return slice(0, width) if spans == 1 else pl.ds(pl.multiple_of(span * width, width), width)

    def pieces_of(tile):
        for piece in (2 * tile, 2 * tile + 1):
            yield piece * LANES // modes, slice(piece * LANES % modes, piece * LANES % modes + LANES)

    def push(pair, tile, register):
        for unit in range(2):
            _, span = unit_of(pair, unit)
            of = width // cells
            rows = slice(0, of) if spans == 1 else pl.ds(span * of, of)
            tall = [other[p, rows, :, lanes].reshape(width, LANES) for p, lanes in pieces_of(tile)]
            pltpu.matmul_push_rhs(jnp.concatenate(tall, axis=1), register, unit, transpose=True)

    def run(*sums):
        def drain(offset, pair, bank):
            for unit in range(2):
                k, span = unit_of(pair, unit)
                columns = columns_of(span)
                inner = pltpu.matmul_pop(sums[2 * unit + bank])
                row = jnp.sum(inner * own[:, columns], axis=0, keepdims=True)
                place = pl.ds(offset + k, 1)
                total[place, columns] = row + add[place, columns] if add is not None else row

        def work(part, pair, bank, start, follower, pending):
            for tile in range(tiles):
                register = (start + tile) % 2
                if tile + 1 < tiles:
                    push(pair, tile + 1, 1 - register)
                elif follower is not None:
                    push(follower, 0, 1 - register)
                for unit in range(2):
                    k, _ = unit_of(pair, unit)
                    wide = [part[p, k, :, lanes] for p, lanes in pieces_of(tile)]
                    pltpu.matmul_acc_lhs(
                        sums[2 * unit + bank], jnp.concatenate(wide, axis=1), register
                    )
                if tile == 0 and pending is not None:
                    drain(*pending)
            return (start + tiles) % 2

        offset, pending, at = 0, None, 0
        push(0, 0, at)
        for number, part in enumerate(parts):
            pairs = part.shape[1] * spans // 2
            at = work(part, 0, 0, at, 1, pending)
            odd = at

            @pl.loop(0, (pairs - 2) // 2)
            def _(step):
                now = work(part, 2 * step + 1, 1, odd, 2 * step + 2, (offset, 2 * step, 0))
                work(part, 2 * step + 2, 0, now, 2 * step + 3, (offset, 2 * step + 1, 1))

            last = number + 1 == len(parts)
            at = work(part, pairs - 1, 1, odd, None if last else 0, (offset, pairs - 2, 0))
            pending = (offset, pairs - 1, 1)
            offset += part.shape[1]
        drain(*pending)

    pl.run_scoped(run, *[pltpu.ACC(unit)((modes, width), jnp.float32) for unit in (0, 0, 1, 1)])


def near_kernel(table, mine, mate, tensors, *refs, partners, pieces):
    parts, (total, own, far, other, sems, load) = refs[:PARTS], refs[PARTS:]
    copies = fetches(table, tensors, far, sems, 0, partners, pieces)
    loads = [pltpu.make_async_copy(x, other.at[at], load.at[at]) for at, x in enumerate((mine, mate))]
    for copy in loads + copies:
        copy.start()
    for copy in loads:
        copy.wait()
    own[...] = other[0].reshape(own.shape[::-1]).astype(jnp.float32).T
    contract(parts, other, own, total, None)
    for copy in copies:
        copy.wait()


def collide_near(table, mine, mate, tensors, parts, partners):
    groups, cells, modes = mine.shape
    out_modes = tensors.shape[1]
    pieces = max(d for d in (1, 2, 3, 4, 6, 8) if out_modes % d == 0)
    anywhere = pl.BlockSpec(memory_space=pl.ANY)
    vmem = pl.BlockSpec(memory_space=pltpu.VMEM)
    return pl.pallas_call(
        functools.partial(near_kernel, partners=partners, pieces=pieces),
        in_specs=[pl.BlockSpec(memory_space=pltpu.SMEM), anywhere, anywhere, anywhere]
        + [vmem] * len(parts),
        out_specs=(vmem, vmem, vmem),
        scratch_shapes=[
            pltpu.VMEM((2, groups, cells, modes), jnp.bfloat16),
            pltpu.SemaphoreType.DMA((len(partners) * pieces,)),
            pltpu.SemaphoreType.DMA((2,)),
        ],
        out_shape=(
            pltpu.VMEM((out_modes, groups * cells), jnp.float32),
            pltpu.VMEM((modes, groups * cells), jnp.float32),
            pltpu.VMEM((len(partners),) + tensors.shape[1:], tensors.dtype),
        ),
        compiler_params=pltpu.CompilerParams(vmem_limit_bytes=WORK),
        cost_estimate=pl.CostEstimate(
            flops=2 * tensors.size // 2 * groups * cells,
            transcendentals=0,
            bytes_accessed=tensors.size,
        ),
        name="collide_near",
    )(table, mine, mate, tensors, *[close(part) for part in parts])


def far_kernel(one, two, far, first, own, limiter, keep, send, other, total, load):
    loads = [pltpu.make_async_copy(x, other.at[at], load.at[at]) for at, x in enumerate((one, two))]
    for copy in loads:
        copy.start()
    for copy in loads:
        copy.wait()
    contract((far,), other, own, total, first)
    _, groups, cells, _ = other.shape
    whole = total[...].T
    out_modes = whole.shape[1]
    fold = fold_of(cells, out_modes)
    rows = cells // fold
    flag = limiter[:, cells - 1 :].astype(jnp.float32)
    spare = jnp.broadcast_to(flag, (rows, LANES - fold * out_modes))
    for d in range(groups):
        start = d * cells
        parts = [whole[start + f * rows : start + (f + 1) * rows] for f in range(fold)]
        block = jnp.concatenate(parts + [spare], axis=1)
        slot = reverse(d, groups)
        half = groups // 2
        if slot < half:
            keep[slot] = block
        else:
            send[slot - half] = block


def collide_far(one, two, far, first, own, limiter):
    groups, cells, modes = one.shape
    out_modes = far.shape[1]
    rows = cells // fold_of(cells, out_modes)
    anywhere = pl.BlockSpec(memory_space=pl.ANY)
    vmem = pl.BlockSpec(memory_space=pltpu.VMEM)
    half = pltpu.VMEM((groups // 2, rows, LANES), jnp.float32)
    return pl.pallas_call(
        far_kernel,
        in_specs=[anywhere, anywhere, vmem, vmem, vmem, vmem],
        out_specs=(vmem, vmem),
        scratch_shapes=[
            pltpu.VMEM((2, groups, cells, modes), jnp.bfloat16),
            pltpu.VMEM((out_modes, groups * cells), jnp.float32),
            pltpu.SemaphoreType.DMA((2,)),
        ],
        out_shape=(half, half),
        compiler_params=pltpu.CompilerParams(vmem_limit_bytes=WORK),
        cost_estimate=pl.CostEstimate(
            flops=2 * far.size * groups * cells, transcendentals=0, bytes_accessed=far.size
        ),
        name="collide_far",
    )(one, two, close(far), close(first), close(own), limiter)


def flux_kernel(mine, limiter, plus, minus, flux):
    groups, cells, modes = mine.shape
    place = lax.axis_index("cell")
    before = slot_of(place, lax.rem(place + groups - 1, groups), groups)
    after = slot_of(place, lax.rem(place + 1, groups), groups)
    wide = jnp.concatenate([mine[d].astype(jnp.float32) for d in (before, 0, after)], axis=0)
    wide = wide[cells - 2 : 2 * cells + 2]
    lower = wide[1:-1] - wide[:-2]
    upper = wide[2:] - wide[1:-1]
    one = minmod_two(lower, upper)
    two = minmod_three(2.0 * lower, 0.5 * (lower + upper), 2.0 * upper)
    flags = column(limiter[...])
    ahead = lax.broadcasted_iota(jnp.int32, (3, 1), 0)

    def chosen(first, second, flag):
        return jnp.where(flag == 1, first, jnp.where(flag == 2, second, 0.0))

    def stack(shift):
        base = wide[1 + shift :]
        faces = base[1 : cells + 1]
        faces = faces + (0.5 - shift) * chosen(
            one[1 + shift : 1 + shift + cells], two[1 + shift : 1 + shift + cells], flags
        )
        edge = base[:1] + (0.5 - shift) * chosen(
            one[shift : shift + 1], two[shift : shift + 1], ahead
        )
        pad = jnp.zeros((flux.shape[0] - cells - 3, modes), jnp.float32)
        return jnp.concatenate([faces, edge, pad], axis=0)

    total = jnp.dot(
        stack(0), plus[0], precision=lax.Precision.HIGHEST, preferred_element_type=jnp.float32
    )
    total = total + jnp.dot(
        stack(1), minus[0], precision=lax.Precision.HIGHEST, preferred_element_type=jnp.float32
    )
    flux[...] = total


def transport(mine, limiter, plus, minus):
    groups, cells, modes = mine.shape
    vmem = pl.BlockSpec(memory_space=pltpu.VMEM)
    return pl.pallas_call(
        flux_kernel,
        in_specs=[vmem, vmem, vmem, vmem],
        out_specs=vmem,
        out_shape=jax.ShapeDtypeStruct((cells + 8, modes), jnp.float32),
        compiler_params=pltpu.CompilerParams(vmem_limit_bytes=4 * MIB),
        name="transport",
    )(mine, limiter, plus, minus)


def finish_kernel(out_modes, received, flux, fields, new_field, collision):
    groups, rows, _ = received.shape
    place = lax.axis_index("cell")
    blocks = [received[slot_of(place, g, groups)] for g in range(groups)]
    cells = fields.shape[1]
    fold = cells // rows
    parts = []
    for f in range(fold):
        pieces = [blocks[g][:, f * out_modes : (f + 1) * out_modes] for g in range(groups)]
        parts.append(jnp.concatenate(pieces, axis=1))
    term = jnp.concatenate(parts, axis=0)
    collision[0] = term
    before = slot_of(place, lax.rem(place + groups - 1, groups), groups)
    flag = received[before][:1, fold * out_modes : fold * out_modes + 1]
    behind = flux[cells : cells + 3]
    edge = jnp.where(flag == 1.0, behind[1:2], jnp.where(flag == 2.0, behind[2:3], behind[:1]))
    faces = flux[:cells]
    ahead = jnp.concatenate([edge, faces[:-1]], axis=0)
    new_field[0] = fields[0].astype(jnp.float32) + 0.4 * (ahead - faces) + 0.5 * term


def finish(received, flux, fields, out_modes):
    vmem = pl.BlockSpec(memory_space=pltpu.VMEM)
    shape = jax.ShapeDtypeStruct(fields.shape, jnp.float32)
    return pl.pallas_call(
        functools.partial(finish_kernel, out_modes),
        in_specs=[vmem, vmem, vmem],
        out_specs=(vmem, vmem),
        out_shape=(shape, shape),
        compiler_params=pltpu.CompilerParams(vmem_limit_bytes=4 * MIB),
        name="finish",
    )(received, flux, fields)


def exchanged(x, axis, bit):
    return lax.ppermute(x, axis, [(i, i ^ bit) for i in range(lax.axis_size(axis))])


def ordered(x, token):
    return lax.optimization_barrier((x, token))[0]


def local(fields, tensors, pair_table, plus_flux, minus_flux, face_limiter):
    groups, species = lax.axis_size("cell"), lax.axis_size("spec")
    count = tensors.shape[1] // PARTS
    mine = fields
    parts = []
    token = fields
    bit = groups // 2
    while bit > 0:
        came = exchanged(mine, "cell", bit)
        if len(parts) < PARTS - 1:
            part, token = fetch(pair_table, mine, tensors, len(parts) * count, count, (0, 1))
            parts.append(part)
            came = ordered(came, token)
        mine = jnp.concatenate([mine, came], axis=0)
        bit //= 2
    mate = exchanged(mine, "spec", 1)
    far_one = exchanged(mine, "spec", 2)
    while len(parts) < PARTS:
        part, token = fetch(pair_table, mine, tensors, len(parts) * count, count, (0, 1))
        parts.append(part)
    mate = ordered(mate, token)
    far_two = exchanged(mate, "spec", 2)
    first, own, far = collide_near(pair_table, mine, mate, tensors, parts, (2, 3))
    keep, send = collide_far(far_one, far_two, far, first, own, face_limiter)
    flux = transport(mine, face_limiter, plus_flux, minus_flux)
    keep, send = keep[None], send[None]
    bit = groups // 2
    while True:
        keep = jnp.concatenate([keep, exchanged(send, "cell", bit)], axis=0)
        bit //= 2
        if bit == 0:
            break
        keep, send = keep[:, :bit], keep[:, bit:]
    return finish(keep[:, 0], flux, fields, tensors.shape[1])


def solution(mesh):
    placed = (
        P("spec", "cell", None),
        P("spec", "cell", None, None),
        P(),
        P("spec", None, None),
        P("spec", None, None),
        P("spec", "cell"),
    )
    return jax.shard_map(
        local,
        mesh=mesh,
        in_specs=placed,
        out_specs=(P("spec", "cell", None), P("spec", "cell", None)),
        check_vma=False,
    )
```

time: 62.9 us -> 85.1 us (1.35)
  Pallas kernels: 24.7 us -> 44.2 us
  local copies, waits for them, and re-layouts: 2.2 us -> 7.86 us
  starting transfers between devices: 20.7 us -> 15.3 us
  other arithmetic: 0 us -> 2.28 us
    pallas_call x1 -> x6, Pallas kernels: 23.1 us -> 42.7 us  [the longest x1 17.1 us: collide_near(): pl.pallas_call(functools.partial(near_kernel, partners=partners, pieces=p...]
    ppermute x3 -> x9, starting transfers between devices: 1.52 us -> 15.3 us  [exchanged(): lax.ppermute(x, axis, [(i, i ^ bit) for i in range(lax.axis_size(axis))])]
    ppermute x7 -> x0, starting transfers between devices: 13.8 us -> none  [shifted(): return lax.ppermute(x, axis, [(i, (i + by) % size) for i in range(size)])]
    ppermute x3 -> x9, waiting for transfers between devices: 5.59 us -> 14.1 us  [exchanged(): lax.ppermute(x, axis, [(i, i ^ bit) for i in range(lax.axis_size(axis))])]
    all_to_all x1 -> x0, waiting for transfers between devices: 6.09 us -> none  [local(): lax.all_to_all(block, 'cell', split_axis=0, concat_axis=0, tiled=False)]
    unnamed x19 -> x22, local copies, waits for them, and re-layouts: 2.19 us -> 7.86 us
    all_to_all x1 -> x0, starting transfers between devices: 5.4 us -> none  [local(): lax.all_to_all(block, 'cell', split_axis=0, concat_axis=0, tiled=False)]
    ppermute x7 -> x0, waiting for transfers between devices: 2.53 us -> none  [shifted(): return lax.ppermute(x, axis, [(i, (i + by) % size) for i in range(size)])]
  transfers between devices with their start and end apart: 11 -> 9, of which waited for: 5 -> 6; matrix products, arithmetic and copies ran while one was open for 1% -> 0% of each run, Pallas kernels for 1% -> 41%
where the time goes in v3:
time: 85.1 us; the launch traced here: 84.6 us
  Pallas kernels  44.2 us (52%)
  starting transfers between devices  15.3 us (18%)
  waiting for transfers between devices  14.1 us (17%)
  local copies, waits for them, and re-layouts  7.86 us (9%)
  other arithmetic  2.28 us (3%)
    pallas_call x1, Pallas kernels, collide_near(): pl.pallas_call(functools.partial(near_kernel, partners=partners, pieces=p...  17.1 us
    pallas_call x4, Pallas kernels, fetch(): pl.pallas_call(functools.partial(fetch_kernel, first=first, partners=part...  17 us
    ppermute x9, starting transfers between devices, exchanged(): lax.ppermute(x, axis, [(i, i ^ bit) for i in range(lax.axis_size(axis))])  15.3 us
    ppermute x9, waiting for transfers between devices, exchanged(): lax.ppermute(x, axis, [(i, i ^ bit) for i in range(lax.axis_size(axis))])  14.1 us
    pallas_call x1, Pallas kernels, collide_far(): pl.pallas_call(far_kernel, in_specs=[anywhere, anywhere, vmem, vmem, vmem...  8.51 us
    unnamed x22, local copies, waits for them, and re-layouts  7.86 us
    concatenate x3, other arithmetic, local(): mine = jnp.concatenate([mine, came], axis=0)  2.26 us
  transfers between devices with their start and end apart: 9, of which 6 were waited for; matrix products, arithmetic and copies ran while one was open for 0% of the time, Pallas kernels for 41%

profile of v3, /device:TPU:0, one launch (start us, length us, event | category | flops | bytes accessed | tf_op | source)
XLA Modules:
  0.0 84.6 jit_solution(9813492082367672440)
XLA Ops:
  0.6 4.1 %collective-permute-start = (bf16[1,32,384]{2,1,0:T(8,128)(2,1)}, bf16[1,32,384]{2,1,0:T(8,128)(2,1)S(1)}, u32[]{:S(2)}, u32[]{:S(2)}) collective-permute-start(bf16[1,32,384]{2,1,0:T(8,128)(2,1)} %fields.1), channel_id=1, source_target_pairs={{0,16},{4,20},{8,24},{12,28},{16,0},{20,4},{24,8},{28,12},{1,17},{... | collective-permute-start | bytes 73736 | tf_op jit(solution)/shard_map/ppermute | solution.py:369
  4.7 2.0 %collective-permute-done = bf16[1,32,384]{2,1,0:T(8,128)(2,1)S(1)} collective-permute-done((bf16[1,32,384]{2,1,0:T(8,128)(2,1)}, bf16[1,32,384]{2,1,0:T(8,128)(2,1)S(1)}, u32[]{:S(2)}, u32[]{:S(2)}) %collective-permute-start) | collective-permute-done | bytes 24608 | tf_op jit(solution)/shard_map/ppermute | solution.py:369
  7.5 1.9 %collective-permute-start.1 = (bf16[2,32,384]{2,1,0:T(8,128)(2,1)S(1)}, bf16[2,32,384]{2,1,0:T(8,128)(2,1)S(1)}, u32[]{:S(2)}, u32[]{:S(2)}) collective-permute-start(bf16[2,32,384]{2,1,0:T(8,128)(2,1)S(1)} %pad_maximum_fusion.2.after), channel_id=1, source_target_pairs={{0,8},{4,12},{8,0},{12,4},{16,24},{20,28},{24,16},{28,20},{1,9},{5... | collective-permute-start | bytes 147464 | tf_op jit(solution)/shard_map/ppermute | solution.py:369
  9.4 2.2 %collective-permute-done.1 = bf16[2,32,384]{2,1,0:T(8,128)(2,1)S(1)} collective-permute-done((bf16[2,32,384]{2,1,0:T(8,128)(2,1)S(1)}, bf16[2,32,384]{2,1,0:T(8,128)(2,1)S(1)}, u32[]{:S(2)}, u32[]{:S(2)}) %collective-permute-start.1) | collective-permute-done | bytes 49184 | tf_op jit(solution)/shard_map/ppermute | solution.py:369
  12.4 2.0 %collective-permute-start.2 = (bf16[4,32,384]{2,1,0:T(8,128)(2,1)S(1)}, bf16[4,32,384]{2,1,0:T(8,128)(2,1)S(1)}, u32[]{:S(2)}, u32[]{:S(2)}) collective-permute-start(bf16[4,32,384]{2,1,0:T(8,128)(2,1)S(1)} %pad_maximum_fusion.1.after), channel_id=1, source_target_pairs={{0,4},{4,0},{8,12},{12,8},{16,20},{20,16},{24,28},{28,24},{1,5},{5... | collective-permute-start | bytes 294920 | tf_op jit(solution)/shard_map/ppermute | solution.py:369
  14.4 2.7 %collective-permute-done.2 = bf16[4,32,384]{2,1,0:T(8,128)(2,1)S(1)} collective-permute-done((bf16[4,32,384]{2,1,0:T(8,128)(2,1)S(1)}, bf16[4,32,384]{2,1,0:T(8,128)(2,1)S(1)}, u32[]{:S(2)}, u32[]{:S(2)}) %collective-permute-start.2) | collective-permute-done | bytes 98336 | tf_op jit(solution)/shard_map/ppermute | solution.py:369
  17.0 0.8 pad_maximum_fusion.after.mine
  19.3 4.3 %fetch.4 = (bf16[2,12,384,384]{3,2,1,0:T(8,128)(2,1)S(1)}, f32[8,128]{1,0:T(8,128)}) custom-call(s32[4,4]{1,0:T(4,128)S(1)} %copy-done.8, bf16[1,32,384]{2,1,0:T(8,128)(2,1)S(1)} %copy-done.4, bf16[4,48,384,384]{3,2,1,0:T(8,128)(2,1)} %tensors.9), custom_call_target="tpu_custom_call" | custom-call | bytes 7077888 | tf_op jit(solution)/shard_map/fetch/pallas_call | solution.py:97
  23.6 2.9 %copy-done = bf16[2,12,384,384]{3,2,1,0:T(8,128)(2,1)} copy-done((bf16[2,12,384,384]{3,2,1,0:T(8,128)(2,1)}, bf16[2,12,384,384]{3,2,1,0:T(8,128)(2,1)S(1)}, u32[]{:S(2)}) %copy-start) | copy-done | bytes 7077912
  26.5 4.3 %fetch.5 = (bf16[2,12,384,384]{3,2,1,0:T(8,128)(2,1)S(1)}, f32[8,128]{1,0:T(8,128)}) custom-call(s32[4,4]{1,0:T(4,128)S(1)} %copy-done.8, bf16[2,32,384]{2,1,0:T(8,128)(2,1)S(1)} %pad_maximum_fusion.2.after, bf16[4,48,384,384]{3,2,1,0:T(8,128)(2,1)} %tensors.9), custom_call_target="tpu_custom_call" | custom-call | bytes 7077888 | tf_op jit(solution)/shard_map/fetch/pallas_call | solution.py:97
  30.7 4.3 %fetch.6 = (bf16[2,12,384,384]{3,2,1,0:T(8,128)(2,1)S(1)}, f32[8,128]{1,0:T(8,128)}) custom-call(s32[4,4]{1,0:T(4,128)S(1)} %copy-done.8, bf16[4,32,384]{2,1,0:T(8,128)(2,1)S(1)} %pad_maximum_fusion.1.after, bf16[4,48,384,384]{3,2,1,0:T(8,128)(2,1)} %tensors.9), custom_call_target="tpu_custom_call" | custom-call | bytes 7077888 | tf_op jit(solution)/shard_map/fetch/pallas_call | solution.py:97
  35.0 4.3 %fetch.7 = (bf16[2,12,384,384]{3,2,1,0:T(8,128)(2,1)S(1)}, f32[8,128]{1,0:T(8,128)}) custom-call(s32[4,4]{1,0:T(4,128)S(1)} %copy-done.8, bf16[8,32,384]{2,1,0:T(8,128)(2,1)S(1)} %pad_maximum_fusion.after.mine, bf16[4,48,384,384]{3,2,1,0:T(8,128)(2,1)} %tensors.9), custom_call_target="tpu_custom_call" | custom-call | bytes 7077888 | tf_op jit(solution)/shard_map/fetch/pallas_call | solution.py:97
  39.3 2.0 %collective-permute-start.3 = (bf16[8,32,384]{2,1,0:T(8,128)(2,1)S(1)}, bf16[8,32,384]{2,1,0:T(8,128)(2,1)S(1)}, u32[]{:S(2)}, u32[]{:S(2)}) collective-permute-start(bf16[8,32,384]{2,1,0:T(8,128)(2,1)S(1)} %pad_maximum_fusion.after.mine), channel_id=1, source_target_pairs={{0,2},{1,3},{2,0},{3,1},{4,6},{5,7},{6,4},{7,5},{8,10},{9,11},{10,... | collective-permute-start | bytes 589832 | tf_op jit(solution)/shard_map/ppermute | solution.py:369
  42.0 3.0 %copy-done.1 = bf16[2,12,384,384]{3,2,1,0:T(8,128)(2,1)S(1)} copy-done((bf16[2,12,384,384]{3,2,1,0:T(8,128)(2,1)S(1)}, bf16[2,12,384,384]{3,2,1,0:T(8,128)(2,1)}, u32[]{:S(2)}) %copy-start.1) | copy-done | bytes 7077912
  45.0 17.1 %collide_near.1 = (f32[48,256]{1,0:T(8,128)S(1)}, f32[384,256]{1,0:T(8,128)S(1)}, bf16[2,48,384,384]{3,2,1,0:T(8,128)(2,1)S(1)}) custom-call(s32[4,4]{1,0:T(4,128)} %table.9, bf16[8,32,384]{2,1,0:T(8,128)(2,1)} %copy-done.2, bf16[8,32,384]{2,1,0:T(8,128)(2,1)} %copy-done.10, bf16[4,48,384,384]{3,2,1,0:T(8,128)(2,1)} %tensors.9, ...), custom_call_target="tpu_custom_call" | custom-call | flops 7247757312 | bytes 28311552 | tf_op jit(solution)/shard_map/collide_near/pallas_call | solution.py:207
  62.2 8.5 %collide_far.1 = (f32[4,16,128]{2,1,0:T(8,128)S(1)}, f32[4,16,128]{2,1,0:T(8,128)S(1)}) custom-call(bf16[8,32,384]{2,1,0:T(8,128)(2,1)S(1)} %collective-permute-done.3.one, bf16[8,32,384]{2,1,0:T(8,128)(2,1)S(1)} %collective-permute-done.5.two, bf16[2,48,384,384]{3,2,1,0:T(8,128)(2,1)S(1)} %get-tuple-element.15.far, f32[48,256]{1,0:T(8,128)S(1)} %get-tuple-element.16.first, ...), custom_call_target="tpu_custom_call" | custom-call | flops 7247757312 | bytes 14155776 | tf_op jit(solution)/shard_map/collide_far/pallas_call | solution.py:265
  70.7 2.5 %collective-permute-start.6 = (f32[1,4,16,128]{3,2,0,1:T(8,128)S(1)}, f32[1,4,16,128]{3,2,0,1:T(8,128)S(1)}, u32[]{:S(2)}, u32[]{:S(2)}) collective-permute-start(f32[1,4,16,128]{3,2,0,1:T(8,128)S(1)} %bitcast.5), channel_id=1, source_target_pairs={{0,16},{4,20},{8,24},{12,28},{16,0},{20,4},{24,8},{28,12},{1,17},{... | collective-permute-start | bytes 98312 | tf_op jit(solution)/shard_map/ppermute | solution.py:369
  73.3 2.7 %collective-permute-done.6 = f32[1,4,16,128]{3,2,0,1:T(8,128)S(1)} collective-permute-done((f32[1,4,16,128]{3,2,0,1:T(8,128)S(1)}, f32[1,4,16,128]{3,2,0,1:T(8,128)S(1)}, u32[]{:S(2)}, u32[]{:S(2)}) %collective-permute-start.6) | collective-permute-done | bytes 32800 | tf_op jit(solution)/shard_map/ppermute | solution.py:369
  76.0 1.1 %collective-permute-start.7 = (f32[2,2,16,128]{3,2,0,1:T(8,128)S(1)}, f32[2,2,16,128]{3,2,0,1:T(8,128)S(1)}, u32[]{:S(2)}, u32[]{:S(2)}) collective-permute-start(f32[2,2,16,128]{3,2,0,1:T(8,128)S(1)} %get-tuple-element.23), channel_id=1, source_target_pairs={{0,8},{4,12},{8,0},{12,4},{16,24},{20,28},{24,16},{28,20},{1,9},{5... | collective-permute-start | bytes 98312 | tf_op jit(solution)/shard_map/ppermute | solution.py:369
  77.1 2.8 %collective-permute-done.7 = f32[2,2,16,128]{3,2,0,1:T(8,128)S(1)} collective-permute-done((f32[2,2,16,128]{3,2,0,1:T(8,128)S(1)}, f32[2,2,16,128]{3,2,0,1:T(8,128)S(1)}, u32[]{:S(2)}, u32[]{:S(2)}) %collective-permute-start.7) | collective-permute-done | bytes 32800 | tf_op jit(solution)/shard_map/ppermute | solution.py:369
  79.9 1.5 %collective-permute-start.8 = (f32[4,1,16,128]{3,2,0,1:T(8,128)S(1)}, f32[4,1,16,128]{3,2,0,1:T(8,128)S(1)}, u32[]{:S(2)}, u32[]{:S(2)}) collective-permute-start(f32[4,1,16,128]{3,2,0,1:T(8,128)S(1)} %get-tuple-element.21), channel_id=1, source_target_pairs={{0,4},{4,0},{8,12},{12,8},{16,20},{20,16},{24,28},{28,24},{1,5},{5... | collective-permute-start | bytes 98312 | tf_op jit(solution)/shard_map/ppermute | solution.py:369
  81.4 0.8 transport.1.flux
  82.2 1.6 %collective-permute-done.8 = f32[4,1,16,128]{3,2,0,1:T(8,128)S(1)} collective-permute-done((f32[4,1,16,128]{3,2,0,1:T(8,128)S(1)}, f32[4,1,16,128]{3,2,0,1:T(8,128)S(1)}, u32[]{:S(2)}, u32[]{:S(2)}) %collective-permute-start.8) | collective-permute-done | bytes 32800 | tf_op jit(solution)/shard_map/ppermute | solution.py:369
  83.8 0.8 finish.1
  (30 shorter events, 3.7 us)
Async XLA Ops:
  0.6 6.1 %collective-permute-start = (bf16[1,32,384]{2,1,0:T(8,128)(2,1)}, bf16[1,32,384]{2,1,0:T(8,128)(2,1)S(1)}, u32[]{:S(2)}, u32[]{:S(2)}) collective-permute-start(bf16[1,32,384]{2,1,0:T(8,128)(2,1)} %fields.1), channel_id=1, source_target_pairs={{0,16},{4,20},{8,24},{12,28},{16,0},{20,4},{24,8},{28,12},{1,17},{... | collective-permute-start | bytes 73736 | tf_op jit(solution)/shard_map/ppermute | solution.py:369
  7.5 4.1 %collective-permute-start.1 = (bf16[2,32,384]{2,1,0:T(8,128)(2,1)S(1)}, bf16[2,32,384]{2,1,0:T(8,128)(2,1)S(1)}, u32[]{:S(2)}, u32[]{:S(2)}) collective-permute-start(bf16[2,32,384]{2,1,0:T(8,128)(2,1)S(1)} %pad_maximum_fusion.2.after), channel_id=1, source_target_pairs={{0,8},{4,12},{8,0},{12,4},{16,24},{20,28},{24,16},{28,20},{1,9},{5... | collective-permute-start | bytes 147464 | tf_op jit(solution)/shard_map/ppermute | solution.py:369
  12.4 4.7 %collective-permute-start.2 = (bf16[4,32,384]{2,1,0:T(8,128)(2,1)S(1)}, bf16[4,32,384]{2,1,0:T(8,128)(2,1)S(1)}, u32[]{:S(2)}, u32[]{:S(2)}) collective-permute-start(bf16[4,32,384]{2,1,0:T(8,128)(2,1)S(1)} %pad_maximum_fusion.1.after), channel_id=1, source_target_pairs={{0,4},{4,0},{8,12},{12,8},{16,20},{20,16},{24,28},{28,24},{1,5},{5... | collective-permute-start | bytes 294920 | tf_op jit(solution)/shard_map/ppermute | solution.py:369
  17.8 21.5 %copy-start.2 = (bf16[8,32,384]{2,1,0:T(8,128)(2,1)}, bf16[8,32,384]{2,1,0:T(8,128)(2,1)S(1)}, u32[]{:S(2)}) copy-start(bf16[8,32,384]{2,1,0:T(8,128)(2,1)S(1)} %pad_maximum_fusion.after.mine) | copy-start | bytes 589828
  17.8 23.5 %collective-permute-start.4 = (bf16[8,32,384]{2,1,0:T(8,128)(2,1)S(1)}, bf16[8,32,384]{2,1,0:T(8,128)(2,1)S(1)}, u32[]{:S(2)}, u32[]{:S(2)}) collective-permute-start(bf16[8,32,384]{2,1,0:T(8,128)(2,1)S(1)} %pad_maximum_fusion.after.mine), channel_id=1, source_target_pairs={{0,1},{1,0},{2,3},{3,2},{4,5},{5,4},{6,7},{7,6},{8,9},{9,8},{10,11... | collective-permute-start | bytes 589832 | tf_op jit(solution)/shard_map/ppermute | solution.py:369
  17.9 0.7 copy-start.4
  18.6 0.7 copy-start.8
  23.6 2.9 %copy-start = (bf16[2,12,384,384]{3,2,1,0:T(8,128)(2,1)}, bf16[2,12,384,384]{3,2,1,0:T(8,128)(2,1)S(1)}, u32[]{:S(2)}) copy-start(bf16[2,12,384,384]{3,2,1,0:T(8,128)(2,1)S(1)} %get-tuple-element.11.refs_0_) | copy-start | bytes 21233668
  39.3 22.9 %collective-permute-start.3 = (bf16[8,32,384]{2,1,0:T(8,128)(2,1)S(1)}, bf16[8,32,384]{2,1,0:T(8,128)(2,1)S(1)}, u32[]{:S(2)}, u32[]{:S(2)}) collective-permute-start(bf16[8,32,384]{2,1,0:T(8,128)(2,1)S(1)} %pad_maximum_fusion.after.mine), channel_id=1, source_target_pairs={{0,2},{1,3},{2,0},{3,1},{4,6},{5,7},{6,4},{7,5},{8,10},{9,11},{10,... | collective-permute-start | bytes 589832 | tf_op jit(solution)/shard_map/ppermute | solution.py:369
  41.3 0.7 copy-start.10
  41.3 20.8 %collective-permute-start.5 = (bf16[8,32,384]{2,1,0:T(8,128)(2,1)S(1)}, bf16[8,32,384]{2,1,0:T(8,128)(2,1)S(1)}, u32[]{:S(2)}, u32[]{:S(2)}) collective-permute-start(bf16[8,32,384]{2,1,0:T(8,128)(2,1)S(1)} %collective-permute-done.4.mate), channel_id=1, source_target_pairs={{0,2},{1,3},{2,0},{3,1},{4,6},{5,7},{6,4},{7,5},{8,10},{9,11},{10,... | collective-permute-start | bytes 589832 | tf_op jit(solution)/shard_map/ppermute | solution.py:369
  42.0 3.0 %copy-start.1 = (bf16[2,12,384,384]{3,2,1,0:T(8,128)(2,1)S(1)}, bf16[2,12,384,384]{3,2,1,0:T(8,128)(2,1)}, u32[]{:S(2)}) copy-start(bf16[2,12,384,384]{3,2,1,0:T(8,128)(2,1)} %copy-done) | copy-start | bytes 21233668
  45.0 17.2 %copy-start.9 = (s32[1,32]{1,0:T(1,128)S(1)}, s32[1,32]{1,0:T(1,128)}, u32[]{:S(2)}) copy-start(s32[1,32]{1,0:T(1,128)} %limiter.3) | copy-start | bytes 388
  62.2 19.2 %copy-start.3 = (bf16[8,32,384]{2,1,0:T(8,128)(2,1)S(1)}, bf16[8,32,384]{2,1,0:T(8,128)(2,1)}, u32[]{:S(2)}) copy-start(bf16[8,32,384]{2,1,0:T(8,128)(2,1)} %copy-done.2) | copy-start | bytes 589828
  62.2 19.2 %copy-start.6 = (f32[1,384,384]{2,1,0:T(8,128)S(1)}, f32[1,384,384]{2,1,0:T(8,128)}, u32[]{:S(2)}) copy-start(f32[1,384,384]{2,1,0:T(8,128)} %plus.1) | copy-start | bytes 1769476
  62.2 19.2 %copy-start.7 = (f32[1,384,384]{2,1,0:T(8,128)S(1)}, f32[1,384,384]{2,1,0:T(8,128)}, u32[]{:S(2)}) copy-start(f32[1,384,384]{2,1,0:T(8,128)} %minus.1) | copy-start | bytes 1769476
  62.2 21.6 %copy-start.5 = (bf16[1,32,384]{2,1,0:T(8,128)(2,1)S(1)}, bf16[1,32,384]{2,1,0:T(8,128)(2,1)}, u32[]{:S(2)}) copy-start(bf16[1,32,384]{2,1,0:T(8,128)(2,1)} %fields.1) | copy-start | bytes 73732
  70.7 5.2 %collective-permute-start.6 = (f32[1,4,16,128]{3,2,0,1:T(8,128)S(1)}, f32[1,4,16,128]{3,2,0,1:T(8,128)S(1)}, u32[]{:S(2)}, u32[]{:S(2)}) collective-permute-start(f32[1,4,16,128]{3,2,0,1:T(8,128)S(1)} %bitcast.5), channel_id=1, source_target_pairs={{0,16},{4,20},{8,24},{12,28},{16,0},{20,4},{24,8},{28,12},{1,17},{... | collective-permute-start | bytes 98312 | tf_op jit(solution)/shard_map/ppermute | solution.py:369
  76.0 3.9 %collective-permute-start.7 = (f32[2,2,16,128]{3,2,0,1:T(8,128)S(1)}, f32[2,2,16,128]{3,2,0,1:T(8,128)S(1)}, u32[]{:S(2)}, u32[]{:S(2)}) collective-permute-start(f32[2,2,16,128]{3,2,0,1:T(8,128)S(1)} %get-tuple-element.23), channel_id=1, source_target_pairs={{0,8},{4,12},{8,0},{12,4},{16,24},{20,28},{24,16},{28,20},{1,9},{5... | collective-permute-start | bytes 98312 | tf_op jit(solution)/shard_map/ppermute | solution.py:369
  79.9 3.9 %collective-permute-start.8 = (f32[4,1,16,128]{3,2,0,1:T(8,128)S(1)}, f32[4,1,16,128]{3,2,0,1:T(8,128)S(1)}, u32[]{:S(2)}, u32[]{:S(2)}) collective-permute-start(f32[4,1,16,128]{3,2,0,1:T(8,128)S(1)} %get-tuple-element.21), channel_id=1, source_target_pairs={{0,4},{4,0},{8,12},{12,8},{16,20},{20,16},{24,28},{28,24},{1,5},{5... | collective-permute-start | bytes 98312 | tf_op jit(solution)/shard_map/ppermute | solution.py:369

commit v4 on v3

v4 whole, which is shorter than its diff:
```python
import functools

import jax
import jax.numpy as jnp
from jax import lax
from jax.experimental import pallas as pl
from jax.experimental.pallas import tpu as pltpu
from jax.sharding import PartitionSpec as P

LANES = 128
MIB = 1 << 20
PARTS = 4


def minmod_two(first, second):
    least = jnp.minimum(jnp.abs(first), jnp.abs(second))
    return jnp.where(first * second > 0, jnp.where(first > 0, least, -least), 0.0)


def minmod_three(first, second, third):
    same = (first * second > 0) & (second * third > 0)
    least = jnp.minimum(jnp.minimum(jnp.abs(first), jnp.abs(second)), jnp.abs(third))
    return jnp.where(same, jnp.where(first > 0, least, -least), 0.0)


def column(row):
    n = row.shape[1]
    down = lax.broadcasted_iota(jnp.int32, (n, n), 0)
    across = lax.broadcasted_iota(jnp.int32, (n, n), 1)
    return jnp.sum(jnp.where(down == across, row, 0), axis=1, keepdims=True)


def fold_of(cells, out_modes):
    fold = 1
    while cells % (2 * fold) == 0 and 2 * fold * out_modes < LANES:
        fold *= 2
    return fold


def close(x):
    return pltpu.with_memory_space_constraint(x, pltpu.VMEM)


def tensor_of(table, partner):
    owner = lax.axis_index("spec")
    return table[owner, owner ^ partner] - owner * table.shape[0]


def fetch_kernel(table, tensors, near, token, sem):
    copy = pltpu.make_async_copy(tensors.at[tensor_of(table, 0)], near, sem)
    copy.start()
    token[...] = jnp.zeros_like(token)
    copy.wait()


def fetch(table, tensors):
    shape = tensors.shape[1:]
    vmem = pl.BlockSpec(memory_space=pltpu.VMEM)
    return pl.pallas_call(
        fetch_kernel,
        in_specs=[pl.BlockSpec(memory_space=pltpu.SMEM), pl.BlockSpec(memory_space=pl.ANY)],
        out_specs=(vmem, vmem),
        scratch_shapes=[pltpu.SemaphoreType.DMA],
        out_shape=(pltpu.VMEM(shape, tensors.dtype), pltpu.VMEM((8, LANES), jnp.float32)),
        compiler_params=pltpu.CompilerParams(vmem_limit_bytes=MIB),
        cost_estimate=pl.CostEstimate(
            flops=0, transcendentals=0, bytes_accessed=4 * tensors.size // tensors.shape[0]
        ),
        name="fetch",
    )(table, tensors)


def contract(read, count, others, own, total, add, ahead):
    groups, cells, modes = others[0].shape
    everyone = groups * cells
    width = 2 * LANES
    tiles = len(others) * modes // width
    spans = everyone // width
    pairs = count * spans // 2

    def unit_of(pair, unit):
        at = 2 * pair + unit
        if spans == 1:
            return at, 0
        return at // spans, at % spans

    def columns_of(span):
        return slice(0, width) if spans == 1 else pl.ds(pl.multiple_of(span * width, width), width)

    def pieces_of(tile):
        for piece in (2 * tile, 2 * tile + 1):
            yield piece * LANES // modes, slice(piece * LANES % modes, piece * LANES % modes + LANES)

    def push(pair, tile, register):
        for unit in range(2):
            _, span = unit_of(pair, unit)
            of = width // cells
            rows = slice(0, of) if spans == 1 else pl.ds(span * of, of)
            tall = [others[p][rows, :, lanes].reshape(width, LANES) for p, lanes in pieces_of(tile)]
            pltpu.matmul_push_rhs(jnp.concatenate(tall, axis=1), register, unit, transpose=True)

    def run(*sums):
        def drain(part, pair, bank):
            for unit in range(2):
                k, span = unit_of(pair, unit)
                columns = columns_of(span)
                inner = pltpu.matmul_pop(sums[2 * unit + bank])
                row = jnp.sum(inner * own[:, columns], axis=0, keepdims=True)
                place = pl.ds(part * count + k, 1)
                total[place, columns] = row + add[place, columns] if add is not None else row

        def work(part, pair, bank, start, follower, pending):
            for tile in range(tiles):
                register = (start + tile) % 2
                if tile + 1 < tiles:
                    push(pair, tile + 1, 1 - register)
                elif follower is not None:
                    push(follower, 0, 1 - register)
                for unit in range(2):
                    k, _ = unit_of(pair, unit)
                    wide = [read(p, part, k, lanes) for p, lanes in pieces_of(tile)]
                    pltpu.matmul_acc_lhs(
                        sums[2 * unit + bank], jnp.concatenate(wide, axis=1), register
                    )
                if tile == 0 and pending is not None:
                    drain(*pending)
            return (start + tiles) % 2

        pending, at = None, 0
        push(0, 0, at)
        for part in range(PARTS):
            ahead(part)
            at = work(part, 0, 0, at, 1, pending)
            odd = at

            @pl.loop(0, (pairs - 2) // 2)
            def _(step):
                now = work(part, 2 * step + 1, 1, odd, 2 * step + 2, (part, 2 * step, 0))
                work(part, 2 * step + 2, 0, now, 2 * step + 3, (part, 2 * step + 1, 1))

            follower = None if part + 1 == PARTS else 0
            at = work(part, pairs - 1, 1, odd, follower, (part, pairs - 2, 0))
            pending = (part, pairs - 1, 1)
        drain(*pending)

    pl.run_scoped(run, *[pltpu.ACC(unit)((modes, width), jnp.float32) for unit in (0, 0, 1, 1)])


def near_kernel(table, mine, mate, tensors, near, total, own, far, beside, sems):
    count = tensors.shape[1] // PARTS
    second = tensor_of(table, 1)
    copies = [
        pltpu.make_async_copy(
            tensors.at[second, pl.ds(part * count, count)],
            beside.at[pl.ds(part * count, count)],
            sems.at[part],
        )
        for part in range(PARTS)
    ] + [
        pltpu.make_async_copy(
            tensors.at[tensor_of(table, 2 + at), pl.ds(0, count)], far.at[at], sems.at[PARTS + at]
        )
        for at in range(2)
    ]
    copies[0].start()
    copies[1].start()
    own[...] = mine[...].reshape(own.shape[::-1]).astype(jnp.float32).T

    def ahead(part):
        copies[part].wait()
        if part + 2 < len(copies):
            copies[part + 2].start()

    def read(p, part, k, lanes):
        return (near, beside)[p][part * count + k, :, lanes]

    contract(read, count, (mine, mate), own, total, None, ahead)
    for copy in copies[PARTS:]:
        copy.wait()


def collide_near(table, mine, mate, tensors, near):
    groups, cells, modes = mine.shape
    out_modes = tensors.shape[1]
    vmem = pl.BlockSpec(memory_space=pltpu.VMEM)
    return pl.pallas_call(
        near_kernel,
        in_specs=[
            pl.BlockSpec(memory_space=pltpu.SMEM),
            vmem,
            vmem,
            pl.BlockSpec(memory_space=pl.ANY),
            vmem,
        ],
        out_specs=(vmem, vmem, vmem),
        scratch_shapes=[
            pltpu.VMEM(tensors.shape[1:], tensors.dtype),
            pltpu.SemaphoreType.DMA((PARTS + 2,)),
        ],
        out_shape=(
            pltpu.VMEM((out_modes, groups * cells), jnp.float32),
            pltpu.VMEM((modes, groups * cells), jnp.float32),
            pltpu.VMEM((2, out_modes // PARTS) + tensors.shape[2:], tensors.dtype),
        ),
        compiler_params=pltpu.CompilerParams(vmem_limit_bytes=17 * MIB),
        cost_estimate=pl.CostEstimate(
            flops=tensors.size * groups * cells, transcendentals=0, bytes_accessed=tensors.size
        ),
        name="collide_near",
    )(table, close(mine), close(mate), tensors, close(near))


def far_kernel(table, one, two, tensors, far, first, own, limiter, out, total, rest, sems):
    count = tensors.shape[1] // PARTS
    copies = [
        [
            pltpu.make_async_copy(
                tensors.at[tensor_of(table, 2 + at), pl.ds(part * count, count)],
                rest.at[at, pl.ds((part - 1) * count, count)],
                sems.at[at, part - 1],
            )
            for at in range(2)
        ]
        for part in range(1, PARTS)
    ]
    for copy in copies[0] + copies[1]:
        copy.start()

    def ahead(part):
        if part > 0:
            for copy in copies[part - 1]:
                copy.wait()
            for copy in copies[part + 1] if part + 1 < len(copies) else ():
                copy.start()

    def read(p, part, k, lanes):
        return far[p, k, :, lanes] if part == 0 else rest[p, (part - 1) * count + k, :, lanes]

    contract(read, count, (one, two), own, total, first, ahead)
    groups, cells, _ = one.shape
    whole = total[...].T
    out_modes = whole.shape[1]
    fold = fold_of(cells, out_modes)
    rows = cells // fold
    flag = limiter[:, cells - 1 :].astype(jnp.float32)
    spare = jnp.broadcast_to(flag, (rows, LANES - fold * out_modes))
    for d in range(groups):
        start = d * cells
        parts = [whole[start + f * rows : start + (f + 1) * rows] for f in range(fold)]
        out[d] = jnp.concatenate(parts + [spare], axis=1)


def collide_far(table, one, two, tensors, far, first, own, limiter):
    groups, cells, modes = one.shape
    out_modes = tensors.shape[1]
    count = out_modes // PARTS
    rows = cells // fold_of(cells, out_modes)
    vmem = pl.BlockSpec(memory_space=pltpu.VMEM)
    return pl.pallas_call(
        far_kernel,
        in_specs=[
            pl.BlockSpec(memory_space=pltpu.SMEM),
            vmem,
            vmem,
            pl.BlockSpec(memory_space=pl.ANY),
            vmem,
            vmem,
            vmem,
            vmem,
        ],
        out_specs=vmem,
        scratch_shapes=[
            pltpu.VMEM((out_modes, groups * cells), jnp.float32),
            pltpu.VMEM((2, out_modes - count) + tensors.shape[2:], tensors.dtype),
            pltpu.SemaphoreType.DMA((2, PARTS - 1)),
        ],
        out_shape=pltpu.VMEM((groups, rows, LANES), jnp.float32),
        compiler_params=pltpu.CompilerParams(vmem_limit_bytes=24 * MIB),
        cost_estimate=pl.CostEstimate(
            flops=tensors.size * groups * cells, transcendentals=0, bytes_accessed=tensors.size
        ),
        name="collide_far",
    )(table, close(one), close(two), tensors, close(far), close(first), close(own), limiter)


def flux_kernel(mine, limiter, plus, minus, flux):
    groups, cells, modes = mine.shape
    here = lax.axis_index("cell")
    around = (lax.rem(here + groups - 1, groups), here, lax.rem(here + 1, groups))
    wide = jnp.concatenate([mine[d].astype(jnp.float32) for d in around], axis=0)
    wide = wide[cells - 2 : 2 * cells + 2]
    lower = wide[1:-1] - wide[:-2]
    upper = wide[2:] - wide[1:-1]
    one = minmod_two(lower, upper)
    two = minmod_three(2.0 * lower, 0.5 * (lower + upper), 2.0 * upper)
    flags = column(limiter[...])
    ahead = lax.broadcasted_iota(jnp.int32, (3, 1), 0)

    def chosen(first, second, flag):
        return jnp.where(flag == 1, first, jnp.where(flag == 2, second, 0.0))

    def stack(shift):
        base = wide[1 + shift :]
        faces = base[1 : cells + 1]
        faces = faces + (0.5 - shift) * chosen(
            one[1 + shift : 1 + shift + cells], two[1 + shift : 1 + shift + cells], flags
        )
        edge = base[:1] + (0.5 - shift) * chosen(
            one[shift : shift + 1], two[shift : shift + 1], ahead
        )
        pad = jnp.zeros((flux.shape[0] - cells - 3, modes), jnp.float32)
        return jnp.concatenate([faces, edge, pad], axis=0)

    total = jnp.dot(
        stack(0), plus[0], precision=lax.Precision.HIGHEST, preferred_element_type=jnp.float32
    )
    total = total + jnp.dot(
        stack(1), minus[0], precision=lax.Precision.HIGHEST, preferred_element_type=jnp.float32
    )
    flux[...] = total


def transport(mine, limiter, plus, minus):
    groups, cells, modes = mine.shape
    vmem = pl.BlockSpec(memory_space=pltpu.VMEM)
    return pl.pallas_call(
        flux_kernel,
        in_specs=[vmem, vmem, vmem, vmem],
        out_specs=vmem,
        out_shape=jax.ShapeDtypeStruct((cells + 8, modes), jnp.float32),
        compiler_params=pltpu.CompilerParams(vmem_limit_bytes=4 * MIB),
        name="transport",
    )(close(mine), limiter, plus, minus)


def finish_kernel(out_modes, received, flux, fields, new_field, collision):
    groups, rows, _ = received.shape
    cells = fields.shape[1]
    fold = cells // rows
    parts = []
    for f in range(fold):
        pieces = [received[g][:, f * out_modes : (f + 1) * out_modes] for g in range(groups)]
        parts.append(jnp.concatenate(pieces, axis=1))
    term = jnp.concatenate(parts, axis=0)
    collision[0] = term
    before = lax.rem(lax.axis_index("cell") + groups - 1, groups)
    flag = received[before][:1, fold * out_modes : fold * out_modes + 1]
    behind = flux[cells : cells + 3]
    edge = jnp.where(flag == 1.0, behind[1:2], jnp.where(flag == 2.0, behind[2:3], behind[:1]))
    faces = flux[:cells]
    ahead = jnp.concatenate([edge, faces[:-1]], axis=0)
    new_field[0] = fields[0].astype(jnp.float32) + 0.4 * (ahead - faces) + 0.5 * term


def finish(received, flux, fields, out_modes):
    vmem = pl.BlockSpec(memory_space=pltpu.VMEM)
    shape = jax.ShapeDtypeStruct(fields.shape, jnp.float32)
    return pl.pallas_call(
        functools.partial(finish_kernel, out_modes),
        in_specs=[vmem, vmem, vmem],
        out_specs=(vmem, vmem),
        out_shape=(shape, shape),
        compiler_params=pltpu.CompilerParams(vmem_limit_bytes=4 * MIB),
        name="finish",
    )(received, flux, fields)


def exchanged(x, axis, bit):
    return lax.ppermute(x, axis, [(i, i ^ bit) for i in range(lax.axis_size(axis))])


def local(fields, tensors, pair_table, plus_flux, minus_flux, face_limiter):
    mine = lax.all_gather(fields[0], "cell", axis=0, tiled=False)
    mate = exchanged(mine, "spec", 1)
    far_one = exchanged(mine, "spec", 2)
    near, token = fetch(pair_table, tensors)
    mate = lax.optimization_barrier((mate, token))[0]
    far_two = exchanged(mate, "spec", 2)
    first, own, far = collide_near(pair_table, mine, mate, tensors, near)
    block = collide_far(pair_table, far_one, far_two, tensors, far, first, own, face_limiter)
    received = lax.all_to_all(block, "cell", split_axis=0, concat_axis=0, tiled=False)
    flux = transport(mine, face_limiter, plus_flux, minus_flux)
    return finish(received, flux, fields, tensors.shape[1])


def solution(mesh):
    placed = (
        P("spec", "cell", None),
        P("spec", "cell", None, None),
        P(),
        P("spec", None, None),
        P("spec", None, None),
        P("spec", "cell"),
    )
    return jax.shard_map(
        local,
        mesh=mesh,
        in_specs=placed,
        out_specs=(P("spec", "cell", None), P("spec", "cell", None)),
        check_vma=False,
    )
```

time: 85.1 us -> 77.2 us (0.907)
  blocking collectives: 0 us -> 32.6 us
  Pallas kernels: 44.2 us -> 29.1 us
  waiting for transfers between devices: 14.1 us -> 6.1 us
  starting transfers between devices: 15.3 us -> 7.61 us
  local copies, waits for them, and re-layouts: 7.86 us -> 0.71 us
  other arithmetic: 2.28 us -> 0 us
    all_gather x0 -> x1, blocking collectives: none -> 32.6 us  [local(): mine = lax.all_gather(fields[0], 'cell', axis=0, tiled=False)]
    pallas_call x6 -> x3, Pallas kernels: 42.7 us -> 27.5 us  [the longest x1 10.9 us: collide_far(): pl.pallas_call(far_kernel, in_specs=[pl.BlockSpec(memory_space=pltpu.SMEM...]
    ppermute x9 -> x3, waiting for transfers between devices: 14.1 us -> 0.01 us  [exchanged(): lax.ppermute(x, axis, [(i, i ^ bit) for i in range(lax.axis_size(axis))])]
    ppermute x9 -> x3, starting transfers between devices: 15.3 us -> 2.16 us  [exchanged(): lax.ppermute(x, axis, [(i, i ^ bit) for i in range(lax.axis_size(axis))])]
    unnamed x22 -> x12, local copies, waits for them, and re-layouts: 7.86 us -> 0.71 us
    all_to_all x0 -> x1, waiting for transfers between devices: none -> 6.1 us  [local(): lax.all_to_all(block, 'cell', split_axis=0, concat_axis=0, tiled=False)]
    all_to_all x0 -> x1, starting transfers between devices: none -> 5.46 us  [local(): lax.all_to_all(block, 'cell', split_axis=0, concat_axis=0, tiled=False)]
    concatenate x5 -> x0, other arithmetic: 2.27 us -> none  [the longest x3 2.26 us: local(): mine = jnp.concatenate([mine, came], axis=0)]
  transfers between devices with their start and end apart: 9 -> 4, of which waited for: 6 -> 1; matrix products, arithmetic and copies ran while one was open for 0% -> 0% of each run, Pallas kernels for 41% -> 23%
where the time goes in v4:
time: 77.2 us; the launch traced here: 76.8 us
  blocking collectives  32.6 us (42%)
  Pallas kernels  29.1 us (38%)
  starting transfers between devices  7.61 us (10%)
  waiting for transfers between devices  6.1 us (8%)
    all_gather x1, blocking collectives, local(): mine = lax.all_gather(fields[0], 'cell', axis=0, tiled=False)  32.6 us
    pallas_call x1, Pallas kernels, collide_far(): pl.pallas_call(far_kernel, in_specs=[pl.BlockSpec(memory_space=pltpu.SMEM...  10.9 us
    pallas_call x1, Pallas kernels, collide_near(): pl.pallas_call(near_kernel, in_specs=[pl.BlockSpec(memory_space=pltpu.SME...  10.4 us
    pallas_call x1, Pallas kernels, fetch(): pl.pallas_call(fetch_kernel, in_specs=[pl.BlockSpec(memory_space=pltpu.SM...  6.2 us
    all_to_all x1, waiting for transfers between devices, local(): lax.all_to_all(block, 'cell', split_axis=0, concat_axis=0, tiled=False)  6.1 us
    all_to_all x1, starting transfers between devices, local(): lax.all_to_all(block, 'cell', split_axis=0, concat_axis=0, tiled=False)  5.46 us
    ppermute x3, starting transfers between devices, exchanged(): lax.ppermute(x, axis, [(i, i ^ bit) for i in range(lax.axis_size(axis))])  2.16 us
  transfers between devices with their start and end apart: 4, of which 1 were waited for; matrix products, arithmetic and copies ran while one was open for 0% of the time, Pallas kernels for 23%

profile of v4, /device:TPU:0, one launch (start us, length us, event | category | flops | bytes accessed | tf_op | source)
XLA Modules:
  0.0 76.8 jit_solution(2611539018207790139)
XLA Ops:
  0.6 0.0 copy-start.4
  0.6 32.6 %all_gather.3.mine = bf16[8,32,384]{2,1,0:T(8,128)(2,1)S(1)} all-gather(bf16[1,32,384]{2,1,0:T(8,128)(2,1)} %fields.1), channel_id=1, replica_groups=mesh['cell'=8,'spec'=4] {'cell'}, dimensions={0}, use_global_device_ids=true | all-gather | bytes 221184 | tf_op jit(solution)/shard_map/all_gather | solution.py:373
  33.3 0.0 collective-permute-start.1
  33.3 1.6 %collective-permute-start = (bf16[8,32,384]{2,1,0:T(8,128)(2,1)S(1)}, bf16[8,32,384]{2,1,0:T(8,128)(2,1)S(1)}, u32[]{:S(2)}, u32[]{:S(2)}) collective-permute-start(bf16[8,32,384]{2,1,0:T(8,128)(2,1)S(1)} %all_gather.3.mine), channel_id=1, source_target_pairs={{0,2},{1,3},{2,0},{3,1},{4,6},{5,7},{6,4},{7,5},{8,10},{9,11},{10,... | collective-permute-start | bytes 589832 | tf_op jit(solution)/shard_map/ppermute | solution.py:369
  34.9 0.7 copy-done.3
  35.5 6.2 %fetch.1 = (bf16[48,384,384]{2,1,0:T(8,128)(2,1)S(1)}, f32[8,128]{1,0:T(8,128)}) custom-call(s32[4,4]{1,0:T(4,128)S(1)} %copy-done.3, bf16[4,48,384,384]{3,2,1,0:T(8,128)(2,1)} %tensors.5), custom_call_target="tpu_custom_call" | custom-call | bytes 28311552 | tf_op jit(solution)/shard_map/fetch/pallas_call | solution.py:59
  41.7 0.0 collective-permute-done.1.mate
  41.8 0.6 collective-permute-start.2
  42.3 0.0 copy-done.4
  42.3 10.4 %collide_near.1 = (f32[48,256]{1,0:T(8,128)S(1)}, f32[384,256]{1,0:T(8,128)S(1)}, bf16[2,12,384,384]{3,2,1,0:T(8,128)(2,1)S(1)}) custom-call(s32[4,4]{1,0:T(4,128)S(1)} %copy-done.4, bf16[8,32,384]{2,1,0:T(8,128)(2,1)S(1)} %all_gather.3.mine, bf16[8,32,384]{2,1,0:T(8,128)(2,1)S(1)} %collective-permute-done.1.mate, bf16[4,48,384,384]{3,2,1,0:T(8,128)(2,1)} %tensors.5, ...), custom_call_target="tpu_custom_call" | custom-call | flops 7247757312 | bytes 28311552 | tf_op jit(solution)/shard_map/collide_near/pallas_call | solution.py:186
  52.8 0.0 collective-permute-done.one
  52.8 0.0 collective-permute-done.2.two
  52.8 0.0 copy-done.5
  52.8 0.0 copy-start
  52.8 0.0 copy-start.1
  52.8 0.0 copy-start.2
  52.9 10.9 %collide_far.1 = f32[8,16,128]{2,1,0:T(8,128)} custom-call(s32[4,4]{1,0:T(4,128)S(1)} %copy-done.4, bf16[8,32,384]{2,1,0:T(8,128)(2,1)S(1)} %collective-permute-done.one, bf16[8,32,384]{2,1,0:T(8,128)(2,1)S(1)} %collective-permute-done.2.two, bf16[4,48,384,384]{3,2,1,0:T(8,128)(2,1)} %tensors.5, bf16[2,12,384,384]{3,2,1,0:T(8,128)(2,1)S(1)} %get-tuple-element.7.far, ...), custom_call_target="tpu_custom_call" | custom-call | flops 7247757312 | bytes 28311552 | tf_op jit(solution)/shard_map/collide_far/pallas_call | solution.py:259
  63.7 5.5 %all-to-all-start = ((f32[8,16,128]{2,1,0:T(8,128)}), f32[8,16,128]{2,1,0:T(8,128)S(1)}, u32[]{:S(2)}, u32[]{:S(2)}) async-start(f32[8,16,128]{2,1,0:T(8,128)} %collide_far.1), calls=%async_computation | async-start | bytes 131072 | tf_op jit(solution)/shard_map/all_to_all | solution.py:381
  69.2 0.0 copy-done
  69.2 0.0 copy-done.1
  69.2 0.8 %transport.1.flux = f32[40,384]{1,0:T(8,128)S(1)} custom-call(bf16[8,32,384]{2,1,0:T(8,128)(2,1)S(1)} %all_gather.3.mine, s32[1,32]{1,0:T(1,128)S(1)} %copy-done.5, f32[1,384,384]{2,1,0:T(8,128)S(1)} %copy-done, f32[1,384,384]{2,1,0:T(8,128)S(1)} %copy-done.1), custom_call_target="tpu_custom_call" | custom-call | tf_op jit(solution)/shard_map/transport/pallas_call | solution.py:326
  70.0 6.1 %all-to-all-done.received = f32[8,16,128]{2,1,0:T(8,128)S(1)} async-done(((f32[8,16,128]{2,1,0:T(8,128)}), f32[8,16,128]{2,1,0:T(8,128)S(1)}, u32[]{:S(2)}, u32[]{:S(2)}) %all-to-all-start) | async-done | bytes 65568 | tf_op jit(solution)/shard_map/all_to_all | solution.py:381
  76.1 0.0 copy-done.2
  76.1 0.7 finish.1
  (2 shorter events, 0.0 us)
Async XLA Ops:
  0.6 41.7 %copy-start.4 = (s32[4,4]{1,0:T(4,128)S(1)}, s32[4,4]{1,0:T(4,128)}, u32[]{:S(2)}) copy-start(s32[4,4]{1,0:T(4,128)} %table.5) | copy-start | bytes 196
  33.3 8.5 %collective-permute-start.1 = (bf16[8,32,384]{2,1,0:T(8,128)(2,1)S(1)}, bf16[8,32,384]{2,1,0:T(8,128)(2,1)S(1)}, u32[]{:S(2)}, u32[]{:S(2)}) collective-permute-start(bf16[8,32,384]{2,1,0:T(8,128)(2,1)S(1)} %all_gather.3.mine), channel_id=1, source_target_pairs={{0,1},{1,0},{2,3},{3,2},{4,5},{5,4},{6,7},{7,6},{8,9},{9,8},{10,11... | collective-permute-start | bytes 589832 | tf_op jit(solution)/shard_map/ppermute | solution.py:369
  33.3 19.5 %collective-permute-start = (bf16[8,32,384]{2,1,0:T(8,128)(2,1)S(1)}, bf16[8,32,384]{2,1,0:T(8,128)(2,1)S(1)}, u32[]{:S(2)}, u32[]{:S(2)}) collective-permute-start(bf16[8,32,384]{2,1,0:T(8,128)(2,1)S(1)} %all_gather.3.mine), channel_id=1, source_target_pairs={{0,2},{1,3},{2,0},{3,1},{4,6},{5,7},{6,4},{7,5},{8,10},{9,11},{10,... | collective-permute-start | bytes 589832 | tf_op jit(solution)/shard_map/ppermute | solution.py:369
  34.9 0.7 copy-start.3
  41.8 11.0 %collective-permute-start.2 = (bf16[8,32,384]{2,1,0:T(8,128)(2,1)S(1)}, bf16[8,32,384]{2,1,0:T(8,128)(2,1)S(1)}, u32[]{:S(2)}, u32[]{:S(2)}) collective-permute-start(bf16[8,32,384]{2,1,0:T(8,128)(2,1)S(1)} %collective-permute-done.1.mate), channel_id=1, source_target_pairs={{0,2},{1,3},{2,0},{3,1},{4,6},{5,7},{6,4},{7,5},{8,10},{9,11},{10,... | collective-permute-start | bytes 589832 | tf_op jit(solution)/shard_map/ppermute | solution.py:369
  42.3 10.5 %copy-start.5 = (s32[1,32]{1,0:T(1,128)S(1)}, s32[1,32]{1,0:T(1,128)}, u32[]{:S(2)}) copy-start(s32[1,32]{1,0:T(1,128)} %limiter.3) | copy-start | bytes 388
  52.8 16.4 %copy-start = (f32[1,384,384]{2,1,0:T(8,128)S(1)}, f32[1,384,384]{2,1,0:T(8,128)}, u32[]{:S(2)}) copy-start(f32[1,384,384]{2,1,0:T(8,128)} %plus.1) | copy-start | bytes 1769476
  52.8 16.4 %copy-start.1 = (f32[1,384,384]{2,1,0:T(8,128)S(1)}, f32[1,384,384]{2,1,0:T(8,128)}, u32[]{:S(2)}) copy-start(f32[1,384,384]{2,1,0:T(8,128)} %minus.1) | copy-start | bytes 1769476
  52.8 23.3 %copy-start.2 = (bf16[1,32,384]{2,1,0:T(8,128)(2,1)S(1)}, bf16[1,32,384]{2,1,0:T(8,128)(2,1)}, u32[]{:S(2)}) copy-start(bf16[1,32,384]{2,1,0:T(8,128)(2,1)} %fields.1) | copy-start | bytes 73732
  63.7 12.4 %all-to-all-start = ((f32[8,16,128]{2,1,0:T(8,128)}), f32[8,16,128]{2,1,0:T(8,128)S(1)}, u32[]{:S(2)}, u32[]{:S(2)}) async-start(f32[8,16,128]{2,1,0:T(8,128)} %collide_far.1), calls=%async_computation | async-start | bytes 131072 | tf_op jit(solution)/shard_map/all_to_all | solution.py:381

commit v5 on v4

--- a/solution.py
+++ b/solution.py
@@ -9,7 +9,7 @@
 
 LANES = 128
 MIB = 1 << 20
-PARTS = 4
+PARTS = 3
 
 
 def minmod_two(first, second):
@@ -37,6 +37,23 @@
     return fold
 
 
+def reverse(number, count):
+    out, bit = 0, 1
+    while bit < count:
+        out = out * 2 + number // bit % 2
+        bit *= 2
+    return out
+
+
+def slot_of(here, there, groups):
+    difference = here ^ there
+    out, bit = 0, 0
+    while (1 << bit) < groups:
+        out = out * 2 + ((difference >> bit) & 1)
+        bit += 1
+    return out
+
+
 def close(x):
     return pltpu.with_memory_space_constraint(x, pltpu.VMEM)
 
@@ -46,28 +63,57 @@
     return table[owner, owner ^ partner] - owner * table.shape[0]
 
 
-def fetch_kernel(table, tensors, near, token, sem):
-    copy = pltpu.make_async_copy(tensors.at[tensor_of(table, 0)], near, sem)
-    copy.start()
+def fetch_kernel(table, after, tensors, near, token, sems, *, first):
+    count = near.shape[1]
+    copies = [
+        pltpu.make_async_copy(
+            tensors.at[tensor_of(table, at), pl.ds(first, count)], near.at[at], sems.at[at]
+        )
+        for at in range(2)
+    ]
+    for copy in copies:
+        copy.start()
     token[...] = jnp.zeros_like(token)
-    copy.wait()
-
-
-def fetch(table, tensors):
-    shape = tensors.shape[1:]
-    vmem = pl.BlockSpec(memory_space=pltpu.VMEM)
-    return pl.pallas_call(
-        fetch_kernel,
-        in_specs=[pl.BlockSpec(memory_space=pltpu.SMEM), pl.BlockSpec(memory_space=pl.ANY)],
+    for copy in copies:
+        copy.wait()
+
+
+def fetch(table, after, tensors, first, count):
+    shape = (2, count) + tensors.shape[2:]
+    anywhere = pl.BlockSpec(memory_space=pl.ANY)
+    vmem = pl.BlockSpec(memory_space=pltpu.VMEM)
+    return pl.pallas_call(
+        functools.partial(fetch_kernel, first=first),
+        in_specs=[pl.BlockSpec(memory_space=pltpu.SMEM), vmem, anywhere],
         out_specs=(vmem, vmem),
-        scratch_shapes=[pltpu.SemaphoreType.DMA],
+        scratch_shapes=[pltpu.SemaphoreType.DMA((2,))],
         out_shape=(pltpu.VMEM(shape, tensors.dtype), pltpu.VMEM((8, LANES), jnp.float32)),
         compiler_params=pltpu.CompilerParams(vmem_limit_bytes=MIB),
         cost_estimate=pl.CostEstimate(
-            flops=0, transcendentals=0, bytes_accessed=4 * tensors.size // tensors.shape[0]
+            flops=0,
+            transcendentals=0,
+            bytes_accessed=4 * 2 * count * tensors.shape[2] * tensors.shape[3],
         ),
         name="fetch",
-    )(table, tensors)
+    )(table, close(after), tensors)
+
+
+def join_kernel(here, came, token, out):
+    count = here.shape[0]
+    out[:count] = here[...]
+    out[count:] = came[...]
+
+
+def join(here, came, token):
+    vmem = pl.BlockSpec(memory_space=pltpu.VMEM)
+    return pl.pallas_call(
+        join_kernel,
+        in_specs=[vmem, vmem, vmem],
+        out_specs=vmem,
+        out_shape=pltpu.VMEM((2 * here.shape[0],) + here.shape[1:], here.dtype),
+        compiler_params=pltpu.CompilerParams(vmem_limit_bytes=MIB),
+        name="join",
+    )(close(here), close(came), close(token))
 
 
 def contract(read, count, others, own, total, add, ahead):
@@ -146,40 +192,27 @@
     pl.run_scoped(run, *[pltpu.ACC(unit)((modes, width), jnp.float32) for unit in (0, 0, 1, 1)])
 
 
-def near_kernel(table, mine, mate, tensors, near, total, own, far, beside, sems):
-    count = tensors.shape[1] // PARTS
-    second = tensor_of(table, 1)
+def near_kernel(table, mine, mate, tensors, *refs):
+    parts, (total, own, far, sems) = refs[:PARTS], refs[PARTS:]
     copies = [
         pltpu.make_async_copy(
-            tensors.at[second, pl.ds(part * count, count)],
-            beside.at[pl.ds(part * count, count)],
-            sems.at[part],
-        )
-        for part in range(PARTS)
-    ] + [
-        pltpu.make_async_copy(
-            tensors.at[tensor_of(table, 2 + at), pl.ds(0, count)], far.at[at], sems.at[PARTS + at]
+            tensors.at[tensor_of(table, 2 + at), pl.ds(0, far.shape[1])], far.at[at], sems.at[at]
         )
         for at in range(2)
     ]
-    copies[0].start()
-    copies[1].start()
+    for copy in copies:
+        copy.start()
     own[...] = mine[...].reshape(own.shape[::-1]).astype(jnp.float32).T
 
-    def ahead(part):
-        copies[part].wait()
-        if part + 2 < len(copies):
-            copies[part + 2].start()
-
     def read(p, part, k, lanes):
-        return (near, beside)[p][part * count + k, :, lanes]
-
-    contract(read, count, (mine, mate), own, total, None, ahead)
-    for copy in copies[PARTS:]:
+        return parts[part][p, k, :, lanes]
+
+    contract(read, parts[0].shape[1], (mine, mate), own, total, None, lambda part: None)
+    for copy in copies:
         copy.wait()
 
 
-def collide_near(table, mine, mate, tensors, near):
+def collide_near(table, mine, mate, tensors, parts):
     groups, cells, modes = mine.shape
     out_modes = tensors.shape[1]
     vmem = pl.BlockSpec(memory_space=pltpu.VMEM)
@@ -190,54 +223,47 @@
             vmem,
             vmem,
             pl.BlockSpec(memory_space=pl.ANY),
-            vmem,
-        ],
+        ]
+        + [vmem] * PARTS,
         out_specs=(vmem, vmem, vmem),
-        scratch_shapes=[
-            pltpu.VMEM(tensors.shape[1:], tensors.dtype),
-            pltpu.SemaphoreType.DMA((PARTS + 2,)),
-        ],
+        scratch_shapes=[pltpu.SemaphoreType.DMA((2,))],
         out_shape=(
             pltpu.VMEM((out_modes, groups * cells), jnp.float32),
             pltpu.VMEM((modes, groups * cells), jnp.float32),
-            pltpu.VMEM((2, out_modes // PARTS) + tensors.shape[2:], tensors.dtype),
+            pltpu.VMEM((2, out_modes - out_modes // PARTS) + tensors.shape[2:], tensors.dtype),
         ),
-        compiler_params=pltpu.CompilerParams(vmem_limit_bytes=17 * MIB),
+        compiler_params=pltpu.CompilerParams(vmem_limit_bytes=2 * MIB),
         cost_estimate=pl.CostEstimate(
             flops=tensors.size * groups * cells, transcendentals=0, bytes_accessed=tensors.size
         ),
         name="collide_near",
-    )(table, close(mine), close(mate), tensors, close(near))
+    )(table, close(mine), close(mate), tensors, *[close(part) for part in parts])
 
 
 def far_kernel(table, one, two, tensors, far, first, own, limiter, out, total, rest, sems):
-    count = tensors.shape[1] // PARTS
+    count = rest.shape[1]
     copies = [
-        [
-            pltpu.make_async_copy(
-                tensors.at[tensor_of(table, 2 + at), pl.ds(part * count, count)],
-                rest.at[at, pl.ds((part - 1) * count, count)],
-                sems.at[at, part - 1],
-            )
-            for at in range(2)
-        ]
-        for part in range(1, PARTS)
+        pltpu.make_async_copy(
+            tensors.at[tensor_of(table, 2 + at), pl.ds(far.shape[1], count)],
+            rest.at[at],
+            sems.at[at],
+        )
+        for at in range(2)
     ]
-    for copy in copies[0] + copies[1]:
+    for copy in copies:
         copy.start()
 
     def ahead(part):
-        if part > 0:
-            for copy in copies[part - 1]:
+        if part + 1 == PARTS:
+            for copy in copies:
                 copy.wait()
-            for copy in copies[part + 1] if part + 1 < len(copies) else ():
-                copy.start()
 
     def read(p, part, k, lanes):
-        return far[p, k, :, lanes] if part == 0 else rest[p, (part - 1) * count + k, :, lanes]
+        return rest[p, k, :, lanes] if part + 1 == PARTS else far[p, part * count + k, :, lanes]
 
     contract(read, count, (one, two), own, total, first, ahead)
     groups, cells, _ = one.shape
+    here = lax.axis_index("cell")
     whole = total[...].T
     out_modes = whole.shape[1]
     fold = fold_of(cells, out_modes)
@@ -247,35 +273,26 @@
     for d in range(groups):
         start = d * cells
         parts = [whole[start + f * rows : start + (f + 1) * rows] for f in range(fold)]
-        out[d] = jnp.concatenate(parts + [spare], axis=1)
+        out[here ^ reverse(d, groups)] = jnp.concatenate(parts + [spare], axis=1)
 
 
 def collide_far(table, one, two, tensors, far, first, own, limiter):
     groups, cells, modes = one.shape
     out_modes = tensors.shape[1]
-    count = out_modes // PARTS
     rows = cells // fold_of(cells, out_modes)
     vmem = pl.BlockSpec(memory_space=pltpu.VMEM)
+    anywhere = pl.BlockSpec(memory_space=pl.ANY)
     return pl.pallas_call(
         far_kernel,
-        in_specs=[
-            pl.BlockSpec(memory_space=pltpu.SMEM),
-            vmem,
-            vmem,
-            pl.BlockSpec(memory_space=pl.ANY),
-            vmem,
-            vmem,
-            vmem,
-            vmem,
-        ],
+        in_specs=[pl.BlockSpec(memory_space=pltpu.SMEM), vmem, vmem, anywhere] + [vmem] * 4,
         out_specs=vmem,
         scratch_shapes=[
             pltpu.VMEM((out_modes, groups * cells), jnp.float32),
-            pltpu.VMEM((2, out_modes - count) + tensors.shape[2:], tensors.dtype),
-            pltpu.SemaphoreType.DMA((2, PARTS - 1)),
+            pltpu.VMEM((2, out_modes // PARTS) + tensors.shape[2:], tensors.dtype),
+            pltpu.SemaphoreType.DMA((2,)),
         ],
         out_shape=pltpu.VMEM((groups, rows, LANES), jnp.float32),
-        compiler_params=pltpu.CompilerParams(vmem_limit_bytes=24 * MIB),
+        compiler_params=pltpu.CompilerParams(vmem_limit_bytes=11 * MIB),
         cost_estimate=pl.CostEstimate(
             flops=tensors.size * groups * cells, transcendentals=0, bytes_accessed=tensors.size
         ),
@@ -285,9 +302,10 @@
 
 def flux_kernel(mine, limiter, plus, minus, flux):
     groups, cells, modes = mine.shape
-    here = lax.axis_index("cell")
-    around = (lax.rem(here + groups - 1, groups), here, lax.rem(here + 1, groups))
-    wide = jnp.concatenate([mine[d].astype(jnp.float32) for d in around], axis=0)
+    place = lax.axis_index("cell")
+    before = slot_of(place, lax.rem(place + groups - 1, groups), groups)
+    after = slot_of(place, lax.rem(place + 1, groups), groups)
+    wide = jnp.concatenate([mine[d].astype(jnp.float32) for d in (before, 0, after)], axis=0)
     wide = wide[cells - 2 : 2 * cells + 2]
     lower = wide[1:-1] - wide[:-2]
     upper = wide[2:] - wide[1:-1]
@@ -370,13 +388,21 @@
 
 
 def local(fields, tensors, pair_table, plus_flux, minus_flux, face_limiter):
-    mine = lax.all_gather(fields[0], "cell", axis=0, tiled=False)
+    groups = lax.axis_size("cell")
+    count = tensors.shape[1] // PARTS
+    mine, parts, token = fields, [], None
+    bit = groups // 2
+    while bit > 0:
+        came = exchanged(mine, "cell", bit)
+        if len(parts) < PARTS:
+            part, token = fetch(pair_table, mine, tensors, len(parts) * count, count)
+            parts.append(part)
+        mine = join(mine, came, token)
+        bit //= 2
     mate = exchanged(mine, "spec", 1)
     far_one = exchanged(mine, "spec", 2)
-    near, token = fetch(pair_table, tensors)
-    mate = lax.optimization_barrier((mate, token))[0]
     far_two = exchanged(mate, "spec", 2)
-    first, own, far = collide_near(pair_table, mine, mate, tensors, near)
+    first, own, far = collide_near(pair_table, mine, mate, tensors, parts)
     block = collide_far(pair_table, far_one, far_two, tensors, far, first, own, face_limiter)
     received = lax.all_to_all(block, "cell", split_axis=0, concat_axis=0, tiled=False)
     flux = transport(mine, face_limiter, plus_flux, minus_flux)

time: 77.2 us -> 54.5 us (0.71)
  blocking collectives: 32.6 us -> 0 us
  starting transfers between devices: 7.61 us -> 13.7 us
  Pallas kernels: 29.1 us -> 32.1 us
    all_gather x1 -> x0, blocking collectives: 32.6 us -> none  [local(): mine = lax.all_gather(fields[0], 'cell', axis=0, tiled=False)]
    ppermute x3 -> x6, starting transfers between devices: 2.16 us -> 10.3 us  [exchanged(): lax.ppermute(x, axis, [(i, i ^ bit) for i in range(lax.axis_size(axis))])]
    pallas_call x1 -> x6, Pallas kernels: 6.2 us -> 13.2 us  [the longest x3 13.1 us: fetch(): pl.pallas_call(functools.partial(fetch_kernel, first=first), in_specs=[pl...]
    pallas_call x1, Pallas kernels: 10.4 us -> 8.33 us  [collide_near(): pl.pallas_call(near_kernel, in_specs=[pl.BlockSpec(memory_space=pltpu.SME...]
    all_to_all x1, starting transfers between devices: 5.46 us -> 3.36 us  [local(): lax.all_to_all(block, 'cell', split_axis=0, concat_axis=0, tiled=False)]
    pallas_call x1, Pallas kernels: 10.9 us -> 9.05 us  [collide_far(): pl.pallas_call(far_kernel, in_specs=[pl.BlockSpec(memory_space=pltpu.SMEM...]
  transfers between devices with their start and end apart: 4 -> 7, of which waited for: 1 -> 2; matrix products, arithmetic and copies ran while one was open for 0% -> 0% of each run, Pallas kernels for 23% -> 41%
where the time goes in v5:
time: 54.5 us; the launch traced here: 54.2 us
  Pallas kernels  32.1 us (59%)
  starting transfers between devices  13.7 us (25%)
  waiting for transfers between devices  6.27 us (12%)
  local copies, waits for them, and re-layouts  1.47 us (3%)
  between operations  0.78 us (1%)
    pallas_call x3, Pallas kernels, fetch(): pl.pallas_call(functools.partial(fetch_kernel, first=first), in_specs=[pl...  13.1 us
    ppermute x6, starting transfers between devices, exchanged(): lax.ppermute(x, axis, [(i, i ^ bit) for i in range(lax.axis_size(axis))])  10.3 us
    pallas_call x1, Pallas kernels, collide_far(): pl.pallas_call(far_kernel, in_specs=[pl.BlockSpec(memory_space=pltpu.SMEM...  9.05 us
    pallas_call x1, Pallas kernels, collide_near(): pl.pallas_call(near_kernel, in_specs=[pl.BlockSpec(memory_space=pltpu.SME...  8.33 us
    all_to_all x1, waiting for transfers between devices, local(): lax.all_to_all(block, 'cell', split_axis=0, concat_axis=0, tiled=False)  6.03 us
    all_to_all x1, starting transfers between devices, local(): lax.all_to_all(block, 'cell', split_axis=0, concat_axis=0, tiled=False)  3.36 us
    unnamed x14, local copies, waits for them, and re-layouts  1.47 us
  transfers between devices with their start and end apart: 7, of which 2 were waited for; matrix products, arithmetic and copies ran while one was open for 0% of the time, Pallas kernels for 41%

profile of v5, /device:TPU:0, one launch (start us, length us, event | category | flops | bytes accessed | tf_op | source)
XLA Modules:
  0.0 54.2 jit_solution(12370409840294724397)
XLA Ops:
  0.6 4.1 %collective-permute-start = (bf16[1,32,384]{2,1,0:T(8,128)(2,1)}, bf16[1,32,384]{2,1,0:T(8,128)(2,1)S(1)}, u32[]{:S(2)}, u32[]{:S(2)}) collective-permute-start(bf16[1,32,384]{2,1,0:T(8,128)(2,1)} %fields.1), channel_id=1, source_target_pairs={{0,16},{4,20},{8,24},{12,28},{16,0},{20,4},{24,8},{28,12},{1,17},{... | collective-permute-start | bytes 73736 | tf_op jit(solution)/shard_map/ppermute | solution.py:387
  4.7 0.8 %copy-done.2 = bf16[1,32,384]{2,1,0:T(8,128)(2,1)S(1)} copy-done((bf16[1,32,384]{2,1,0:T(8,128)(2,1)S(1)}, bf16[1,32,384]{2,1,0:T(8,128)(2,1)}, u32[]{:S(2)}) %copy-start.2) | copy-done | bytes 24600
  5.5 0.7 %copy-done.4 = s32[4,4]{1,0:T(4,128)S(1)} copy-done((s32[4,4]{1,0:T(4,128)S(1)}, s32[4,4]{1,0:T(4,128)}, u32[]{:S(2)}) %copy-start.4) | copy-done | bytes 88
  6.2 4.4 %fetch.3 = (bf16[2,16,384,384]{3,2,1,0:T(8,128)(2,1)S(1)}, f32[8,128]{1,0:T(8,128)S(1)}) custom-call(s32[4,4]{1,0:T(4,128)S(1)} %copy-done.4, bf16[1,32,384]{2,1,0:T(8,128)(2,1)S(1)} %copy-done.2, bf16[4,48,384,384]{3,2,1,0:T(8,128)(2,1)} %tensors.9), custom_call_target="tpu_custom_call" | custom-call | bytes 18874368 | tf_op jit(solution)/shard_map/fetch/pallas_call | solution.py:85
  10.6 0.0 collective-permute-done.came
  10.6 1.6 %collective-permute-start.1 = (bf16[2,32,384]{2,1,0:T(8,128)(2,1)S(1)}, bf16[2,32,384]{2,1,0:T(8,128)(2,1)S(1)}, u32[]{:S(2)}, u32[]{:S(2)}) collective-permute-start(bf16[2,32,384]{2,1,0:T(8,128)(2,1)S(1)} %join.3.after.here), channel_id=1, source_target_pairs={{0,8},{4,12},{8,0},{12,4},{16,24},{20,28},{24,16},{28,20},{1,9},{5... | collective-permute-start | bytes 147464 | tf_op jit(solution)/shard_map/ppermute | solution.py:387
  12.2 4.4 %fetch.4 = (bf16[2,16,384,384]{3,2,1,0:T(8,128)(2,1)S(1)}, f32[8,128]{1,0:T(8,128)S(1)}) custom-call(s32[4,4]{1,0:T(4,128)S(1)} %copy-done.5, bf16[2,32,384]{2,1,0:T(8,128)(2,1)S(1)} %join.3.after.here, bf16[4,48,384,384]{3,2,1,0:T(8,128)(2,1)} %tensors.9), custom_call_target="tpu_custom_call" | custom-call | bytes 18874368 | tf_op jit(solution)/shard_map/fetch/pallas_call | solution.py:85
  16.6 0.0 collective-permute-done.1.came
  16.7 1.6 %collective-permute-start.2 = (bf16[4,32,384]{2,1,0:T(8,128)(2,1)S(1)}, bf16[4,32,384]{2,1,0:T(8,128)(2,1)S(1)}, u32[]{:S(2)}, u32[]{:S(2)}) collective-permute-start(bf16[4,32,384]{2,1,0:T(8,128)(2,1)S(1)} %join.4.after.here), channel_id=1, source_target_pairs={{0,4},{4,0},{8,12},{12,8},{16,20},{20,16},{24,28},{28,24},{1,5},{5... | collective-permute-start | bytes 294920 | tf_op jit(solution)/shard_map/ppermute | solution.py:387
  18.2 4.4 %fetch.5 = (bf16[2,16,384,384]{3,2,1,0:T(8,128)(2,1)S(1)}, f32[8,128]{1,0:T(8,128)S(1)}) custom-call(s32[4,4]{1,0:T(4,128)S(1)} %copy-done.5, bf16[4,32,384]{2,1,0:T(8,128)(2,1)S(1)} %join.4.after.here, bf16[4,48,384,384]{3,2,1,0:T(8,128)(2,1)} %tensors.9), custom_call_target="tpu_custom_call" | custom-call | bytes 18874368 | tf_op jit(solution)/shard_map/fetch/pallas_call | solution.py:85
  22.6 0.0 collective-permute-done.2.came
  22.6 0.1 collective-permute-start.4
  22.7 1.6 %collective-permute-start.3 = (bf16[8,32,384]{2,1,0:T(8,128)(2,1)S(1)}, bf16[8,32,384]{2,1,0:T(8,128)(2,1)S(1)}, u32[]{:S(2)}, u32[]{:S(2)}) collective-permute-start(bf16[8,32,384]{2,1,0:T(8,128)(2,1)S(1)} %join.5.mine), channel_id=1, source_target_pairs={{0,2},{1,3},{2,0},{3,1},{4,6},{5,7},{6,4},{7,5},{8,10},{9,11},{10,... | collective-permute-start | bytes 589832 | tf_op jit(solution)/shard_map/ppermute | solution.py:387
  24.3 0.0 collective-permute-done.4.mate
  24.3 1.4 %collective-permute-start.5 = (bf16[8,32,384]{2,1,0:T(8,128)(2,1)S(1)}, bf16[8,32,384]{2,1,0:T(8,128)(2,1)S(1)}, u32[]{:S(2)}, u32[]{:S(2)}) collective-permute-start(bf16[8,32,384]{2,1,0:T(8,128)(2,1)S(1)} %collective-permute-done.4.mate), channel_id=1, source_target_pairs={{0,2},{1,3},{2,0},{3,1},{4,6},{5,7},{6,4},{7,5},{8,10},{9,11},{10,... | collective-permute-start | bytes 589832 | tf_op jit(solution)/shard_map/ppermute | solution.py:387
  25.7 8.3 %collide_near.1 = (f32[48,256]{1,0:T(8,128)S(1)}, f32[384,256]{1,0:T(8,128)S(1)}, bf16[2,32,384,384]{3,2,1,0:T(8,128)(2,1)S(1)}) custom-call(s32[4,4]{1,0:T(4,128)S(1)} %copy-done.5, bf16[8,32,384]{2,1,0:T(8,128)(2,1)S(1)} %join.5.mine, bf16[8,32,384]{2,1,0:T(8,128)(2,1)S(1)} %collective-permute-done.4.mate, bf16[4,48,384,384]{3,2,1,0:T(8,128)(2,1)} %tensors.9, ...), custom_call_target="tpu_custom_call" | custom-call | flops 7247757312 | bytes 28311552 | tf_op jit(solution)/shard_map/collide_near/pallas_call | solution.py:219
  34.0 0.0 collective-permute-done.3.one
  34.0 0.2 collective-permute-done.5.two
  34.2 0.0 copy-done.6
  34.2 9.0 %collide_far.1 = f32[8,16,128]{2,1,0:T(8,128)} custom-call(s32[4,4]{1,0:T(4,128)S(1)} %copy-done.5, bf16[8,32,384]{2,1,0:T(8,128)(2,1)S(1)} %collective-permute-done.3.one, bf16[8,32,384]{2,1,0:T(8,128)(2,1)S(1)} %collective-permute-done.5.two, bf16[4,48,384,384]{3,2,1,0:T(8,128)(2,1)} %tensors.9, bf16[2,32,384,384]{3,2,1,0:T(8,128)(2,1)S(1)} %get-tuple-element.17.far, ...), custom_call_target="tpu_custom_call" | custom-call | flops 7247757312 | bytes 28311552 | tf_op jit(solution)/shard_map/collide_far/pallas_call | solution.py:285
  43.3 3.4 %all-to-all-start = ((f32[8,16,128]{2,1,0:T(8,128)}), f32[8,16,128]{2,1,0:T(8,128)S(1)}, u32[]{:S(2)}, u32[]{:S(2)}) async-start(f32[8,16,128]{2,1,0:T(8,128)} %collide_far.1), calls=%async_computation | async-start | bytes 131072 | tf_op jit(solution)/shard_map/all_to_all | solution.py:407
  46.7 0.8 %transport.1.flux = f32[40,384]{1,0:T(8,128)S(1)} custom-call(bf16[8,32,384]{2,1,0:T(8,128)(2,1)S(1)} %join.5.mine, s32[1,32]{1,0:T(1,128)S(1)} %copy-done.6, f32[1,384,384]{2,1,0:T(8,128)S(1)} %copy-done, f32[1,384,384]{2,1,0:T(8,128)S(1)} %copy-done.1), custom_call_target="tpu_custom_call" | custom-call | tf_op jit(solution)/shard_map/transport/pallas_call | solution.py:344
  47.5 6.0 %all-to-all-done.received = f32[8,16,128]{2,1,0:T(8,128)S(1)} async-done(((f32[8,16,128]{2,1,0:T(8,128)}), f32[8,16,128]{2,1,0:T(8,128)S(1)}, u32[]{:S(2)}, u32[]{:S(2)}) %all-to-all-start) | async-done | bytes 65568 | tf_op jit(solution)/shard_map/all_to_all | solution.py:407
  53.5 0.7 %finish.1 = (f32[1,32,384]{2,1,0:T(8,128)}, f32[1,32,384]{2,1,0:T(8,128)}) custom-call(f32[8,16,128]{2,1,0:T(8,128)S(1)} %all-to-all-done.received, f32[40,384]{1,0:T(8,128)S(1)} %transport.1.flux, bf16[1,32,384]{2,1,0:T(8,128)(2,1)S(1)} %copy-done.3), custom_call_target="tpu_custom_call" | custom-call | tf_op jit(solution)/shard_map/finish/pallas_call | solution.py:376
  (14 shorter events, 0.1 us)
Async XLA Ops:
  0.6 9.9 %collective-permute-start = (bf16[1,32,384]{2,1,0:T(8,128)(2,1)}, bf16[1,32,384]{2,1,0:T(8,128)(2,1)S(1)}, u32[]{:S(2)}, u32[]{:S(2)}) collective-permute-start(bf16[1,32,384]{2,1,0:T(8,128)(2,1)} %fields.1), channel_id=1, source_target_pairs={{0,16},{4,20},{8,24},{12,28},{16,0},{20,4},{24,8},{28,12},{1,17},{... | collective-permute-start | bytes 73736 | tf_op jit(solution)/shard_map/ppermute | solution.py:387
  4.7 0.8 %copy-start.2 = (bf16[1,32,384]{2,1,0:T(8,128)(2,1)S(1)}, bf16[1,32,384]{2,1,0:T(8,128)(2,1)}, u32[]{:S(2)}) copy-start(bf16[1,32,384]{2,1,0:T(8,128)(2,1)} %fields.1) | copy-start | bytes 73732
  5.5 0.7 %copy-start.4 = (s32[4,4]{1,0:T(4,128)S(1)}, s32[4,4]{1,0:T(4,128)}, u32[]{:S(2)}) copy-start(s32[4,4]{1,0:T(4,128)} %table.9) | copy-start | bytes 196
  6.2 4.4 %copy-start.3 = (bf16[1,32,384]{2,1,0:T(8,128)(2,1)S(1)}, bf16[1,32,384]{2,1,0:T(8,128)(2,1)}, u32[]{:S(2)}) copy-start(bf16[1,32,384]{2,1,0:T(8,128)(2,1)} %fields.1) | copy-start | bytes 73732
  6.2 6.1 %copy-start.5 = (s32[4,4]{1,0:T(4,128)S(1)}, s32[4,4]{1,0:T(4,128)}, u32[]{:S(2)}) copy-start(s32[4,4]{1,0:T(4,128)} %table.9) | copy-start | bytes 196
  10.6 6.0 %collective-permute-start.1 = (bf16[2,32,384]{2,1,0:T(8,128)(2,1)S(1)}, bf16[2,32,384]{2,1,0:T(8,128)(2,1)S(1)}, u32[]{:S(2)}, u32[]{:S(2)}) collective-permute-start(bf16[2,32,384]{2,1,0:T(8,128)(2,1)S(1)} %join.3.after.here), channel_id=1, source_target_pairs={{0,8},{4,12},{8,0},{12,4},{16,24},{20,28},{24,16},{28,20},{1,9},{5... | collective-permute-start | bytes 147464 | tf_op jit(solution)/shard_map/ppermute | solution.py:387
  16.7 5.9 %collective-permute-start.2 = (bf16[4,32,384]{2,1,0:T(8,128)(2,1)S(1)}, bf16[4,32,384]{2,1,0:T(8,128)(2,1)S(1)}, u32[]{:S(2)}, u32[]{:S(2)}) collective-permute-start(bf16[4,32,384]{2,1,0:T(8,128)(2,1)S(1)} %join.4.after.here), channel_id=1, source_target_pairs={{0,4},{4,0},{8,12},{12,8},{16,20},{20,16},{24,28},{28,24},{1,5},{5... | collective-permute-start | bytes 294920 | tf_op jit(solution)/shard_map/ppermute | solution.py:387
  22.6 1.7 %collective-permute-start.4 = (bf16[8,32,384]{2,1,0:T(8,128)(2,1)S(1)}, bf16[8,32,384]{2,1,0:T(8,128)(2,1)S(1)}, u32[]{:S(2)}, u32[]{:S(2)}) collective-permute-start(bf16[8,32,384]{2,1,0:T(8,128)(2,1)S(1)} %join.5.mine), channel_id=1, source_target_pairs={{0,1},{1,0},{2,3},{3,2},{4,5},{5,4},{6,7},{7,6},{8,9},{9,8},{10,11... | collective-permute-start | bytes 589832 | tf_op jit(solution)/shard_map/ppermute | solution.py:387
  22.7 11.3 %collective-permute-start.3 = (bf16[8,32,384]{2,1,0:T(8,128)(2,1)S(1)}, bf16[8,32,384]{2,1,0:T(8,128)(2,1)S(1)}, u32[]{:S(2)}, u32[]{:S(2)}) collective-permute-start(bf16[8,32,384]{2,1,0:T(8,128)(2,1)S(1)} %join.5.mine), channel_id=1, source_target_pairs={{0,2},{1,3},{2,0},{3,1},{4,6},{5,7},{6,4},{7,5},{8,10},{9,11},{10,... | collective-permute-start | bytes 589832 | tf_op jit(solution)/shard_map/ppermute | solution.py:387
  24.3 9.9 %collective-permute-start.5 = (bf16[8,32,384]{2,1,0:T(8,128)(2,1)S(1)}, bf16[8,32,384]{2,1,0:T(8,128)(2,1)S(1)}, u32[]{:S(2)}, u32[]{:S(2)}) collective-permute-start(bf16[8,32,384]{2,1,0:T(8,128)(2,1)S(1)} %collective-permute-done.4.mate), channel_id=1, source_target_pairs={{0,2},{1,3},{2,0},{3,1},{4,6},{5,7},{6,4},{7,5},{8,10},{9,11},{10,... | collective-permute-start | bytes 589832 | tf_op jit(solution)/shard_map/ppermute | solution.py:387
  25.7 8.6 %copy-start.6 = (s32[1,32]{1,0:T(1,128)S(1)}, s32[1,32]{1,0:T(1,128)}, u32[]{:S(2)}) copy-start(s32[1,32]{1,0:T(1,128)} %limiter.3) | copy-start | bytes 388
  34.2 12.4 %copy-start = (f32[1,384,384]{2,1,0:T(8,128)S(1)}, f32[1,384,384]{2,1,0:T(8,128)}, u32[]{:S(2)}) copy-start(f32[1,384,384]{2,1,0:T(8,128)} %plus.1) | copy-start | bytes 1769476
  34.2 12.4 %copy-start.1 = (f32[1,384,384]{2,1,0:T(8,128)S(1)}, f32[1,384,384]{2,1,0:T(8,128)}, u32[]{:S(2)}) copy-start(f32[1,384,384]{2,1,0:T(8,128)} %minus.1) | copy-start | bytes 1769476
  43.3 10.2 %all-to-all-start = ((f32[8,16,128]{2,1,0:T(8,128)}), f32[8,16,128]{2,1,0:T(8,128)S(1)}, u32[]{:S(2)}, u32[]{:S(2)}) async-start(f32[8,16,128]{2,1,0:T(8,128)} %collide_far.1), calls=%async_computation | async-start | bytes 131072 | tf_op jit(solution)/shard_map/all_to_all | solution.py:407

commit v6 on v5

--- a/solution.py
+++ b/solution.py
@@ -9,7 +9,7 @@
 
 LANES = 128
 MIB = 1 << 20
-PARTS = 3
+SETS = 3
 
 
 def minmod_two(first, second):
@@ -63,39 +63,33 @@
     return table[owner, owner ^ partner] - owner * table.shape[0]
 
 
-def fetch_kernel(table, after, tensors, near, token, sems, *, first):
-    count = near.shape[1]
-    copies = [
-        pltpu.make_async_copy(
-            tensors.at[tensor_of(table, at), pl.ds(first, count)], near.at[at], sems.at[at]
-        )
-        for at in range(2)
-    ]
-    for copy in copies:
-        copy.start()
+def fetch_kernel(tensors, *refs, first, count):
+    near, token, sem = refs[-3:]
+    copy = pltpu.make_async_copy(tensors.at[:, pl.ds(first, count)], near, sem)
+    copy.start()
     token[...] = jnp.zeros_like(token)
-    for copy in copies:
-        copy.wait()
-
-
-def fetch(table, after, tensors, first, count):
-    shape = (2, count) + tensors.shape[2:]
+    copy.wait()
+
+
+def fetch(after, tensors, first, count):
+    shape = (tensors.shape[0], count) + tensors.shape[2:]
     anywhere = pl.BlockSpec(memory_space=pl.ANY)
     vmem = pl.BlockSpec(memory_space=pltpu.VMEM)
-    return pl.pallas_call(
-        functools.partial(fetch_kernel, first=first),
-        in_specs=[pl.BlockSpec(memory_space=pltpu.SMEM), vmem, anywhere],
+    held = [] if after is None else [close(after)]
+    return pl.pallas_call(
+        functools.partial(fetch_kernel, first=first, count=count),
+        in_specs=[anywhere] + [vmem] * len(held),
         out_specs=(vmem, vmem),
-        scratch_shapes=[pltpu.SemaphoreType.DMA((2,))],
+        scratch_shapes=[pltpu.SemaphoreType.DMA],
         out_shape=(pltpu.VMEM(shape, tensors.dtype), pltpu.VMEM((8, LANES), jnp.float32)),
         compiler_params=pltpu.CompilerParams(vmem_limit_bytes=MIB),
         cost_estimate=pl.CostEstimate(
             flops=0,
             transcendentals=0,
-            bytes_accessed=4 * 2 * count * tensors.shape[2] * tensors.shape[3],
+            bytes_accessed=4 * tensors.shape[0] * count * tensors.shape[2] * tensors.shape[3],
         ),
         name="fetch",
-    )(table, close(after), tensors)
+    )(tensors, *held)
 
 
 def join_kernel(here, came, token, out):
@@ -116,13 +110,12 @@
     )(close(here), close(came), close(token))
 
 
-def contract(read, count, others, own, total, add, ahead):
+def contract(parts, others, own, total, add, ready):
     groups, cells, modes = others[0].shape
     everyone = groups * cells
     width = 2 * LANES
     tiles = len(others) * modes // width
     spans = everyone // width
-    pairs = count * spans // 2
 
     def unit_of(pair, unit):
         at = 2 * pair + unit
@@ -152,7 +145,7 @@
                 columns = columns_of(span)
                 inner = pltpu.matmul_pop(sums[2 * unit + bank])
                 row = jnp.sum(inner * own[:, columns], axis=0, keepdims=True)
-                place = pl.ds(part * count + k, 1)
+                place = pl.ds(sum(count for _, count in parts[:part]) + k, 1)
                 total[place, columns] = row + add[place, columns] if add is not None else row
 
         def work(part, pair, bank, start, follower, pending):
@@ -164,7 +157,7 @@
                     push(follower, 0, 1 - register)
                 for unit in range(2):
                     k, _ = unit_of(pair, unit)
-                    wide = [read(p, part, k, lanes) for p, lanes in pieces_of(tile)]
+                    wide = [parts[part][0](p, k, lanes) for p, lanes in pieces_of(tile)]
                     pltpu.matmul_acc_lhs(
                         sums[2 * unit + bank], jnp.concatenate(wide, axis=1), register
                     )
@@ -174,17 +167,26 @@
 
         pending, at = None, 0
         push(0, 0, at)
-        for part in range(PARTS):
-            ahead(part)
+        for part in range(len(parts)):
+            last = part + 1 == len(parts)
+            pairs = parts[part][1] * spans // 2
+            if last:
+                ready(0)
             at = work(part, 0, 0, at, 1, pending)
             odd = at
 
             @pl.loop(0, (pairs - 2) // 2)
             def _(step):
+                for number in range(1, SETS if last else 0):
+
+                    @pl.when(step == (number * (pairs // SETS) - 1) // 2)
+                    def _():
+                        ready(number)
+
                 now = work(part, 2 * step + 1, 1, odd, 2 * step + 2, (part, 2 * step, 0))
                 work(part, 2 * step + 2, 0, now, 2 * step + 3, (part, 2 * step + 1, 1))
 
-            follower = None if part + 1 == PARTS else 0
+            follower = None if last else 0
             at = work(part, pairs - 1, 1, odd, follower, (part, pairs - 2, 0))
             pending = (part, pairs - 1, 1)
         drain(*pending)
@@ -192,76 +194,83 @@
     pl.run_scoped(run, *[pltpu.ACC(unit)((modes, width), jnp.float32) for unit in (0, 0, 1, 1)])
 
 
+def stream(table, tensors, held, beside, sems, partners):
+    done = sum(ref.shape[1] for ref in held)
+    count = beside.shape[1] // SETS
+    picks = [tensor_of(table, partner) for partner in partners]
+
+    def copies(number):
+        return [
+            pltpu.make_async_copy(
+                tensors.at[pick, pl.ds(done + number * count, count)],
+                beside.at[at, pl.ds(number * count, count)],
+                sems.at[at, number],
+            )
+            for at, pick in enumerate(picks)
+        ]
+
+    def start(number):
+        for copy in copies(number):
+            copy.start()
+
+    def ready(number):
+        for copy in copies(number):
+            copy.wait()
+        if number + 2 < SETS:
+            start(number + 2)
+
+    def early(ref):
+        return lambda p, k, lanes: ref[picks[p], k, :, lanes]
+
+    def late(p, k, lanes):
+        return beside[p, k, :, lanes]
+
+    start(0)
+    start(1)
+    return [(early(ref), ref.shape[1]) for ref in held] + [(late, beside.shape[1])], ready
+
+
 def near_kernel(table, mine, mate, tensors, *refs):
-    parts, (total, own, far, sems) = refs[:PARTS], refs[PARTS:]
-    copies = [
-        pltpu.make_async_copy(
-            tensors.at[tensor_of(table, 2 + at), pl.ds(0, far.shape[1])], far.at[at], sems.at[at]
-        )
-        for at in range(2)
+    held, (total, own, beside, sems) = refs[:SETS], refs[SETS:]
+    parts, ready = stream(table, tensors, held, beside, sems, (0, 1))
+    own[...] = mine[...].reshape(own.shape[::-1]).astype(jnp.float32).T
+    contract(parts, (mine, mate), own, total, None, ready)
+
+
+def streamed(tensors, held):
+    left = tensors.shape[1] - sum(part.shape[1] for part in held)
+    return [
+        pltpu.VMEM((2, left) + tensors.shape[2:], tensors.dtype),
+        pltpu.SemaphoreType.DMA((2, SETS)),
     ]
-    for copy in copies:
-        copy.start()
-    own[...] = mine[...].reshape(own.shape[::-1]).astype(jnp.float32).T
-
-    def read(p, part, k, lanes):
-        return parts[part][p, k, :, lanes]
-
-    contract(read, parts[0].shape[1], (mine, mate), own, total, None, lambda part: None)
-    for copy in copies:
-        copy.wait()
-
-
-def collide_near(table, mine, mate, tensors, parts):
+
+
+def collide_near(table, mine, mate, tensors, held):
     groups, cells, modes = mine.shape
     out_modes = tensors.shape[1]
     vmem = pl.BlockSpec(memory_space=pltpu.VMEM)
+    anywhere = pl.BlockSpec(memory_space=pl.ANY)
     return pl.pallas_call(
         near_kernel,
-        in_specs=[
-            pl.BlockSpec(memory_space=pltpu.SMEM),
-            vmem,
-            vmem,
-            pl.BlockSpec(memory_space=pl.ANY),
-        ]
-        + [vmem] * PARTS,
-        out_specs=(vmem, vmem, vmem),
-        scratch_shapes=[pltpu.SemaphoreType.DMA((2,))],
+        in_specs=[pl.BlockSpec(memory_space=pltpu.SMEM), vmem, vmem, anywhere] + [vmem] * SETS,
+        out_specs=(vmem, vmem),
+        scratch_shapes=streamed(tensors, held),
         out_shape=(
             pltpu.VMEM((out_modes, groups * cells), jnp.float32),
             pltpu.VMEM((modes, groups * cells), jnp.float32),
-            pltpu.VMEM((2, out_modes - out_modes // PARTS) + tensors.shape[2:], tensors.dtype),
         ),
-        compiler_params=pltpu.CompilerParams(vmem_limit_bytes=2 * MIB),
+        compiler_params=pltpu.CompilerParams(vmem_limit_bytes=16 * MIB),
         cost_estimate=pl.CostEstimate(
             flops=tensors.size * groups * cells, transcendentals=0, bytes_accessed=tensors.size
         ),
         name="collide_near",
-    )(table, close(mine), close(mate), tensors, *[close(part) for part in parts])
-
-
-def far_kernel(table, one, two, tensors, far, first, own, limiter, out, total, rest, sems):
-    count = rest.shape[1]
-    copies = [
-        pltpu.make_async_copy(
-            tensors.at[tensor_of(table, 2 + at), pl.ds(far.shape[1], count)],
-            rest.at[at],
-            sems.at[at],
-        )
-        for at in range(2)
-    ]
-    for copy in copies:
-        copy.start()
-
-    def ahead(part):
-        if part + 1 == PARTS:
-            for copy in copies:
-                copy.wait()
-
-    def read(p, part, k, lanes):
-        return rest[p, k, :, lanes] if part + 1 == PARTS else far[p, part * count + k, :, lanes]
-
-    contract(read, count, (one, two), own, total, first, ahead)
+    )(table, close(mine), close(mate), tensors, *[close(part) for part in held])
+
+
+def far_kernel(table, one, two, tensors, *refs):
+    held, (first, own, limiter, out, total, beside, sems) = refs[:SETS], refs[SETS:]
+    parts, ready = stream(table, tensors, held, beside, sems, (2, 3))
+    contract(parts, (one, two), own, total, first, ready)
     groups, cells, _ = one.shape
     here = lax.axis_index("cell")
     whole = total[...].T
@@ -276,7 +285,7 @@
         out[here ^ reverse(d, groups)] = jnp.concatenate(parts + [spare], axis=1)
 
 
-def collide_far(table, one, two, tensors, far, first, own, limiter):
+def collide_far(table, one, two, tensors, held, first, own, limiter):
     groups, cells, modes = one.shape
     out_modes = tensors.shape[1]
     rows = cells // fold_of(cells, out_modes)
@@ -284,20 +293,28 @@
     anywhere = pl.BlockSpec(memory_space=pl.ANY)
     return pl.pallas_call(
         far_kernel,
-        in_specs=[pl.BlockSpec(memory_space=pltpu.SMEM), vmem, vmem, anywhere] + [vmem] * 4,
+        in_specs=[pl.BlockSpec(memory_space=pltpu.SMEM), vmem, vmem, anywhere] + [vmem] * (SETS + 3),
         out_specs=vmem,
         scratch_shapes=[
             pltpu.VMEM((out_modes, groups * cells), jnp.float32),
-            pltpu.VMEM((2, out_modes // PARTS) + tensors.shape[2:], tensors.dtype),
-            pltpu.SemaphoreType.DMA((2,)),
+            *streamed(tensors, held),
         ],
         out_shape=pltpu.VMEM((groups, rows, LANES), jnp.float32),
-        compiler_params=pltpu.CompilerParams(vmem_limit_bytes=11 * MIB),
+        compiler_params=pltpu.CompilerParams(vmem_limit_bytes=16 * MIB),
         cost_estimate=pl.CostEstimate(
             flops=tensors.size * groups * cells, transcendentals=0, bytes_accessed=tensors.size
         ),
         name="collide_far",
-    )(table, close(one), close(two), tensors, close(far), close(first), close(own), limiter)
+    )(
+        table,
+        close(one),
+        close(two),
+        tensors,
+        *[close(part) for part in held],
+        close(first),
+        close(own),
+        limiter,
+    )
 
 
 def flux_kernel(mine, limiter, plus, minus, flux):
@@ -389,21 +406,23 @@
 
 def local(fields, tensors, pair_table, plus_flux, minus_flux, face_limiter):
     groups = lax.axis_size("cell")
-    count = tensors.shape[1] // PARTS
-    mine, parts, token = fields, [], None
+    count = tensors.shape[1] // (2 * SETS)
+    mine, held, token = fields, [], None
     bit = groups // 2
     while bit > 0:
         came = exchanged(mine, "cell", bit)
-        if len(parts) < PARTS:
-            part, token = fetch(pair_table, mine, tensors, len(parts) * count, count)
-            parts.append(part)
+        if len(held) < SETS:
+            part, token = fetch(mine if held else None, tensors, len(held) * count, count)
+            held.append(part)
         mine = join(mine, came, token)
         bit //= 2
+    while len(held) < SETS:
+        held.append(fetch(mine, tensors, len(held) * count, count)[0])
     mate = exchanged(mine, "spec", 1)
     far_one = exchanged(mine, "spec", 2)
     far_two = exchanged(mate, "spec", 2)
-    first, own, far = collide_near(pair_table, mine, mate, tensors, parts)
-    block = collide_far(pair_table, far_one, far_two, tensors, far, first, own, face_limiter)
+    first, own = collide_near(pair_table, mine, mate, tensors, held)
+    block = collide_far(pair_table, far_one, far_two, tensors, held, first, own, face_limiter)
     received = lax.all_to_all(block, "cell", split_axis=0, concat_axis=0, tiled=False)
     flux = transport(mine, face_limiter, plus_flux, minus_flux)
     return finish(received, flux, fields, tensors.shape[1])

time: 54.5 us -> 57.1 us (1.048)
  Pallas kernels: 32.1 us -> 36.2 us
  local copies, waits for them, and re-layouts: 1.47 us -> 0.03 us
    pallas_call x1, Pallas kernels: 9.05 us -> 12.2 us  [collide_far(): pl.pallas_call(far_kernel, in_specs=[pl.BlockSpec(memory_space=pltpu.SMEM...]
    pallas_call x1, Pallas kernels: 8.33 us -> 11.4 us  [collide_near(): pl.pallas_call(near_kernel, in_specs=[pl.BlockSpec(memory_space=pltpu.SME...]
    pallas_call x3, Pallas kernels: 13.1 us -> 11.1 us  [fetch(): pl.pallas_call(functools.partial(fetch_kernel, first=first, count=count),...]
    unnamed x14 -> x10, local copies, waits for them, and re-layouts: 1.47 us -> 0.03 us
  transfers between devices with their start and end apart: 7 -> 7, of which waited for: 2 -> 1; matrix products, arithmetic and copies ran while one was open for 0% -> 0% of each run, Pallas kernels for 41% -> 41%
where the time goes in v6:
time: 57.1 us; the launch traced here: 56.8 us
  Pallas kernels  36.2 us (63%)
  starting transfers between devices  13.7 us (24%)
  waiting for transfers between devices  6.05 us (11%)
  between operations  0.82 us (1%)
    pallas_call x1, Pallas kernels, collide_far(): pl.pallas_call(far_kernel, in_specs=[pl.BlockSpec(memory_space=pltpu.SMEM...  12.2 us
    pallas_call x1, Pallas kernels, collide_near(): pl.pallas_call(near_kernel, in_specs=[pl.BlockSpec(memory_space=pltpu.SME...  11.4 us
    pallas_call x3, Pallas kernels, fetch(): pl.pallas_call(functools.partial(fetch_kernel, first=first, count=count),...  11.1 us
    ppermute x6, starting transfers between devices, exchanged(): lax.ppermute(x, axis, [(i, i ^ bit) for i in range(lax.axis_size(axis))])  10.3 us
    all_to_all x1, waiting for transfers between devices, local(): lax.all_to_all(block, 'cell', split_axis=0, concat_axis=0, tiled=False)  6.03 us
    all_to_all x1, starting transfers between devices, local(): lax.all_to_all(block, 'cell', split_axis=0, concat_axis=0, tiled=False)  3.36 us
  transfers between devices with their start and end apart: 7, of which 1 were waited for; matrix products, arithmetic and copies ran while one was open for 0% of the time, Pallas kernels for 41%

profile of v6, /device:TPU:0, one launch (start us, length us, event | category | flops | bytes accessed | tf_op | source)
XLA Modules:
  0.0 56.8 jit_solution(15983702392048679204)
XLA Ops:
  0.6 4.1 %collective-permute-start = (bf16[1,32,384]{2,1,0:T(8,128)(2,1)}, bf16[1,32,384]{2,1,0:T(8,128)(2,1)S(1)}, u32[]{:S(2)}, u32[]{:S(2)}) collective-permute-start(bf16[1,32,384]{2,1,0:T(8,128)(2,1)} %fields.1), channel_id=1, source_target_pairs={{0,16},{4,20},{8,24},{12,28},{16,0},{20,4},{24,8},{28,12},{1,17},{... | collective-permute-start | bytes 73736 | tf_op jit(solution)/shard_map/ppermute | solution.py:404
  4.7 3.7 %fetch.3 = (bf16[4,8,384,384]{3,2,1,0:T(8,128)(2,1)S(1)}, f32[8,128]{1,0:T(8,128)S(1)}) custom-call(bf16[4,48,384,384]{3,2,1,0:T(8,128)(2,1)} %tensors.9), custom_call_target="tpu_custom_call" | custom-call | bytes 18874368 | tf_op jit(solution)/shard_map/fetch/pallas_call | solution.py:79
  8.5 0.0 collective-permute-done.came
  8.5 1.6 %collective-permute-start.1 = (bf16[2,32,384]{2,1,0:T(8,128)(2,1)S(1)}, bf16[2,32,384]{2,1,0:T(8,128)(2,1)S(1)}, u32[]{:S(2)}, u32[]{:S(2)}) collective-permute-start(bf16[2,32,384]{2,1,0:T(8,128)(2,1)S(1)} %join.3.refs_0_.here), channel_id=1, source_target_pairs={{0,8},{4,12},{8,0},{12,4},{16,24},{20,28},{24,16},{28,20},{1,9},{5... | collective-permute-start | bytes 147464 | tf_op jit(solution)/shard_map/ppermute | solution.py:404
  10.1 3.7 %fetch.4 = (bf16[4,8,384,384]{3,2,1,0:T(8,128)(2,1)S(1)}, f32[8,128]{1,0:T(8,128)S(1)}) custom-call(bf16[4,48,384,384]{3,2,1,0:T(8,128)(2,1)} %tensors.9, bf16[2,32,384]{2,1,0:T(8,128)(2,1)S(1)} %join.3.refs_0_.here), custom_call_target="tpu_custom_call" | custom-call | bytes 18874368 | tf_op jit(solution)/shard_map/fetch/pallas_call | solution.py:79
  13.8 0.0 collective-permute-done.1.came
  13.9 0.0 copy-start.3
  13.9 1.6 %collective-permute-start.2 = (bf16[4,32,384]{2,1,0:T(8,128)(2,1)S(1)}, bf16[4,32,384]{2,1,0:T(8,128)(2,1)S(1)}, u32[]{:S(2)}, u32[]{:S(2)}) collective-permute-start(bf16[4,32,384]{2,1,0:T(8,128)(2,1)S(1)} %join.4.refs_0_.here), channel_id=1, source_target_pairs={{0,4},{4,0},{8,12},{12,8},{16,20},{20,16},{24,28},{28,24},{1,5},{5... | collective-permute-start | bytes 294920 | tf_op jit(solution)/shard_map/ppermute | solution.py:404
  15.4 3.7 %fetch.5 = (bf16[4,8,384,384]{3,2,1,0:T(8,128)(2,1)S(1)}, f32[8,128]{1,0:T(8,128)S(1)}) custom-call(bf16[4,48,384,384]{3,2,1,0:T(8,128)(2,1)} %tensors.9, bf16[4,32,384]{2,1,0:T(8,128)(2,1)S(1)} %join.4.refs_0_.here), custom_call_target="tpu_custom_call" | custom-call | bytes 18874368 | tf_op jit(solution)/shard_map/fetch/pallas_call | solution.py:79
  19.1 0.0 collective-permute-done.2.came
  19.2 0.1 collective-permute-start.4
  19.2 1.6 %collective-permute-start.3 = (bf16[8,32,384]{2,1,0:T(8,128)(2,1)S(1)}, bf16[8,32,384]{2,1,0:T(8,128)(2,1)S(1)}, u32[]{:S(2)}, u32[]{:S(2)}) collective-permute-start(bf16[8,32,384]{2,1,0:T(8,128)(2,1)S(1)} %join.5.mine), channel_id=1, source_target_pairs={{0,2},{1,3},{2,0},{3,1},{4,6},{5,7},{6,4},{7,5},{8,10},{9,11},{10,... | collective-permute-start | bytes 589832 | tf_op jit(solution)/shard_map/ppermute | solution.py:404
  20.8 0.0 collective-permute-done.4.mate
  20.8 1.4 %collective-permute-start.5 = (bf16[8,32,384]{2,1,0:T(8,128)(2,1)S(1)}, bf16[8,32,384]{2,1,0:T(8,128)(2,1)S(1)}, u32[]{:S(2)}, u32[]{:S(2)}) collective-permute-start(bf16[8,32,384]{2,1,0:T(8,128)(2,1)S(1)} %collective-permute-done.4.mate), channel_id=1, source_target_pairs={{0,2},{1,3},{2,0},{3,1},{4,6},{5,7},{6,4},{7,5},{8,10},{9,11},{10,... | collective-permute-start | bytes 589832 | tf_op jit(solution)/shard_map/ppermute | solution.py:404
  22.2 11.4 %collide_near.1 = (f32[48,256]{1,0:T(8,128)S(1)}, f32[384,256]{1,0:T(8,128)S(1)}) custom-call(s32[4,4]{1,0:T(4,128)S(1)} %copy-done.3, bf16[8,32,384]{2,1,0:T(8,128)(2,1)S(1)} %join.5.mine, bf16[8,32,384]{2,1,0:T(8,128)(2,1)S(1)} %collective-permute-done.4.mate, bf16[4,48,384,384]{3,2,1,0:T(8,128)(2,1)} %tensors.9, ...), custom_call_target="tpu_custom_call" | custom-call | flops 7247757312 | bytes 28311552 | tf_op jit(solution)/shard_map/collide_near/pallas_call | solution.py:253
  33.6 0.0 collective-permute-done.3.one
  33.6 0.0 collective-permute-done.5.two
  33.6 0.0 copy-start
  33.6 0.0 copy-start.1
  33.6 12.2 %collide_far.1 = f32[8,16,128]{2,1,0:T(8,128)} custom-call(s32[4,4]{1,0:T(4,128)S(1)} %copy-done.3, bf16[8,32,384]{2,1,0:T(8,128)(2,1)S(1)} %collective-permute-done.3.one, bf16[8,32,384]{2,1,0:T(8,128)(2,1)S(1)} %collective-permute-done.5.two, bf16[4,48,384,384]{3,2,1,0:T(8,128)(2,1)} %tensors.9, bf16[4,8,384,384]{3,2,1,0:T(8,128)(2,1)S(1)} %get-tuple-element.13.refs_0_, ...), custom_call_target="tpu_custom_call" | custom-call | flops 7247757312 | bytes 28311552 | tf_op jit(solution)/shard_map/collide_far/pallas_call | solution.py:294
  45.8 3.4 %all-to-all-start = ((f32[8,16,128]{2,1,0:T(8,128)}), f32[8,16,128]{2,1,0:T(8,128)S(1)}, u32[]{:S(2)}, u32[]{:S(2)}) async-start(f32[8,16,128]{2,1,0:T(8,128)} %collide_far.1), calls=%async_computation | async-start | bytes 131072 | tf_op jit(solution)/shard_map/all_to_all | solution.py:426
  49.2 0.8 %transport.1.flux = f32[40,384]{1,0:T(8,128)S(1)} custom-call(bf16[8,32,384]{2,1,0:T(8,128)(2,1)S(1)} %join.5.mine, s32[1,32]{1,0:T(1,128)S(1)} %copy-done.4, f32[1,384,384]{2,1,0:T(8,128)S(1)} %copy-done, f32[1,384,384]{2,1,0:T(8,128)S(1)} %copy-done.1), custom_call_target="tpu_custom_call" | custom-call | tf_op jit(solution)/shard_map/transport/pallas_call | solution.py:361
  50.0 6.0 %all-to-all-done.received = f32[8,16,128]{2,1,0:T(8,128)S(1)} async-done(((f32[8,16,128]{2,1,0:T(8,128)}), f32[8,16,128]{2,1,0:T(8,128)S(1)}, u32[]{:S(2)}, u32[]{:S(2)}) %all-to-all-start) | async-done | bytes 65568 | tf_op jit(solution)/shard_map/all_to_all | solution.py:426
  56.0 0.7 %finish.1 = (f32[1,32,384]{2,1,0:T(8,128)}, f32[1,32,384]{2,1,0:T(8,128)}) custom-call(f32[8,16,128]{2,1,0:T(8,128)S(1)} %all-to-all-done.received, f32[40,384]{1,0:T(8,128)S(1)} %transport.1.flux, bf16[1,32,384]{2,1,0:T(8,128)(2,1)S(1)} %copy-done.2), custom_call_target="tpu_custom_call" | custom-call | tf_op jit(solution)/shard_map/finish/pallas_call | solution.py:393
  (10 shorter events, 0.1 us)
Async XLA Ops:
  0.6 7.8 %copy-start.2 = (bf16[1,32,384]{2,1,0:T(8,128)(2,1)S(1)}, bf16[1,32,384]{2,1,0:T(8,128)(2,1)}, u32[]{:S(2)}) copy-start(bf16[1,32,384]{2,1,0:T(8,128)(2,1)} %fields.1) | copy-start | bytes 73732
  0.6 7.8 %collective-permute-start = (bf16[1,32,384]{2,1,0:T(8,128)(2,1)}, bf16[1,32,384]{2,1,0:T(8,128)(2,1)S(1)}, u32[]{:S(2)}, u32[]{:S(2)}) collective-permute-start(bf16[1,32,384]{2,1,0:T(8,128)(2,1)} %fields.1), channel_id=1, source_target_pairs={{0,16},{4,20},{8,24},{12,28},{16,0},{20,4},{24,8},{28,12},{1,17},{... | collective-permute-start | bytes 73736 | tf_op jit(solution)/shard_map/ppermute | solution.py:404
  8.5 5.3 %collective-permute-start.1 = (bf16[2,32,384]{2,1,0:T(8,128)(2,1)S(1)}, bf16[2,32,384]{2,1,0:T(8,128)(2,1)S(1)}, u32[]{:S(2)}, u32[]{:S(2)}) collective-permute-start(bf16[2,32,384]{2,1,0:T(8,128)(2,1)S(1)} %join.3.refs_0_.here), channel_id=1, source_target_pairs={{0,8},{4,12},{8,0},{12,4},{16,24},{20,28},{24,16},{28,20},{1,9},{5... | collective-permute-start | bytes 147464 | tf_op jit(solution)/shard_map/ppermute | solution.py:404
  13.9 8.3 %copy-start.3 = (s32[4,4]{1,0:T(4,128)S(1)}, s32[4,4]{1,0:T(4,128)}, u32[]{:S(2)}) copy-start(s32[4,4]{1,0:T(4,128)} %table.3) | copy-start | bytes 196
  13.9 5.3 %collective-permute-start.2 = (bf16[4,32,384]{2,1,0:T(8,128)(2,1)S(1)}, bf16[4,32,384]{2,1,0:T(8,128)(2,1)S(1)}, u32[]{:S(2)}, u32[]{:S(2)}) collective-permute-start(bf16[4,32,384]{2,1,0:T(8,128)(2,1)S(1)} %join.4.refs_0_.here), channel_id=1, source_target_pairs={{0,4},{4,0},{8,12},{12,8},{16,20},{20,16},{24,28},{28,24},{1,5},{5... | collective-permute-start | bytes 294920 | tf_op jit(solution)/shard_map/ppermute | solution.py:404
  19.2 1.7 %collective-permute-start.4 = (bf16[8,32,384]{2,1,0:T(8,128)(2,1)S(1)}, bf16[8,32,384]{2,1,0:T(8,128)(2,1)S(1)}, u32[]{:S(2)}, u32[]{:S(2)}) collective-permute-start(bf16[8,32,384]{2,1,0:T(8,128)(2,1)S(1)} %join.5.mine), channel_id=1, source_target_pairs={{0,1},{1,0},{2,3},{3,2},{4,5},{5,4},{6,7},{7,6},{8,9},{9,8},{10,11... | collective-permute-start | bytes 589832 | tf_op jit(solution)/shard_map/ppermute | solution.py:404
  19.2 14.3 %collective-permute-start.3 = (bf16[8,32,384]{2,1,0:T(8,128)(2,1)S(1)}, bf16[8,32,384]{2,1,0:T(8,128)(2,1)S(1)}, u32[]{:S(2)}, u32[]{:S(2)}) collective-permute-start(bf16[8,32,384]{2,1,0:T(8,128)(2,1)S(1)} %join.5.mine), channel_id=1, source_target_pairs={{0,2},{1,3},{2,0},{3,1},{4,6},{5,7},{6,4},{7,5},{8,10},{9,11},{10,... | collective-permute-start | bytes 589832 | tf_op jit(solution)/shard_map/ppermute | solution.py:404
  20.8 12.8 %collective-permute-start.5 = (bf16[8,32,384]{2,1,0:T(8,128)(2,1)S(1)}, bf16[8,32,384]{2,1,0:T(8,128)(2,1)S(1)}, u32[]{:S(2)}, u32[]{:S(2)}) collective-permute-start(bf16[8,32,384]{2,1,0:T(8,128)(2,1)S(1)} %collective-permute-done.4.mate), channel_id=1, source_target_pairs={{0,2},{1,3},{2,0},{3,1},{4,6},{5,7},{6,4},{7,5},{8,10},{9,11},{10,... | collective-permute-start | bytes 589832 | tf_op jit(solution)/shard_map/ppermute | solution.py:404
  22.2 11.4 %copy-start.4 = (s32[1,32]{1,0:T(1,128)S(1)}, s32[1,32]{1,0:T(1,128)}, u32[]{:S(2)}) copy-start(s32[1,32]{1,0:T(1,128)} %limiter.1) | copy-start | bytes 388
  33.6 15.6 %copy-start = (f32[1,384,384]{2,1,0:T(8,128)S(1)}, f32[1,384,384]{2,1,0:T(8,128)}, u32[]{:S(2)}) copy-start(f32[1,384,384]{2,1,0:T(8,128)} %plus.1) | copy-start | bytes 1769476
  33.6 15.6 %copy-start.1 = (f32[1,384,384]{2,1,0:T(8,128)S(1)}, f32[1,384,384]{2,1,0:T(8,128)}, u32[]{:S(2)}) copy-start(f32[1,384,384]{2,1,0:T(8,128)} %minus.1) | copy-start | bytes 1769476
  45.8 10.2 %all-to-all-start = ((f32[8,16,128]{2,1,0:T(8,128)}), f32[8,16,128]{2,1,0:T(8,128)S(1)}, u32[]{:S(2)}, u32[]{:S(2)}) async-start(f32[8,16,128]{2,1,0:T(8,128)} %collide_far.1), calls=%async_computation | async-start | bytes 131072 | tf_op jit(solution)/shard_map/all_to_all | solution.py:426

commit v7 on v6

--- a/solution.py
+++ b/solution.py
@@ -9,7 +9,7 @@
 
 LANES = 128
 MIB = 1 << 20
-SETS = 3
+SIXTHS = 6
 
 
 def minmod_two(first, second):
@@ -63,33 +63,76 @@
     return table[owner, owner ^ partner] - owner * table.shape[0]
 
 
-def fetch_kernel(tensors, *refs, first, count):
-    near, token, sem = refs[-3:]
-    copy = pltpu.make_async_copy(tensors.at[:, pl.ds(first, count)], near, sem)
+def copies_of(table, tensors, partners, first, near, sems):
+    modes = pl.ds(first, near.shape[1])
+    return [
+        pltpu.make_async_copy(
+            tensors.at[tensor_of(table, partner), modes], near.at[at], sems.at[at]
+        )
+        for at, partner in enumerate(partners)
+    ]
+
+
+def start_all(copies):
+    for copy in copies:
+        copy.start()
+
+
+def wait_all(copies):
+    for copy in copies:
+        copy.wait()
+
+
+def fetch_all_kernel(tensors, near, token, sem):
+    copy = pltpu.make_async_copy(tensors.at[:, pl.ds(0, near.shape[1])], near, sem)
     copy.start()
     token[...] = jnp.zeros_like(token)
     copy.wait()
 
 
-def fetch(after, tensors, first, count):
-    shape = (tensors.shape[0], count) + tensors.shape[2:]
-    anywhere = pl.BlockSpec(memory_space=pl.ANY)
-    vmem = pl.BlockSpec(memory_space=pltpu.VMEM)
-    held = [] if after is None else [close(after)]
-    return pl.pallas_call(
-        functools.partial(fetch_kernel, first=first, count=count),
-        in_specs=[anywhere] + [vmem] * len(held),
+def fetch_near_kernel(table, after, tensors, near, token, sems, *, first):
+    copies = copies_of(table, tensors, (0, 1), first, near, sems)
+    start_all(copies)
+    token[...] = jnp.zeros_like(token)
+    wait_all(copies)
+
+
+def fetch(kernel, operands, specs, tensors, species, count, sems):
+    shape = (species, count) + tensors.shape[2:]
+    vmem = pl.BlockSpec(memory_space=pltpu.VMEM)
+    return pl.pallas_call(
+        kernel,
+        in_specs=specs + [pl.BlockSpec(memory_space=pl.ANY)],
         out_specs=(vmem, vmem),
-        scratch_shapes=[pltpu.SemaphoreType.DMA],
+        scratch_shapes=[sems],
         out_shape=(pltpu.VMEM(shape, tensors.dtype), pltpu.VMEM((8, LANES), jnp.float32)),
         compiler_params=pltpu.CompilerParams(vmem_limit_bytes=MIB),
         cost_estimate=pl.CostEstimate(
             flops=0,
             transcendentals=0,
-            bytes_accessed=4 * tensors.shape[0] * count * tensors.shape[2] * tensors.shape[3],
+            bytes_accessed=4 * species * count * tensors.shape[2] * tensors.shape[3],
         ),
         name="fetch",
-    )(tensors, *held)
+    )(*operands, tensors)
+
+
+def fetch_all(tensors, count):
+    return fetch(
+        fetch_all_kernel, [], [], tensors, tensors.shape[0], count, pltpu.SemaphoreType.DMA
+    )
+
+
+def fetch_near(table, after, tensors, first, count):
+    specs = [pl.BlockSpec(memory_space=pltpu.SMEM), pl.BlockSpec(memory_space=pltpu.VMEM)]
+    return fetch(
+        functools.partial(fetch_near_kernel, first=first),
+        [table, close(after)],
+        specs,
+        tensors,
+        2,
+        count,
+        pltpu.SemaphoreType.DMA((2,)),
+    )
 
 
 def join_kernel(here, came, token, out):
@@ -110,7 +153,7 @@
     )(close(here), close(came), close(token))
 
 
-def contract(parts, others, own, total, add, ready):
+def contract(parts, others, own, total, add):
     groups, cells, modes = others[0].shape
     everyone = groups * cells
     width = 2 * LANES
@@ -145,7 +188,7 @@
                 columns = columns_of(span)
                 inner = pltpu.matmul_pop(sums[2 * unit + bank])
                 row = jnp.sum(inner * own[:, columns], axis=0, keepdims=True)
-                place = pl.ds(sum(count for _, count in parts[:part]) + k, 1)
+                place = pl.ds(sum(count for _, count, _ in parts[:part]) + k, 1)
                 total[place, columns] = row + add[place, columns] if add is not None else row
 
         def work(part, pair, bank, start, follower, pending):
@@ -170,19 +213,12 @@
         for part in range(len(parts)):
             last = part + 1 == len(parts)
             pairs = parts[part][1] * spans // 2
-            if last:
-                ready(0)
+            parts[part][2]()
             at = work(part, 0, 0, at, 1, pending)
             odd = at
 
             @pl.loop(0, (pairs - 2) // 2)
             def _(step):
-                for number in range(1, SETS if last else 0):
-
-                    @pl.when(step == (number * (pairs // SETS) - 1) // 2)
-                    def _():
-                        ready(number)
-
                 now = work(part, 2 * step + 1, 1, odd, 2 * step + 2, (part, 2 * step, 0))
                 work(part, 2 * step + 2, 0, now, 2 * step + 3, (part, 2 * step + 1, 1))
 
@@ -194,83 +230,65 @@
     pl.run_scoped(run, *[pltpu.ACC(unit)((modes, width), jnp.float32) for unit in (0, 0, 1, 1)])
 
 
-def stream(table, tensors, held, beside, sems, partners):
-    done = sum(ref.shape[1] for ref in held)
-    count = beside.shape[1] // SETS
-    picks = [tensor_of(table, partner) for partner in partners]
-
-    def copies(number):
-        return [
-            pltpu.make_async_copy(
-                tensors.at[pick, pl.ds(done + number * count, count)],
-                beside.at[at, pl.ds(number * count, count)],
-                sems.at[at, number],
-            )
-            for at, pick in enumerate(picks)
-        ]
-
-    def start(number):
-        for copy in copies(number):
-            copy.start()
-
-    def ready(number):
-        for copy in copies(number):
-            copy.wait()
-        if number + 2 < SETS:
-            start(number + 2)
-
-    def early(ref):
-        return lambda p, k, lanes: ref[picks[p], k, :, lanes]
-
-    def late(p, k, lanes):
-        return beside[p, k, :, lanes]
-
-    start(0)
-    start(1)
-    return [(early(ref), ref.shape[1]) for ref in held] + [(late, beside.shape[1])], ready
-
-
-def near_kernel(table, mine, mate, tensors, *refs):
-    held, (total, own, beside, sems) = refs[:SETS], refs[SETS:]
-    parts, ready = stream(table, tensors, held, beside, sems, (0, 1))
+def part_of(ref, picks=None, shift=0, count=None, before=lambda: None):
+    def read(p, k, lanes):
+        return ref[p if picks is None else picks[p], shift + k, :, lanes]
+
+    return read, ref.shape[1] if count is None else count, before
+
+
+def near_kernel(
+    table, mine, mate, tensors, shared, two, three, total, own, far, beside, far_sems, sems
+):
+    first = shared.shape[1]
+    last = copies_of(table, tensors, (0, 1), tensors.shape[1] - first, beside, sems)
+    later = copies_of(table, tensors, (2, 3), first, far, far_sems)
+    start_all(last + later)
     own[...] = mine[...].reshape(own.shape[::-1]).astype(jnp.float32).T
-    contract(parts, (mine, mate), own, total, None, ready)
-
-
-def streamed(tensors, held):
-    left = tensors.shape[1] - sum(part.shape[1] for part in held)
-    return [
-        pltpu.VMEM((2, left) + tensors.shape[2:], tensors.dtype),
-        pltpu.SemaphoreType.DMA((2, SETS)),
-    ]
-
-
-def collide_near(table, mine, mate, tensors, held):
+    picks = [tensor_of(table, partner) for partner in (0, 1)]
+    parts = [part_of(shared, picks), part_of(two), part_of(three)]
+    parts.append(part_of(beside, before=lambda: wait_all(last)))
+    contract(parts, (mine, mate), own, total, None)
+    wait_all(later)
+
+
+def collide_near(table, mine, mate, tensors, shared, two, three):
     groups, cells, modes = mine.shape
     out_modes = tensors.shape[1]
+    ahead = out_modes // 2
     vmem = pl.BlockSpec(memory_space=pltpu.VMEM)
     anywhere = pl.BlockSpec(memory_space=pl.ANY)
     return pl.pallas_call(
         near_kernel,
-        in_specs=[pl.BlockSpec(memory_space=pltpu.SMEM), vmem, vmem, anywhere] + [vmem] * SETS,
-        out_specs=(vmem, vmem),
-        scratch_shapes=streamed(tensors, held),
+        in_specs=[pl.BlockSpec(memory_space=pltpu.SMEM), vmem, vmem, anywhere] + [vmem] * 3,
+        out_specs=(vmem, vmem, vmem),
+        scratch_shapes=[
+            pltpu.VMEM((2, shared.shape[1]) + tensors.shape[2:], tensors.dtype),
+            pltpu.SemaphoreType.DMA((2,)),
+            pltpu.SemaphoreType.DMA((2,)),
+        ],
         out_shape=(
             pltpu.VMEM((out_modes, groups * cells), jnp.float32),
             pltpu.VMEM((modes, groups * cells), jnp.float32),
+            pltpu.VMEM((2, ahead) + tensors.shape[2:], tensors.dtype),
         ),
-        compiler_params=pltpu.CompilerParams(vmem_limit_bytes=16 * MIB),
+        compiler_params=pltpu.CompilerParams(vmem_limit_bytes=7 * MIB),
         cost_estimate=pl.CostEstimate(
             flops=tensors.size * groups * cells, transcendentals=0, bytes_accessed=tensors.size
         ),
         name="collide_near",
-    )(table, close(mine), close(mate), tensors, *[close(part) for part in held])
-
-
-def far_kernel(table, one, two, tensors, *refs):
-    held, (first, own, limiter, out, total, beside, sems) = refs[:SETS], refs[SETS:]
-    parts, ready = stream(table, tensors, held, beside, sems, (2, 3))
-    contract(parts, (one, two), own, total, first, ready)
+    )(table, close(mine), close(mate), tensors, close(shared), close(two), close(three))
+
+
+def far_kernel(
+    table, one, two, tensors, shared, far, first, own, limiter, out, total, beside, sems
+):
+    last = copies_of(table, tensors, (2, 3), tensors.shape[1] - beside.shape[1], beside, sems)
+    start_all(last)
+    picks = [tensor_of(table, partner) for partner in (2, 3)]
+    parts = [part_of(shared, picks), part_of(far)]
+    parts.append(part_of(beside, before=lambda: wait_all(last)))
+    contract(parts, (one, two), own, total, first)
     groups, cells, _ = one.shape
     here = lax.axis_index("cell")
     whole = total[...].T
@@ -285,22 +303,24 @@
         out[here ^ reverse(d, groups)] = jnp.concatenate(parts + [spare], axis=1)
 
 
-def collide_far(table, one, two, tensors, held, first, own, limiter):
+def collide_far(table, one, two, tensors, shared, far, first, own, limiter):
     groups, cells, modes = one.shape
     out_modes = tensors.shape[1]
     rows = cells // fold_of(cells, out_modes)
+    left = out_modes - shared.shape[1] - far.shape[1]
     vmem = pl.BlockSpec(memory_space=pltpu.VMEM)
     anywhere = pl.BlockSpec(memory_space=pl.ANY)
     return pl.pallas_call(
         far_kernel,
-        in_specs=[pl.BlockSpec(memory_space=pltpu.SMEM), vmem, vmem, anywhere] + [vmem] * (SETS + 3),
+        in_specs=[pl.BlockSpec(memory_space=pltpu.SMEM), vmem, vmem, anywhere] + [vmem] * 5,
         out_specs=vmem,
         scratch_shapes=[
             pltpu.VMEM((out_modes, groups * cells), jnp.float32),
-            *streamed(tensors, held),
+            pltpu.VMEM((2, left) + tensors.shape[2:], tensors.dtype),
+            pltpu.SemaphoreType.DMA((2,)),
         ],
         out_shape=pltpu.VMEM((groups, rows, LANES), jnp.float32),
-        compiler_params=pltpu.CompilerParams(vmem_limit_bytes=16 * MIB),
+        compiler_params=pltpu.CompilerParams(vmem_limit_bytes=11 * MIB),
         cost_estimate=pl.CostEstimate(
             flops=tensors.size * groups * cells, transcendentals=0, bytes_accessed=tensors.size
         ),
@@ -310,7 +330,8 @@
         close(one),
         close(two),
         tensors,
-        *[close(part) for part in held],
+        close(shared),
+        close(far),
         close(first),
         close(own),
         limiter,
@@ -406,23 +427,31 @@
 
 def local(fields, tensors, pair_table, plus_flux, minus_flux, face_limiter):
     groups = lax.axis_size("cell")
-    count = tensors.shape[1] // (2 * SETS)
+    count = tensors.shape[1] // SIXTHS
     mine, held, token = fields, [], None
+
+    def more():
+        if not held:
+            return fetch_all(tensors, count)
+        return fetch_near(pair_table, mine, tensors, (2 * len(held) - 1) * count, 2 * count)
+
     bit = groups // 2
     while bit > 0:
         came = exchanged(mine, "cell", bit)
-        if len(held) < SETS:
-            part, token = fetch(mine if held else None, tensors, len(held) * count, count)
+        if len(held) < 3:
+            part, token = more()
             held.append(part)
         mine = join(mine, came, token)
         bit //= 2
-    while len(held) < SETS:
-        held.append(fetch(mine, tensors, len(held) * count, count)[0])
+    while len(held) < 3:
+        held.append(more()[0])
     mate = exchanged(mine, "spec", 1)
     far_one = exchanged(mine, "spec", 2)
     far_two = exchanged(mate, "spec", 2)
-    first, own = collide_near(pair_table, mine, mate, tensors, held)
-    block = collide_far(pair_table, far_one, far_two, tensors, held, first, own, face_limiter)
+    first, own, far = collide_near(pair_table, mine, mate, tensors, *held)
+    block = collide_far(
+        pair_table, far_one, far_two, tensors, held[0], far, first, own, face_limiter
+    )
     received = lax.all_to_all(block, "cell", split_axis=0, concat_axis=0, tiled=False)
     flux = transport(mine, face_limiter, plus_flux, minus_flux)
     return finish(received, flux, fields, tensors.shape[1])

time: 57.1 us -> 52.5 us (0.919)
  Pallas kernels: 36.2 us -> 31.5 us
    pallas_call x1, Pallas kernels: 12.2 us -> 9.13 us  [collide_far(): pl.pallas_call(far_kernel, in_specs=[pl.BlockSpec(memory_space=pltpu.SMEM...]
    pallas_call x1, Pallas kernels: 11.4 us -> 8.33 us  [collide_near(): pl.pallas_call(near_kernel, in_specs=[pl.BlockSpec(memory_space=pltpu.SME...]
    pallas_call x3, Pallas kernels: 11.1 us -> 12.4 us  [fetch(): pl.pallas_call(kernel, in_specs=specs + [pl.BlockSpec(memory_space=pl.ANY...]
  transfers between devices with their start and end apart: 7 -> 7, of which waited for: 1 -> 2; matrix products, arithmetic and copies ran while one was open for 0% -> 0% of each run, Pallas kernels for 41% -> 41%
where the time goes in v7:
time: 52.5 us; the launch traced here: 52.2 us
  Pallas kernels  31.5 us (60%)
  starting transfers between devices  13.7 us (26%)
  waiting for transfers between devices  6.28 us (12%)
  between operations  0.79 us (2%)
    pallas_call x3, Pallas kernels, fetch(): pl.pallas_call(kernel, in_specs=specs + [pl.BlockSpec(memory_space=pl.ANY...  12.4 us
    ppermute x6, starting transfers between devices, exchanged(): lax.ppermute(x, axis, [(i, i ^ bit) for i in range(lax.axis_size(axis))])  10.3 us
    pallas_call x1, Pallas kernels, collide_far(): pl.pallas_call(far_kernel, in_specs=[pl.BlockSpec(memory_space=pltpu.SMEM...  9.13 us
    pallas_call x1, Pallas kernels, collide_near(): pl.pallas_call(near_kernel, in_specs=[pl.BlockSpec(memory_space=pltpu.SME...  8.33 us
    all_to_all x1, waiting for transfers between devices, local(): lax.all_to_all(block, 'cell', split_axis=0, concat_axis=0, tiled=False)  6.03 us
    all_to_all x1, starting transfers between devices, local(): lax.all_to_all(block, 'cell', split_axis=0, concat_axis=0, tiled=False)  3.36 us
  transfers between devices with their start and end apart: 7, of which 2 were waited for; matrix products, arithmetic and copies ran while one was open for 0% of the time, Pallas kernels for 41%

profile of v7, /device:TPU:0, one launch (start us, length us, event | category | flops | bytes accessed | tf_op | source)
XLA Modules:
  0.0 52.2 jit_solution(11287768734908034425)
XLA Ops:
  0.6 0.0 copy-start.2
  0.6 0.0 copy-start.3
  0.6 4.1 %collective-permute-start = (bf16[1,32,384]{2,1,0:T(8,128)(2,1)}, bf16[1,32,384]{2,1,0:T(8,128)(2,1)S(1)}, u32[]{:S(2)}, u32[]{:S(2)}) collective-permute-start(bf16[1,32,384]{2,1,0:T(8,128)(2,1)} %fields.1), channel_id=1, source_target_pairs={{0,16},{4,20},{8,24},{12,28},{16,0},{20,4},{24,8},{28,12},{1,17},{... | collective-permute-start | bytes 73736 | tf_op jit(solution)/shard_map/ppermute | solution.py:425
  4.8 3.7 %fetch.3 = (bf16[4,8,384,384]{3,2,1,0:T(8,128)(2,1)S(1)}, f32[8,128]{1,0:T(8,128)S(1)}) custom-call(bf16[4,48,384,384]{3,2,1,0:T(8,128)(2,1)} %tensors.9), custom_call_target="tpu_custom_call" | custom-call | bytes 18874368 | tf_op jit(solution)/shard_map/fetch/pallas_call | solution.py:103
  8.5 0.0 collective-permute-done.came
  8.5 1.6 %collective-permute-start.1 = (bf16[2,32,384]{2,1,0:T(8,128)(2,1)S(1)}, bf16[2,32,384]{2,1,0:T(8,128)(2,1)S(1)}, u32[]{:S(2)}, u32[]{:S(2)}) collective-permute-start(bf16[2,32,384]{2,1,0:T(8,128)(2,1)S(1)} %join.3.after.here), channel_id=1, source_target_pairs={{0,8},{4,12},{8,0},{12,4},{16,24},{20,28},{24,16},{28,20},{1,9},{5... | collective-permute-start | bytes 147464 | tf_op jit(solution)/shard_map/ppermute | solution.py:425
  10.1 0.0 copy-done.3
  10.1 4.4 %fetch.4 = (bf16[2,16,384,384]{3,2,1,0:T(8,128)(2,1)S(1)}, f32[8,128]{1,0:T(8,128)S(1)}) custom-call(s32[4,4]{1,0:T(4,128)S(1)} %copy-done.3, bf16[2,32,384]{2,1,0:T(8,128)(2,1)S(1)} %join.3.after.here, bf16[4,48,384,384]{3,2,1,0:T(8,128)(2,1)} %tensors.9), custom_call_target="tpu_custom_call" | custom-call | bytes 18874368 | tf_op jit(solution)/shard_map/fetch/pallas_call | solution.py:103
  14.5 0.0 collective-permute-done.1.came
  14.6 1.6 %collective-permute-start.2 = (bf16[4,32,384]{2,1,0:T(8,128)(2,1)S(1)}, bf16[4,32,384]{2,1,0:T(8,128)(2,1)S(1)}, u32[]{:S(2)}, u32[]{:S(2)}) collective-permute-start(bf16[4,32,384]{2,1,0:T(8,128)(2,1)S(1)} %join.4.after.here), channel_id=1, source_target_pairs={{0,4},{4,0},{8,12},{12,8},{16,20},{20,16},{24,28},{28,24},{1,5},{5... | collective-permute-start | bytes 294920 | tf_op jit(solution)/shard_map/ppermute | solution.py:425
  16.1 4.4 %fetch.5 = (bf16[2,16,384,384]{3,2,1,0:T(8,128)(2,1)S(1)}, f32[8,128]{1,0:T(8,128)S(1)}) custom-call(s32[4,4]{1,0:T(4,128)S(1)} %copy-done.3, bf16[4,32,384]{2,1,0:T(8,128)(2,1)S(1)} %join.4.after.here, bf16[4,48,384,384]{3,2,1,0:T(8,128)(2,1)} %tensors.9), custom_call_target="tpu_custom_call" | custom-call | bytes 18874368 | tf_op jit(solution)/shard_map/fetch/pallas_call | solution.py:103
  20.5 0.0 collective-permute-done.2.came
  20.5 0.1 collective-permute-start.4
  20.6 1.6 %collective-permute-start.3 = (bf16[8,32,384]{2,1,0:T(8,128)(2,1)S(1)}, bf16[8,32,384]{2,1,0:T(8,128)(2,1)S(1)}, u32[]{:S(2)}, u32[]{:S(2)}) collective-permute-start(bf16[8,32,384]{2,1,0:T(8,128)(2,1)S(1)} %join.5.mine), channel_id=1, source_target_pairs={{0,2},{1,3},{2,0},{3,1},{4,6},{5,7},{6,4},{7,5},{8,10},{9,11},{10,... | collective-permute-start | bytes 589832 | tf_op jit(solution)/shard_map/ppermute | solution.py:425
  22.2 0.0 collective-permute-done.4.mate
  22.2 1.4 %collective-permute-start.5 = (bf16[8,32,384]{2,1,0:T(8,128)(2,1)S(1)}, bf16[8,32,384]{2,1,0:T(8,128)(2,1)S(1)}, u32[]{:S(2)}, u32[]{:S(2)}) collective-permute-start(bf16[8,32,384]{2,1,0:T(8,128)(2,1)S(1)} %collective-permute-done.4.mate), channel_id=1, source_target_pairs={{0,2},{1,3},{2,0},{3,1},{4,6},{5,7},{6,4},{7,5},{8,10},{9,11},{10,... | collective-permute-start | bytes 589832 | tf_op jit(solution)/shard_map/ppermute | solution.py:425
  23.6 8.3 %collide_near.1 = (f32[48,256]{1,0:T(8,128)S(1)}, f32[384,256]{1,0:T(8,128)S(1)}, bf16[2,24,384,384]{3,2,1,0:T(8,128)(2,1)S(1)}) custom-call(s32[4,4]{1,0:T(4,128)S(1)} %copy-done.3, bf16[8,32,384]{2,1,0:T(8,128)(2,1)S(1)} %join.5.mine, bf16[8,32,384]{2,1,0:T(8,128)(2,1)S(1)} %collective-permute-done.4.mate, bf16[4,48,384,384]{3,2,1,0:T(8,128)(2,1)} %tensors.9, ...), custom_call_target="tpu_custom_call" | custom-call | flops 7247757312 | bytes 28311552 | tf_op jit(solution)/shard_map/collide_near/pallas_call | solution.py:261
  31.9 0.0 collective-permute-done.3.one
  31.9 0.2 collective-permute-done.5.two
  32.1 9.1 %collide_far.1 = f32[8,16,128]{2,1,0:T(8,128)} custom-call(s32[4,4]{1,0:T(4,128)S(1)} %copy-done.3, bf16[8,32,384]{2,1,0:T(8,128)(2,1)S(1)} %collective-permute-done.3.one, bf16[8,32,384]{2,1,0:T(8,128)(2,1)S(1)} %collective-permute-done.5.two, bf16[4,48,384,384]{3,2,1,0:T(8,128)(2,1)} %tensors.9, bf16[4,8,384,384]{3,2,1,0:T(8,128)(2,1)S(1)} %get-tuple-element.14.shared, ...), custom_call_target="tpu_custom_call" | custom-call | flops 7247757312 | bytes 28311552 | tf_op jit(solution)/shard_map/collide_far/pallas_call | solution.py:313
  41.3 3.4 %all-to-all-start = ((f32[8,16,128]{2,1,0:T(8,128)}), f32[8,16,128]{2,1,0:T(8,128)S(1)}, u32[]{:S(2)}, u32[]{:S(2)}) async-start(f32[8,16,128]{2,1,0:T(8,128)} %collide_far.1), calls=%async_computation | async-start | bytes 131072 | tf_op jit(solution)/shard_map/all_to_all | solution.py:455
  44.7 0.8 %transport.1.flux = f32[40,384]{1,0:T(8,128)S(1)} custom-call(bf16[8,32,384]{2,1,0:T(8,128)(2,1)S(1)} %join.5.mine, s32[1,32]{1,0:T(1,128)S(1)} %copy-done.4, f32[1,384,384]{2,1,0:T(8,128)S(1)} %copy-done, f32[1,384,384]{2,1,0:T(8,128)S(1)} %copy-done.1), custom_call_target="tpu_custom_call" | custom-call | tf_op jit(solution)/shard_map/transport/pallas_call | solution.py:382
  45.5 6.0 %all-to-all-done.received = f32[8,16,128]{2,1,0:T(8,128)S(1)} async-done(((f32[8,16,128]{2,1,0:T(8,128)}), f32[8,16,128]{2,1,0:T(8,128)S(1)}, u32[]{:S(2)}, u32[]{:S(2)}) %all-to-all-start) | async-done | bytes 65568 | tf_op jit(solution)/shard_map/all_to_all | solution.py:455
  51.5 0.7 %finish.1 = (f32[1,32,384]{2,1,0:T(8,128)}, f32[1,32,384]{2,1,0:T(8,128)}) custom-call(f32[8,16,128]{2,1,0:T(8,128)S(1)} %all-to-all-done.received, f32[40,384]{1,0:T(8,128)S(1)} %transport.1.flux, bf16[1,32,384]{2,1,0:T(8,128)(2,1)S(1)} %copy-done.2), custom_call_target="tpu_custom_call" | custom-call | tf_op jit(solution)/shard_map/finish/pallas_call | solution.py:414
  (10 shorter events, 0.1 us)
Async XLA Ops:
  0.6 7.8 %copy-start.2 = (bf16[1,32,384]{2,1,0:T(8,128)(2,1)S(1)}, bf16[1,32,384]{2,1,0:T(8,128)(2,1)}, u32[]{:S(2)}) copy-start(bf16[1,32,384]{2,1,0:T(8,128)(2,1)} %fields.1) | copy-start | bytes 73732
  0.6 9.5 %copy-start.3 = (s32[4,4]{1,0:T(4,128)S(1)}, s32[4,4]{1,0:T(4,128)}, u32[]{:S(2)}) copy-start(s32[4,4]{1,0:T(4,128)} %table.7) | copy-start | bytes 196
  0.6 7.8 %collective-permute-start = (bf16[1,32,384]{2,1,0:T(8,128)(2,1)}, bf16[1,32,384]{2,1,0:T(8,128)(2,1)S(1)}, u32[]{:S(2)}, u32[]{:S(2)}) collective-permute-start(bf16[1,32,384]{2,1,0:T(8,128)(2,1)} %fields.1), channel_id=1, source_target_pairs={{0,16},{4,20},{8,24},{12,28},{16,0},{20,4},{24,8},{28,12},{1,17},{... | collective-permute-start | bytes 73736 | tf_op jit(solution)/shard_map/ppermute | solution.py:425
  8.5 6.0 %collective-permute-start.1 = (bf16[2,32,384]{2,1,0:T(8,128)(2,1)S(1)}, bf16[2,32,384]{2,1,0:T(8,128)(2,1)S(1)}, u32[]{:S(2)}, u32[]{:S(2)}) collective-permute-start(bf16[2,32,384]{2,1,0:T(8,128)(2,1)S(1)} %join.3.after.here), channel_id=1, source_target_pairs={{0,8},{4,12},{8,0},{12,4},{16,24},{20,28},{24,16},{28,20},{1,9},{5... | collective-permute-start | bytes 147464 | tf_op jit(solution)/shard_map/ppermute | solution.py:425
  14.6 5.9 %collective-permute-start.2 = (bf16[4,32,384]{2,1,0:T(8,128)(2,1)S(1)}, bf16[4,32,384]{2,1,0:T(8,128)(2,1)S(1)}, u32[]{:S(2)}, u32[]{:S(2)}) collective-permute-start(bf16[4,32,384]{2,1,0:T(8,128)(2,1)S(1)} %join.4.after.here), channel_id=1, source_target_pairs={{0,4},{4,0},{8,12},{12,8},{16,20},{20,16},{24,28},{28,24},{1,5},{5... | collective-permute-start | bytes 294920 | tf_op jit(solution)/shard_map/ppermute | solution.py:425
  20.5 1.7 %collective-permute-start.4 = (bf16[8,32,384]{2,1,0:T(8,128)(2,1)S(1)}, bf16[8,32,384]{2,1,0:T(8,128)(2,1)S(1)}, u32[]{:S(2)}, u32[]{:S(2)}) collective-permute-start(bf16[8,32,384]{2,1,0:T(8,128)(2,1)S(1)} %join.5.mine), channel_id=1, source_target_pairs={{0,1},{1,0},{2,3},{3,2},{4,5},{5,4},{6,7},{7,6},{8,9},{9,8},{10,11... | collective-permute-start | bytes 589832 | tf_op jit(solution)/shard_map/ppermute | solution.py:425
  20.6 11.3 %collective-permute-start.3 = (bf16[8,32,384]{2,1,0:T(8,128)(2,1)S(1)}, bf16[8,32,384]{2,1,0:T(8,128)(2,1)S(1)}, u32[]{:S(2)}, u32[]{:S(2)}) collective-permute-start(bf16[8,32,384]{2,1,0:T(8,128)(2,1)S(1)} %join.5.mine), channel_id=1, source_target_pairs={{0,2},{1,3},{2,0},{3,1},{4,6},{5,7},{6,4},{7,5},{8,10},{9,11},{10,... | collective-permute-start | bytes 589832 | tf_op jit(solution)/shard_map/ppermute | solution.py:425
  22.2 9.9 %collective-permute-start.5 = (bf16[8,32,384]{2,1,0:T(8,128)(2,1)S(1)}, bf16[8,32,384]{2,1,0:T(8,128)(2,1)S(1)}, u32[]{:S(2)}, u32[]{:S(2)}) collective-permute-start(bf16[8,32,384]{2,1,0:T(8,128)(2,1)S(1)} %collective-permute-done.4.mate), channel_id=1, source_target_pairs={{0,2},{1,3},{2,0},{3,1},{4,6},{5,7},{6,4},{7,5},{8,10},{9,11},{10,... | collective-permute-start | bytes 589832 | tf_op jit(solution)/shard_map/ppermute | solution.py:425
  23.6 8.6 %copy-start.4 = (s32[1,32]{1,0:T(1,128)S(1)}, s32[1,32]{1,0:T(1,128)}, u32[]{:S(2)}) copy-start(s32[1,32]{1,0:T(1,128)} %limiter.3) | copy-start | bytes 388
  32.1 12.5 %copy-start = (f32[1,384,384]{2,1,0:T(8,128)S(1)}, f32[1,384,384]{2,1,0:T(8,128)}, u32[]{:S(2)}) copy-start(f32[1,384,384]{2,1,0:T(8,128)} %plus.1) | copy-start | bytes 1769476
  32.1 12.5 %copy-start.1 = (f32[1,384,384]{2,1,0:T(8,128)S(1)}, f32[1,384,384]{2,1,0:T(8,128)}, u32[]{:S(2)}) copy-start(f32[1,384,384]{2,1,0:T(8,128)} %minus.1) | copy-start | bytes 1769476
  41.3 10.2 %all-to-all-start = ((f32[8,16,128]{2,1,0:T(8,128)}), f32[8,16,128]{2,1,0:T(8,128)S(1)}, u32[]{:S(2)}, u32[]{:S(2)}) async-start(f32[8,16,128]{2,1,0:T(8,128)} %collide_far.1), calls=%async_computation | async-start | bytes 131072 | tf_op jit(solution)/shard_map/all_to_all | solution.py:455

commit v8 on v7

--- a/solution.py
+++ b/solution.py
@@ -83,8 +83,9 @@
         copy.wait()
 
 
-def fetch_all_kernel(tensors, near, token, sem):
-    copy = pltpu.make_async_copy(tensors.at[:, pl.ds(0, near.shape[1])], near, sem)
+def fetch_all_kernel(*refs, first):
+    tensors, near, token, sem = refs[-4:]
+    copy = pltpu.make_async_copy(tensors.at[:, pl.ds(first, near.shape[1])], near, sem)
     copy.start()
     token[...] = jnp.zeros_like(token)
     copy.wait()
@@ -116,9 +117,16 @@
     )(*operands, tensors)
 
 
-def fetch_all(tensors, count):
+def fetch_all(after, tensors, first, count):
+    operands = [] if after is None else [close(after)]
     return fetch(
-        fetch_all_kernel, [], [], tensors, tensors.shape[0], count, pltpu.SemaphoreType.DMA
+        functools.partial(fetch_all_kernel, first=first),
+        operands,
+        [pl.BlockSpec(memory_space=pltpu.VMEM)] * len(operands),
+        tensors,
+        tensors.shape[0],
+        count,
+        pltpu.SemaphoreType.DMA,
     )
 
 
@@ -160,11 +168,11 @@
     tiles = len(others) * modes // width
     spans = everyone // width
 
-    def unit_of(pair, unit):
-        at = 2 * pair + unit
+    def unit_of(group, bank, unit):
         if spans == 1:
-            return at, 0
-        return at // spans, at % spans
+            return 4 * group + 2 * bank + unit, 0
+        at = 2 * group + unit
+        return at // spans * 2 + bank, at % spans
 
     def columns_of(span):
         return slice(0, width) if spans == 1 else pl.ds(pl.multiple_of(span * width, width), width)
@@ -173,59 +181,65 @@
         for piece in (2 * tile, 2 * tile + 1):
             yield piece * LANES // modes, slice(piece * LANES % modes, piece * LANES % modes + LANES)
 
-    def push(pair, tile, register):
+    def push(group, tile, register):
         for unit in range(2):
-            _, span = unit_of(pair, unit)
+            _, span = unit_of(group, 0, unit)
             of = width // cells
             rows = slice(0, of) if spans == 1 else pl.ds(span * of, of)
             tall = [others[p][rows, :, lanes].reshape(width, LANES) for p, lanes in pieces_of(tile)]
             pltpu.matmul_push_rhs(jnp.concatenate(tall, axis=1), register, unit, transpose=True)
 
     def run(*sums):
-        def drain(part, pair, bank):
+        def drain(part, group, bank):
             for unit in range(2):
-                k, span = unit_of(pair, unit)
+                k, span = unit_of(group, bank, unit)
                 columns = columns_of(span)
                 inner = pltpu.matmul_pop(sums[2 * unit + bank])
                 row = jnp.sum(inner * own[:, columns], axis=0, keepdims=True)
                 place = pl.ds(sum(count for _, count, _ in parts[:part]) + k, 1)
                 total[place, columns] = row + add[place, columns] if add is not None else row
 
-        def work(part, pair, bank, start, follower, pending):
+        def work(part, group, start, follower, pending):
             for tile in range(tiles):
                 register = (start + tile) % 2
                 if tile + 1 < tiles:
-                    push(pair, tile + 1, 1 - register)
+                    push(group, tile + 1, 1 - register)
                 elif follower is not None:
                     push(follower, 0, 1 - register)
-                for unit in range(2):
-                    k, _ = unit_of(pair, unit)
-                    wide = [parts[part][0](p, k, lanes) for p, lanes in pieces_of(tile)]
-                    pltpu.matmul_acc_lhs(
-                        sums[2 * unit + bank], jnp.concatenate(wide, axis=1), register
-                    )
-                if tile == 0 and pending is not None:
-                    drain(*pending)
+                for bank in range(2):
+                    for unit in range(2):
+                        k, _ = unit_of(group, bank, unit)
+                        wide = [parts[part][0](p, k, lanes) for p, lanes in pieces_of(tile)]
+                        pltpu.matmul_acc_lhs(
+                            sums[2 * unit + bank],
+                            jnp.concatenate(wide, axis=1),
+                            register if bank == 0 else None,
+                        )
+                    if bank == 0 and tile == 0 and pending is not None:
+                        drain(*pending, 1)
+            drain(part, group, 0)
             return (start + tiles) % 2
 
         pending, at = None, 0
         push(0, 0, at)
         for part in range(len(parts)):
             last = part + 1 == len(parts)
-            pairs = parts[part][1] * spans // 2
+            groups_here = parts[part][1] * spans // 4
             parts[part][2]()
-            at = work(part, 0, 0, at, 1, pending)
+            at = work(part, 0, at, 1, pending)
             odd = at
 
-            @pl.loop(0, (pairs - 2) // 2)
-            def _(step):
-                now = work(part, 2 * step + 1, 1, odd, 2 * step + 2, (part, 2 * step, 0))
-                work(part, 2 * step + 2, 0, now, 2 * step + 3, (part, 2 * step + 1, 1))
+            if groups_here > 2:
+
+                @pl.loop(0, (groups_here - 2) // 2)
+                def _(step):
+                    now = work(part, 2 * step + 1, odd, 2 * step + 2, (part, 2 * step))
+                    work(part, 2 * step + 2, now, 2 * step + 3, (part, 2 * step + 1))
 
             follower = None if last else 0
-            at = work(part, pairs - 1, 1, odd, follower, (part, pairs - 2, 0))
-            pending = (part, pairs - 1, 1)
-        drain(*pending)
+            at = work(part, groups_here - 1, odd, follower, (part, groups_here - 2))
+            pending = (part, groups_here - 1)
+        drain(*pending, 1)
 
     pl.run_scoped(run, *[pltpu.ACC(unit)((modes, width), jnp.float32) for unit in (0, 0, 1, 1)])
 
@@ -238,24 +252,28 @@
 
 
 def near_kernel(
-    table, mine, mate, tensors, shared, two, three, total, own, far, beside, far_sems, sems
+    table, mine, mate, tensors, one, two, three, total, own, far, beside, far_sems, sems
 ):
-    first = shared.shape[1]
-    last = copies_of(table, tensors, (0, 1), tensors.shape[1] - first, beside, sems)
-    later = copies_of(table, tensors, (2, 3), first, far, far_sems)
-    start_all(last + later)
+    ahead = one.shape[1] + two.shape[1]
+    last = copies_of(table, tensors, (0, 1), ahead + three.shape[1], beside, sems)
+    later = copies_of(table, tensors, (2, 3), ahead, far, far_sems)
+    start_all(last)
     own[...] = mine[...].reshape(own.shape[::-1]).astype(jnp.float32).T
     picks = [tensor_of(table, partner) for partner in (0, 1)]
-    parts = [part_of(shared, picks), part_of(two), part_of(three)]
-    parts.append(part_of(beside, before=lambda: wait_all(last)))
+    parts = [
+        part_of(one, picks),
+        part_of(two, picks),
+        part_of(three, before=lambda: start_all(later)),
+        part_of(beside, before=lambda: wait_all(last)),
+    ]
     contract(parts, (mine, mate), own, total, None)
     wait_all(later)
 
 
-def collide_near(table, mine, mate, tensors, shared, two, three):
+def collide_near(table, mine, mate, tensors, one, two, three):
     groups, cells, modes = mine.shape
     out_modes = tensors.shape[1]
-    ahead = out_modes // 2
+    count = three.shape[1]
     vmem = pl.BlockSpec(memory_space=pltpu.VMEM)
     anywhere = pl.BlockSpec(memory_space=pl.ANY)
     return pl.pallas_call(
@@ -263,30 +281,30 @@
         in_specs=[pl.BlockSpec(memory_space=pltpu.SMEM), vmem, vmem, anywhere] + [vmem] * 3,
         out_specs=(vmem, vmem, vmem),
         scratch_shapes=[
-            pltpu.VMEM((2, shared.shape[1]) + tensors.shape[2:], tensors.dtype),
+            pltpu.VMEM((2, count) + tensors.shape[2:], tensors.dtype),
             pltpu.SemaphoreType.DMA((2,)),
             pltpu.SemaphoreType.DMA((2,)),
         ],
         out_shape=(
             pltpu.VMEM((out_modes, groups * cells), jnp.float32),
             pltpu.VMEM((modes, groups * cells), jnp.float32),
-            pltpu.VMEM((2, ahead) + tensors.shape[2:], tensors.dtype),
+            pltpu.VMEM((2, count) + tensors.shape[2:], tensors.dtype),
         ),
-        compiler_params=pltpu.CompilerParams(vmem_limit_bytes=7 * MIB),
+        compiler_params=pltpu.CompilerParams(vmem_limit_bytes=20 * MIB),
         cost_estimate=pl.CostEstimate(
             flops=tensors.size * groups * cells, transcendentals=0, bytes_accessed=tensors.size
         ),
         name="collide_near",
-    )(table, close(mine), close(mate), tensors, close(shared), close(two), close(three))
+    )(table, close(mine), close(mate), tensors, close(one), close(two), close(three))
 
 
 def far_kernel(
-    table, one, two, tensors, shared, far, first, own, limiter, out, total, beside, sems
+    table, one, two, tensors, early, next_, far, first, own, limiter, out, total, beside, sems
 ):
     last = copies_of(table, tensors, (2, 3), tensors.shape[1] - beside.shape[1], beside, sems)
     start_all(last)
     picks = [tensor_of(table, partner) for partner in (2, 3)]
-    parts = [part_of(shared, picks), part_of(far)]
+    parts = [part_of(early, picks), part_of(next_, picks), part_of(far)]
     parts.append(part_of(beside, before=lambda: wait_all(last)))
     contract(parts, (one, two), own, total, first)
     groups, cells, _ = one.shape
@@ -303,16 +321,16 @@
         out[here ^ reverse(d, groups)] = jnp.concatenate(parts + [spare], axis=1)
 
 
-def collide_far(table, one, two, tensors, shared, far, first, own, limiter):
+def collide_far(table, one, two, tensors, early, next_, far, first, own, limiter):
     groups, cells, modes = one.shape
     out_modes = tensors.shape[1]
     rows = cells // fold_of(cells, out_modes)
-    left = out_modes - shared.shape[1] - far.shape[1]
+    left = out_modes - early.shape[1] - next_.shape[1] - far.shape[1]
     vmem = pl.BlockSpec(memory_space=pltpu.VMEM)
     anywhere = pl.BlockSpec(memory_space=pl.ANY)
     return pl.pallas_call(
         far_kernel,
-        in_specs=[pl.BlockSpec(memory_space=pltpu.SMEM), vmem, vmem, anywhere] + [vmem] * 5,
+        in_specs=[pl.BlockSpec(memory_space=pltpu.SMEM), vmem, vmem, anywhere] + [vmem] * 6,
         out_specs=vmem,
         scratch_shapes=[
             pltpu.VMEM((out_modes, groups * cells), jnp.float32),
@@ -320,7 +338,7 @@
             pltpu.SemaphoreType.DMA((2,)),
         ],
         out_shape=pltpu.VMEM((groups, rows, LANES), jnp.float32),
-        compiler_params=pltpu.CompilerParams(vmem_limit_bytes=11 * MIB),
+        compiler_params=pltpu.CompilerParams(vmem_limit_bytes=20 * MIB),
         cost_estimate=pl.CostEstimate(
             flops=tensors.size * groups * cells, transcendentals=0, bytes_accessed=tensors.size
         ),
@@ -330,7 +348,8 @@
         close(one),
         close(two),
         tensors,
-        close(shared),
+        close(early),
+        close(next_),
         close(far),
         close(first),
         close(own),
@@ -431,9 +450,10 @@
     mine, held, token = fields, [], None
 
     def more():
-        if not held:
-            return fetch_all(tensors, count)
-        return fetch_near(pair_table, mine, tensors, (2 * len(held) - 1) * count, 2 * count)
+        first = len(held) * count
+        if len(held) < 2:
+            return fetch_all(mine if held else None, tensors, first, count)
+        return fetch_near(pair_table, mine, tensors, first, 2 * count)
 
     bit = groups // 2
     while bit > 0:
@@ -450,7 +470,7 @@
     far_two = exchanged(mate, "spec", 2)
     first, own, far = collide_near(pair_table, mine, mate, tensors, *held)
     block = collide_far(
-        pair_table, far_one, far_two, tensors, held[0], far, first, own, face_limiter
+        pair_table, far_one, far_two, tensors, held[0], held[1], far, first, own, face_limiter
     )
     received = lax.all_to_all(block, "cell", split_axis=0, concat_axis=0, tiled=False)
     flux = transport(mine, face_limiter, plus_flux, minus_flux)

time: 52.5 us -> 55.5 us (1.057)
  Pallas kernels: 31.5 us -> 34.7 us
    pallas_call x1, Pallas kernels: 8.33 us -> 11.2 us  [collide_near(): pl.pallas_call(near_kernel, in_specs=[pl.BlockSpec(memory_space=pltpu.SME...]
    pallas_call x1, Pallas kernels: 9.13 us -> 10.2 us  [collide_far(): pl.pallas_call(far_kernel, in_specs=[pl.BlockSpec(memory_space=pltpu.SMEM...]
    pallas_call x3, Pallas kernels: 12.4 us -> 11.8 us  [fetch(): pl.pallas_call(kernel, in_specs=specs + [pl.BlockSpec(memory_space=pl.ANY...]
  transfers between devices with their start and end apart: 7 -> 7, of which waited for: 2 -> 1; matrix products, arithmetic and copies ran while one was open for 0% -> 0% of each run, Pallas kernels for 41% -> 43%
where the time goes in v8:
time: 55.5 us; the launch traced here: 55.2 us
  Pallas kernels  34.7 us (63%)
  starting transfers between devices  13.7 us (25%)
  waiting for transfers between devices  6.05 us (11%)
  between operations  0.83 us (1%)
    pallas_call x3, Pallas kernels, fetch(): pl.pallas_call(kernel, in_specs=specs + [pl.BlockSpec(memory_space=pl.ANY...  11.8 us
    pallas_call x1, Pallas kernels, collide_near(): pl.pallas_call(near_kernel, in_specs=[pl.BlockSpec(memory_space=pltpu.SME...  11.2 us
    ppermute x6, starting transfers between devices, exchanged(): lax.ppermute(x, axis, [(i, i ^ bit) for i in range(lax.axis_size(axis))])  10.3 us
    pallas_call x1, Pallas kernels, collide_far(): pl.pallas_call(far_kernel, in_specs=[pl.BlockSpec(memory_space=pltpu.SMEM...  10.2 us
    all_to_all x1, waiting for transfers between devices, local(): lax.all_to_all(block, 'cell', split_axis=0, concat_axis=0, tiled=False)  6.03 us
    all_to_all x1, starting transfers between devices, local(): lax.all_to_all(block, 'cell', split_axis=0, concat_axis=0, tiled=False)  3.36 us
  transfers between devices with their start and end apart: 7, of which 1 were waited for; matrix products, arithmetic and copies ran while one was open for 0% of the time, Pallas kernels for 43%

profile of v8, /device:TPU:0, one launch (start us, length us, event | category | flops | bytes accessed | tf_op | source)
XLA Modules:
  0.0 55.2 jit_solution(15797250400418768479)
XLA Ops:
  0.6 4.1 %collective-permute-start = (bf16[1,32,384]{2,1,0:T(8,128)(2,1)}, bf16[1,32,384]{2,1,0:T(8,128)(2,1)S(1)}, u32[]{:S(2)}, u32[]{:S(2)}) collective-permute-start(bf16[1,32,384]{2,1,0:T(8,128)(2,1)} %fields.1), channel_id=1, source_target_pairs={{0,16},{4,20},{8,24},{12,28},{16,0},{20,4},{24,8},{28,12},{1,17},{... | collective-permute-start | bytes 73736 | tf_op jit(solution)/shard_map/ppermute | solution.py:444
  4.7 3.7 %fetch.3 = (bf16[4,8,384,384]{3,2,1,0:T(8,128)(2,1)S(1)}, f32[8,128]{1,0:T(8,128)S(1)}) custom-call(bf16[4,48,384,384]{3,2,1,0:T(8,128)(2,1)} %tensors.5), custom_call_target="tpu_custom_call" | custom-call | bytes 18874368 | tf_op jit(solution)/shard_map/fetch/pallas_call | solution.py:104
  8.5 0.0 collective-permute-done.came
  8.5 0.0 copy-start.3
  8.5 1.6 %collective-permute-start.1 = (bf16[2,32,384]{2,1,0:T(8,128)(2,1)S(1)}, bf16[2,32,384]{2,1,0:T(8,128)(2,1)S(1)}, u32[]{:S(2)}, u32[]{:S(2)}) collective-permute-start(bf16[2,32,384]{2,1,0:T(8,128)(2,1)S(1)} %join.3.refs_0_.here), channel_id=1, source_target_pairs={{0,8},{4,12},{8,0},{12,4},{16,24},{20,28},{24,16},{28,20},{1,9},{5... | collective-permute-start | bytes 147464 | tf_op jit(solution)/shard_map/ppermute | solution.py:444
  10.1 3.7 %fetch.4 = (bf16[4,8,384,384]{3,2,1,0:T(8,128)(2,1)S(1)}, f32[8,128]{1,0:T(8,128)S(1)}) custom-call(bf16[2,32,384]{2,1,0:T(8,128)(2,1)S(1)} %join.3.refs_0_.here, bf16[4,48,384,384]{3,2,1,0:T(8,128)(2,1)} %tensors.5), custom_call_target="tpu_custom_call" | custom-call | bytes 18874368 | tf_op jit(solution)/shard_map/fetch/pallas_call | solution.py:104
  13.8 0.0 collective-permute-done.1.came
  13.9 1.6 %collective-permute-start.2 = (bf16[4,32,384]{2,1,0:T(8,128)(2,1)S(1)}, bf16[4,32,384]{2,1,0:T(8,128)(2,1)S(1)}, u32[]{:S(2)}, u32[]{:S(2)}) collective-permute-start(bf16[4,32,384]{2,1,0:T(8,128)(2,1)S(1)} %join.4.after.here), channel_id=1, source_target_pairs={{0,4},{4,0},{8,12},{12,8},{16,20},{20,16},{24,28},{28,24},{1,5},{5... | collective-permute-start | bytes 294920 | tf_op jit(solution)/shard_map/ppermute | solution.py:444
  15.4 4.4 %fetch.5 = (bf16[2,16,384,384]{3,2,1,0:T(8,128)(2,1)S(1)}, f32[8,128]{1,0:T(8,128)S(1)}) custom-call(s32[4,4]{1,0:T(4,128)S(1)} %copy-done.3, bf16[4,32,384]{2,1,0:T(8,128)(2,1)S(1)} %join.4.after.here, bf16[4,48,384,384]{3,2,1,0:T(8,128)(2,1)} %tensors.5), custom_call_target="tpu_custom_call" | custom-call | bytes 18874368 | tf_op jit(solution)/shard_map/fetch/pallas_call | solution.py:104
  19.8 0.0 collective-permute-done.2.came
  19.8 0.1 collective-permute-start.4
  19.9 1.6 %collective-permute-start.3 = (bf16[8,32,384]{2,1,0:T(8,128)(2,1)S(1)}, bf16[8,32,384]{2,1,0:T(8,128)(2,1)S(1)}, u32[]{:S(2)}, u32[]{:S(2)}) collective-permute-start(bf16[8,32,384]{2,1,0:T(8,128)(2,1)S(1)} %join.5.mine), channel_id=1, source_target_pairs={{0,2},{1,3},{2,0},{3,1},{4,6},{5,7},{6,4},{7,5},{8,10},{9,11},{10,... | collective-permute-start | bytes 589832 | tf_op jit(solution)/shard_map/ppermute | solution.py:444
  21.5 0.0 collective-permute-done.4.mate
  21.5 1.4 %collective-permute-start.5 = (bf16[8,32,384]{2,1,0:T(8,128)(2,1)S(1)}, bf16[8,32,384]{2,1,0:T(8,128)(2,1)S(1)}, u32[]{:S(2)}, u32[]{:S(2)}) collective-permute-start(bf16[8,32,384]{2,1,0:T(8,128)(2,1)S(1)} %collective-permute-done.4.mate), channel_id=1, source_target_pairs={{0,2},{1,3},{2,0},{3,1},{4,6},{5,7},{6,4},{7,5},{8,10},{9,11},{10,... | collective-permute-start | bytes 589832 | tf_op jit(solution)/shard_map/ppermute | solution.py:444
  22.9 11.2 %collide_near.1 = (f32[48,256]{1,0:T(8,128)S(1)}, f32[384,256]{1,0:T(8,128)S(1)}, bf16[2,16,384,384]{3,2,1,0:T(8,128)(2,1)S(1)}) custom-call(s32[4,4]{1,0:T(4,128)} %table.5, bf16[8,32,384]{2,1,0:T(8,128)(2,1)S(1)} %join.5.mine, bf16[8,32,384]{2,1,0:T(8,128)(2,1)S(1)} %collective-permute-done.4.mate, bf16[4,48,384,384]{3,2,1,0:T(8,128)(2,1)} %tensors.5, ...), custom_call_target="tpu_custom_call" | custom-call | flops 7247757312 | bytes 28311552 | tf_op jit(solution)/shard_map/collide_near/pallas_call | solution.py:279
  34.1 0.0 collective-permute-done.3.one
  34.1 0.0 collective-permute-done.5.two
  34.1 0.0 copy-start
  34.1 0.0 copy-start.1
  34.1 10.2 %collide_far.1 = f32[8,16,128]{2,1,0:T(8,128)} custom-call(s32[4,4]{1,0:T(4,128)S(1)} %copy-done.4, bf16[8,32,384]{2,1,0:T(8,128)(2,1)S(1)} %collective-permute-done.3.one, bf16[8,32,384]{2,1,0:T(8,128)(2,1)S(1)} %collective-permute-done.5.two, bf16[4,48,384,384]{3,2,1,0:T(8,128)(2,1)} %tensors.5, bf16[4,8,384,384]{3,2,1,0:T(8,128)(2,1)S(1)} %get-tuple-element.14.one.early, ...), custom_call_target="tpu_custom_call" | custom-call | flops 7247757312 | bytes 28311552 | tf_op jit(solution)/shard_map/collide_far/pallas_call | solution.py:331
  44.3 3.4 %all-to-all-start = ((f32[8,16,128]{2,1,0:T(8,128)}), f32[8,16,128]{2,1,0:T(8,128)S(1)}, u32[]{:S(2)}, u32[]{:S(2)}) async-start(f32[8,16,128]{2,1,0:T(8,128)} %collide_far.1), calls=%async_computation | async-start | bytes 131072 | tf_op jit(solution)/shard_map/all_to_all | solution.py:475
  47.7 0.8 %transport.1.flux = f32[40,384]{1,0:T(8,128)S(1)} custom-call(bf16[8,32,384]{2,1,0:T(8,128)(2,1)S(1)} %join.5.mine, s32[1,32]{1,0:T(1,128)S(1)} %copy-done.5, f32[1,384,384]{2,1,0:T(8,128)S(1)} %copy-done, f32[1,384,384]{2,1,0:T(8,128)S(1)} %copy-done.1), custom_call_target="tpu_custom_call" | custom-call | tf_op jit(solution)/shard_map/transport/pallas_call | solution.py:401
  48.5 6.0 %all-to-all-done.received = f32[8,16,128]{2,1,0:T(8,128)S(1)} async-done(((f32[8,16,128]{2,1,0:T(8,128)}), f32[8,16,128]{2,1,0:T(8,128)S(1)}, u32[]{:S(2)}, u32[]{:S(2)}) %all-to-all-start) | async-done | bytes 65568 | tf_op jit(solution)/shard_map/all_to_all | solution.py:475
  54.5 0.7 %finish.1 = (f32[1,32,384]{2,1,0:T(8,128)}, f32[1,32,384]{2,1,0:T(8,128)}) custom-call(f32[8,16,128]{2,1,0:T(8,128)S(1)} %all-to-all-done.received, f32[40,384]{1,0:T(8,128)S(1)} %transport.1.flux, bf16[1,32,384]{2,1,0:T(8,128)(2,1)S(1)} %copy-done.2), custom_call_target="tpu_custom_call" | custom-call | tf_op jit(solution)/shard_map/finish/pallas_call | solution.py:433
  (12 shorter events, 0.1 us)
Async XLA Ops:
  0.6 7.8 %copy-start.2 = (bf16[1,32,384]{2,1,0:T(8,128)(2,1)S(1)}, bf16[1,32,384]{2,1,0:T(8,128)(2,1)}, u32[]{:S(2)}) copy-start(bf16[1,32,384]{2,1,0:T(8,128)(2,1)} %fields.1) | copy-start | bytes 73732
  0.6 7.8 %collective-permute-start = (bf16[1,32,384]{2,1,0:T(8,128)(2,1)}, bf16[1,32,384]{2,1,0:T(8,128)(2,1)S(1)}, u32[]{:S(2)}, u32[]{:S(2)}) collective-permute-start(bf16[1,32,384]{2,1,0:T(8,128)(2,1)} %fields.1), channel_id=1, source_target_pairs={{0,16},{4,20},{8,24},{12,28},{16,0},{20,4},{24,8},{28,12},{1,17},{... | collective-permute-start | bytes 73736 | tf_op jit(solution)/shard_map/ppermute | solution.py:444
  8.5 6.9 %copy-start.3 = (s32[4,4]{1,0:T(4,128)S(1)}, s32[4,4]{1,0:T(4,128)}, u32[]{:S(2)}) copy-start(s32[4,4]{1,0:T(4,128)} %table.5) | copy-start | bytes 196
  8.5 5.3 %collective-permute-start.1 = (bf16[2,32,384]{2,1,0:T(8,128)(2,1)S(1)}, bf16[2,32,384]{2,1,0:T(8,128)(2,1)S(1)}, u32[]{:S(2)}, u32[]{:S(2)}) collective-permute-start(bf16[2,32,384]{2,1,0:T(8,128)(2,1)S(1)} %join.3.refs_0_.here), channel_id=1, source_target_pairs={{0,8},{4,12},{8,0},{12,4},{16,24},{20,28},{24,16},{28,20},{1,9},{5... | collective-permute-start | bytes 147464 | tf_op jit(solution)/shard_map/ppermute | solution.py:444
  13.9 5.9 %collective-permute-start.2 = (bf16[4,32,384]{2,1,0:T(8,128)(2,1)S(1)}, bf16[4,32,384]{2,1,0:T(8,128)(2,1)S(1)}, u32[]{:S(2)}, u32[]{:S(2)}) collective-permute-start(bf16[4,32,384]{2,1,0:T(8,128)(2,1)S(1)} %join.4.after.here), channel_id=1, source_target_pairs={{0,4},{4,0},{8,12},{12,8},{16,20},{20,16},{24,28},{28,24},{1,5},{5... | collective-permute-start | bytes 294920 | tf_op jit(solution)/shard_map/ppermute | solution.py:444
  19.8 1.7 %collective-permute-start.4 = (bf16[8,32,384]{2,1,0:T(8,128)(2,1)S(1)}, bf16[8,32,384]{2,1,0:T(8,128)(2,1)S(1)}, u32[]{:S(2)}, u32[]{:S(2)}) collective-permute-start(bf16[8,32,384]{2,1,0:T(8,128)(2,1)S(1)} %join.5.mine), channel_id=1, source_target_pairs={{0,1},{1,0},{2,3},{3,2},{4,5},{5,4},{6,7},{7,6},{8,9},{9,8},{10,11... | collective-permute-start | bytes 589832 | tf_op jit(solution)/shard_map/ppermute | solution.py:444
  19.9 14.1 %collective-permute-start.3 = (bf16[8,32,384]{2,1,0:T(8,128)(2,1)S(1)}, bf16[8,32,384]{2,1,0:T(8,128)(2,1)S(1)}, u32[]{:S(2)}, u32[]{:S(2)}) collective-permute-start(bf16[8,32,384]{2,1,0:T(8,128)(2,1)S(1)} %join.5.mine), channel_id=1, source_target_pairs={{0,2},{1,3},{2,0},{3,1},{4,6},{5,7},{6,4},{7,5},{8,10},{9,11},{10,... | collective-permute-start | bytes 589832 | tf_op jit(solution)/shard_map/ppermute | solution.py:444
  21.5 12.6 %collective-permute-start.5 = (bf16[8,32,384]{2,1,0:T(8,128)(2,1)S(1)}, bf16[8,32,384]{2,1,0:T(8,128)(2,1)S(1)}, u32[]{:S(2)}, u32[]{:S(2)}) collective-permute-start(bf16[8,32,384]{2,1,0:T(8,128)(2,1)S(1)} %collective-permute-done.4.mate), channel_id=1, source_target_pairs={{0,2},{1,3},{2,0},{3,1},{4,6},{5,7},{6,4},{7,5},{8,10},{9,11},{10,... | collective-permute-start | bytes 589832 | tf_op jit(solution)/shard_map/ppermute | solution.py:444
  22.9 11.2 %copy-start.4 = (s32[4,4]{1,0:T(4,128)S(1)}, s32[4,4]{1,0:T(4,128)}, u32[]{:S(2)}) copy-start(s32[4,4]{1,0:T(4,128)} %table.5) | copy-start | bytes 196
  22.9 11.2 %copy-start.5 = (s32[1,32]{1,0:T(1,128)S(1)}, s32[1,32]{1,0:T(1,128)}, u32[]{:S(2)}) copy-start(s32[1,32]{1,0:T(1,128)} %limiter.3) | copy-start | bytes 388
  34.1 13.6 %copy-start = (f32[1,384,384]{2,1,0:T(8,128)S(1)}, f32[1,384,384]{2,1,0:T(8,128)}, u32[]{:S(2)}) copy-start(f32[1,384,384]{2,1,0:T(8,128)} %plus.1) | copy-start | bytes 1769476
  34.1 13.6 %copy-start.1 = (f32[1,384,384]{2,1,0:T(8,128)S(1)}, f32[1,384,384]{2,1,0:T(8,128)}, u32[]{:S(2)}) copy-start(f32[1,384,384]{2,1,0:T(8,128)} %minus.1) | copy-start | bytes 1769476
  44.3 10.2 %all-to-all-start = ((f32[8,16,128]{2,1,0:T(8,128)}), f32[8,16,128]{2,1,0:T(8,128)S(1)}, u32[]{:S(2)}, u32[]{:S(2)}) async-start(f32[8,16,128]{2,1,0:T(8,128)} %collide_far.1), calls=%async_computation | async-start | bytes 131072 | tf_op jit(solution)/shard_map/all_to_all | solution.py:475

commit v9 on v7

--- a/solution.py
+++ b/solution.py
@@ -10,6 +10,9 @@
 LANES = 128
 MIB = 1 << 20
 SIXTHS = 6
+NEAR = 7 * MIB
+NEXT = 7 * MIB
+FAR = 11 * MIB
 
 
 def minmod_two(first, second):
@@ -153,7 +156,7 @@
     )(close(here), close(came), close(token))
 
 
-def contract(parts, others, own, total, add):
+def contract(parts, others, own, total):
     groups, cells, modes = others[0].shape
     everyone = groups * cells
     width = 2 * LANES
@@ -188,8 +191,11 @@
                 columns = columns_of(span)
                 inner = pltpu.matmul_pop(sums[2 * unit + bank])
                 row = jnp.sum(inner * own[:, columns], axis=0, keepdims=True)
-                place = pl.ds(sum(count for _, count, _ in parts[:part]) + k, 1)
-                total[place, columns] = row + add[place, columns] if add is not None else row
+                place = pl.ds(sum(count for _, count, _, _, _ in parts[:part]) + k, 1)
+                add, shift = parts[part][3:]
+                if add is not None:
+                    row = row + add[pl.ds(shift + k, 1), columns]
+                total[place, columns] = row
 
         def work(part, pair, bank, start, follower, pending):
             for tile in range(tiles):
@@ -230,65 +236,116 @@
     pl.run_scoped(run, *[pltpu.ACC(unit)((modes, width), jnp.float32) for unit in (0, 0, 1, 1)])
 
 
-def part_of(ref, picks=None, shift=0, count=None, before=lambda: None):
+def hold_kernel(x, after, out):
+    out[...] = x[...]
+
+
+def hold(x, after):
+    vmem = pl.BlockSpec(memory_space=pltpu.VMEM)
+    return pl.pallas_call(
+        hold_kernel,
+        in_specs=[vmem, vmem],
+        out_specs=vmem,
+        out_shape=pltpu.VMEM(x.shape, x.dtype),
+        compiler_params=pltpu.CompilerParams(vmem_limit_bytes=MIB),
+        name="hold",
+    )(close(x), close(after))
+
+
+def part_of(ref, picks=None, before=lambda: None, add=None, shift=0):
     def read(p, k, lanes):
-        return ref[p if picks is None else picks[p], shift + k, :, lanes]
-
-    return read, ref.shape[1] if count is None else count, before
-
-
-def near_kernel(
-    table, mine, mate, tensors, shared, two, three, total, own, far, beside, far_sems, sems
-):
-    first = shared.shape[1]
-    last = copies_of(table, tensors, (0, 1), tensors.shape[1] - first, beside, sems)
-    later = copies_of(table, tensors, (2, 3), first, far, far_sems)
-    start_all(last + later)
+        return ref[p if picks is None else picks[p], k, :, lanes]
+
+    return read, ref.shape[1], before, add, shift
+
+
+def near_kernel(table, mine, mate, tensors, shared, two, total, own, far, sems):
+    later = copies_of(table, tensors, (2, 3), shared.shape[1], far, sems)
+    start_all(later)
     own[...] = mine[...].reshape(own.shape[::-1]).astype(jnp.float32).T
     picks = [tensor_of(table, partner) for partner in (0, 1)]
-    parts = [part_of(shared, picks), part_of(two), part_of(three)]
-    parts.append(part_of(beside, before=lambda: wait_all(last)))
-    contract(parts, (mine, mate), own, total, None)
+    contract([part_of(shared, picks), part_of(two)], (mine, mate), own, total)
     wait_all(later)
 
 
-def collide_near(table, mine, mate, tensors, shared, two, three):
+def collide_near(table, mine, mate, tensors, shared, two):
     groups, cells, modes = mine.shape
-    out_modes = tensors.shape[1]
-    ahead = out_modes // 2
     vmem = pl.BlockSpec(memory_space=pltpu.VMEM)
     anywhere = pl.BlockSpec(memory_space=pl.ANY)
+    count = shared.shape[1] + two.shape[1]
     return pl.pallas_call(
         near_kernel,
-        in_specs=[pl.BlockSpec(memory_space=pltpu.SMEM), vmem, vmem, anywhere] + [vmem] * 3,
+        in_specs=[pl.BlockSpec(memory_space=pltpu.SMEM), vmem, vmem, anywhere, vmem, vmem],
         out_specs=(vmem, vmem, vmem),
+        scratch_shapes=[pltpu.SemaphoreType.DMA((2,))],
+        out_shape=(
+            pltpu.VMEM((count, groups * cells), jnp.float32),
+            pltpu.VMEM((modes, groups * cells), jnp.float32),
+            pltpu.VMEM(two.shape, tensors.dtype),
+        ),
+        compiler_params=pltpu.CompilerParams(vmem_limit_bytes=NEAR),
+        cost_estimate=pl.CostEstimate(
+            flops=tensors.size // 2 * groups * cells,
+            transcendentals=0,
+            bytes_accessed=tensors.size // 2,
+        ),
+        name="collide_near",
+    )(table, close(mine), close(mate), tensors, close(shared), close(two))
+
+
+def next_kernel(
+    table, after, mine, mate, tensors, three, own, total, far, beside, far_sems, sems
+):
+    count = beside.shape[1]
+    last = copies_of(table, tensors, (0, 1), tensors.shape[1] - count, beside, sems)
+    later = copies_of(table, tensors, (2, 3), tensors.shape[1] // 2, far, far_sems)
+    start_all(last + later)
+    parts = [part_of(three), part_of(beside, before=lambda: wait_all(last))]
+    contract(parts, (mine, mate), own, total)
+    wait_all(later)
+
+
+def collide_next(table, after, mine, mate, tensors, three, own):
+    groups, cells, modes = mine.shape
+    vmem = pl.BlockSpec(memory_space=pltpu.VMEM)
+    anywhere = pl.BlockSpec(memory_space=pl.ANY)
+    count = tensors.shape[1] // 2
+    few = (2, count - three.shape[1]) + tensors.shape[2:]
+    return pl.pallas_call(
+        next_kernel,
+        in_specs=[pl.BlockSpec(memory_space=pltpu.SMEM)] + [vmem] * 3 + [anywhere, vmem, vmem],
+        out_specs=(vmem, vmem),
         scratch_shapes=[
-            pltpu.VMEM((2, shared.shape[1]) + tensors.shape[2:], tensors.dtype),
+            pltpu.VMEM(few, tensors.dtype),
             pltpu.SemaphoreType.DMA((2,)),
             pltpu.SemaphoreType.DMA((2,)),
         ],
         out_shape=(
-            pltpu.VMEM((out_modes, groups * cells), jnp.float32),
-            pltpu.VMEM((modes, groups * cells), jnp.float32),
-            pltpu.VMEM((2, ahead) + tensors.shape[2:], tensors.dtype),
+            pltpu.VMEM((count, groups * cells), jnp.float32),
+            pltpu.VMEM(few, tensors.dtype),
         ),
-        compiler_params=pltpu.CompilerParams(vmem_limit_bytes=7 * MIB),
+        compiler_params=pltpu.CompilerParams(vmem_limit_bytes=NEXT),
         cost_estimate=pl.CostEstimate(
-            flops=tensors.size * groups * cells, transcendentals=0, bytes_accessed=tensors.size
+            flops=tensors.size // 2 * groups * cells,
+            transcendentals=0,
+            bytes_accessed=tensors.size // 2,
         ),
-        name="collide_near",
-    )(table, close(mine), close(mate), tensors, close(shared), close(two), close(three))
-
-
-def far_kernel(
-    table, one, two, tensors, shared, far, first, own, limiter, out, total, beside, sems
-):
+        name="collide_next",
+    )(table, close(after), close(mine), close(mate), tensors, close(three), close(own))
+
+
+def far_kernel(table, one, two, tensors, *refs):
+    shared, far, more, first, second, own, limiter, out, total, beside, sems = refs
     last = copies_of(table, tensors, (2, 3), tensors.shape[1] - beside.shape[1], beside, sems)
     start_all(last)
     picks = [tensor_of(table, partner) for partner in (2, 3)]
-    parts = [part_of(shared, picks), part_of(far)]
-    parts.append(part_of(beside, before=lambda: wait_all(last)))
-    contract(parts, (one, two), own, total, first)
+    parts = [
+        part_of(shared, picks, add=first),
+        part_of(far, add=first, shift=shared.shape[1]),
+        part_of(more, add=second),
+        part_of(beside, before=lambda: wait_all(last), add=second, shift=more.shape[1]),
+    ]
+    contract(parts, (one, two), own, total)
     groups, cells, _ = one.shape
     here = lax.axis_index("cell")
     whole = total[...].T
@@ -303,16 +360,16 @@
         out[here ^ reverse(d, groups)] = jnp.concatenate(parts + [spare], axis=1)
 
 
-def collide_far(table, one, two, tensors, shared, far, first, own, limiter):
+def collide_far(table, one, two, tensors, shared, far, more, first, second, own, limiter):
     groups, cells, modes = one.shape
     out_modes = tensors.shape[1]
     rows = cells // fold_of(cells, out_modes)
-    left = out_modes - shared.shape[1] - far.shape[1]
+    left = out_modes - shared.shape[1] - far.shape[1] - more.shape[1]
     vmem = pl.BlockSpec(memory_space=pltpu.VMEM)
     anywhere = pl.BlockSpec(memory_space=pl.ANY)
     return pl.pallas_call(
         far_kernel,
-        in_specs=[pl.BlockSpec(memory_space=pltpu.SMEM), vmem, vmem, anywhere] + [vmem] * 5,
+        in_specs=[pl.BlockSpec(memory_space=pltpu.SMEM), vmem, vmem, anywhere] + [vmem] * 7,
         out_specs=vmem,
         scratch_shapes=[
             pltpu.VMEM((out_modes, groups * cells), jnp.float32),
@@ -320,7 +377,7 @@
             pltpu.SemaphoreType.DMA((2,)),
         ],
         out_shape=pltpu.VMEM((groups, rows, LANES), jnp.float32),
-        compiler_params=pltpu.CompilerParams(vmem_limit_bytes=11 * MIB),
+        compiler_params=pltpu.CompilerParams(vmem_limit_bytes=FAR),
         cost_estimate=pl.CostEstimate(
             flops=tensors.size * groups * cells, transcendentals=0, bytes_accessed=tensors.size
         ),
@@ -332,7 +389,9 @@
         tensors,
         close(shared),
         close(far),
+        close(more),
         close(first),
+        close(second),
         close(own),
         limiter,
     )
@@ -447,10 +506,23 @@
         held.append(more()[0])
     mate = exchanged(mine, "spec", 1)
     far_one = exchanged(mine, "spec", 2)
-    far_two = exchanged(mate, "spec", 2)
-    first, own, far = collide_near(pair_table, mine, mate, tensors, *held)
+    shared, two, three = held
+    first, own, far = collide_near(pair_table, mine, mate, tensors, shared, two)
+    far_one = hold(far_one, first)
+    far_two = exchanged(far_one, "spec", 1)
+    second, more_far = collide_next(pair_table, far_one, mine, mate, tensors, three, own)
     block = collide_far(
-        pair_table, far_one, far_two, tensors, held[0], far, first, own, face_limiter
+        pair_table,
+        far_one,
+        far_two,
+        tensors,
+        shared,
+        far,
+        more_far,
+        first,
+        second,
+        own,
+        face_limiter,
     )
     received = lax.all_to_all(block, "cell", split_axis=0, concat_axis=0, tiled=False)
     flux = transport(mine, face_limiter, plus_flux, minus_flux)

time: 52.5 us -> 53.7 us (1.023)
  Pallas kernels: 31.5 us -> 33.9 us
  starting transfers between devices: 13.7 us -> 12.4 us
    pallas_call x0 -> x2, Pallas kernels: none -> 5.15 us  [the longest x1 5.14 us: collide_next(): pl.pallas_call(next_kernel, in_specs=[pl.BlockSpec(memory_space=pltpu.SME...]
    pallas_call x1, Pallas kernels: 8.33 us -> 5.53 us  [collide_near(): pl.pallas_call(near_kernel, in_specs=[pl.BlockSpec(memory_space=pltpu.SME...]
    ppermute x6, starting transfers between devices: 10.3 us -> 9.03 us  [exchanged(): lax.ppermute(x, axis, [(i, i ^ bit) for i in range(lax.axis_size(axis))])]
  transfers between devices with their start and end apart: 7 -> 7, of which waited for: 2 -> 2; matrix products, arithmetic and copies ran while one was open for 0% -> 0% of each run, Pallas kernels for 41% -> 45%
where the time goes in v9:
time: 53.7 us; the launch traced here: 53.4 us
  Pallas kernels  33.9 us (63%)
  starting transfers between devices  12.4 us (23%)
  waiting for transfers between devices  6.27 us (12%)
  between operations  0.84 us (2%)
    pallas_call x3, Pallas kernels, fetch(): pl.pallas_call(kernel, in_specs=specs + [pl.BlockSpec(memory_space=pl.ANY...  12.4 us
    pallas_call x1, Pallas kernels, collide_far(): pl.pallas_call(far_kernel, in_specs=[pl.BlockSpec(memory_space=pltpu.SMEM...  9.21 us
    ppermute x6, starting transfers between devices, exchanged(): lax.ppermute(x, axis, [(i, i ^ bit) for i in range(lax.axis_size(axis))])  9.03 us
    all_to_all x1, waiting for transfers between devices, local(): lax.all_to_all(block, 'cell', split_axis=0, concat_axis=0, tiled=False)  6.06 us
    pallas_call x1, Pallas kernels, collide_near(): pl.pallas_call(near_kernel, in_specs=[pl.BlockSpec(memory_space=pltpu.SME...  5.53 us
    pallas_call x1, Pallas kernels, collide_next(): pl.pallas_call(next_kernel, in_specs=[pl.BlockSpec(memory_space=pltpu.SME...  5.14 us
    all_to_all x1, starting transfers between devices, local(): lax.all_to_all(block, 'cell', split_axis=0, concat_axis=0, tiled=False)  3.36 us
  transfers between devices with their start and end apart: 7, of which 2 were waited for; matrix products, arithmetic and copies ran while one was open for 0% of the time, Pallas kernels for 45%

profile of v9, /device:TPU:0, one launch (start us, length us, event | category | flops | bytes accessed | tf_op | source)
XLA Modules:
  0.0 53.4 jit_solution(5460190361073306773)
XLA Ops:
  0.6 4.1 %collective-permute-start = (bf16[1,32,384]{2,1,0:T(8,128)(2,1)}, bf16[1,32,384]{2,1,0:T(8,128)(2,1)S(1)}, u32[]{:S(2)}, u32[]{:S(2)}) collective-permute-start(bf16[1,32,384]{2,1,0:T(8,128)(2,1)} %fields.1), channel_id=1, source_target_pairs={{0,16},{4,20},{8,24},{12,28},{16,0},{20,4},{24,8},{28,12},{1,17},{... | collective-permute-start | bytes 73736 | tf_op jit(solution)/shard_map/ppermute | solution.py:484
  4.8 3.7 %fetch.3 = (bf16[4,8,384,384]{3,2,1,0:T(8,128)(2,1)S(1)}, f32[8,128]{1,0:T(8,128)S(1)}) custom-call(bf16[4,48,384,384]{3,2,1,0:T(8,128)(2,1)} %tensors.11), custom_call_target="tpu_custom_call" | custom-call | bytes 18874368 | tf_op jit(solution)/shard_map/fetch/pallas_call | solution.py:106
  8.5 0.0 collective-permute-done.came
  8.5 1.6 %collective-permute-start.1 = (bf16[2,32,384]{2,1,0:T(8,128)(2,1)S(1)}, bf16[2,32,384]{2,1,0:T(8,128)(2,1)S(1)}, u32[]{:S(2)}, u32[]{:S(2)}) collective-permute-start(bf16[2,32,384]{2,1,0:T(8,128)(2,1)S(1)} %join.3.after.here), channel_id=1, source_target_pairs={{0,8},{4,12},{8,0},{12,4},{16,24},{20,28},{24,16},{28,20},{1,9},{5... | collective-permute-start | bytes 147464 | tf_op jit(solution)/shard_map/ppermute | solution.py:484
  10.1 4.4 %fetch.4 = (bf16[2,16,384,384]{3,2,1,0:T(8,128)(2,1)S(1)}, f32[8,128]{1,0:T(8,128)S(1)}) custom-call(s32[4,4]{1,0:T(4,128)S(1)} %copy-done.3, bf16[2,32,384]{2,1,0:T(8,128)(2,1)S(1)} %join.3.after.here, bf16[4,48,384,384]{3,2,1,0:T(8,128)(2,1)} %tensors.11), custom_call_target="tpu_custom_call" | custom-call | bytes 18874368 | tf_op jit(solution)/shard_map/fetch/pallas_call | solution.py:106
  14.5 0.0 collective-permute-done.1.came
  14.6 1.6 %collective-permute-start.2 = (bf16[4,32,384]{2,1,0:T(8,128)(2,1)S(1)}, bf16[4,32,384]{2,1,0:T(8,128)(2,1)S(1)}, u32[]{:S(2)}, u32[]{:S(2)}) collective-permute-start(bf16[4,32,384]{2,1,0:T(8,128)(2,1)S(1)} %join.4.after.here), channel_id=1, source_target_pairs={{0,4},{4,0},{8,12},{12,8},{16,20},{20,16},{24,28},{28,24},{1,5},{5... | collective-permute-start | bytes 294920 | tf_op jit(solution)/shard_map/ppermute | solution.py:484
  16.1 4.4 %fetch.5 = (bf16[2,16,384,384]{3,2,1,0:T(8,128)(2,1)S(1)}, f32[8,128]{1,0:T(8,128)S(1)}) custom-call(s32[4,4]{1,0:T(4,128)S(1)} %copy-done.3, bf16[4,32,384]{2,1,0:T(8,128)(2,1)S(1)} %join.4.after.here, bf16[4,48,384,384]{3,2,1,0:T(8,128)(2,1)} %tensors.11), custom_call_target="tpu_custom_call" | custom-call | bytes 18874368 | tf_op jit(solution)/shard_map/fetch/pallas_call | solution.py:106
  20.5 0.0 collective-permute-done.2.came
  20.5 0.1 collective-permute-start.4
  20.6 1.6 %collective-permute-start.3 = (bf16[8,32,384]{2,1,0:T(8,128)(2,1)S(1)}, bf16[8,32,384]{2,1,0:T(8,128)(2,1)S(1)}, u32[]{:S(2)}, u32[]{:S(2)}) collective-permute-start(bf16[8,32,384]{2,1,0:T(8,128)(2,1)S(1)} %join.5.mine), channel_id=1, source_target_pairs={{0,2},{1,3},{2,0},{3,1},{4,6},{5,7},{6,4},{7,5},{8,10},{9,11},{10,... | collective-permute-start | bytes 589832 | tf_op jit(solution)/shard_map/ppermute | solution.py:484
  22.2 0.0 collective-permute-done.4.mate
  22.2 5.5 %collide_near.1 = (f32[24,256]{1,0:T(8,128)S(1)}, f32[384,256]{1,0:T(8,128)S(1)}, bf16[2,16,384,384]{3,2,1,0:T(8,128)(2,1)S(1)}) custom-call(s32[4,4]{1,0:T(4,128)S(1)} %copy-done.3, bf16[8,32,384]{2,1,0:T(8,128)(2,1)S(1)} %join.5.mine, bf16[8,32,384]{2,1,0:T(8,128)(2,1)S(1)} %collective-permute-done.4.mate, bf16[4,48,384,384]{3,2,1,0:T(8,128)(2,1)} %tensors.11, ...), custom_call_target="tpu_custom_call" | custom-call | flops 3623878656 | bytes 14155776 | tf_op jit(solution)/shard_map/collide_near/pallas_call | solution.py:276
  27.7 0.2 collective-permute-done.3.x
  27.9 0.1 collective-permute-start.5
  28.0 0.0 copy-start.4
  28.0 5.1 %collide_next.1 = (f32[24,256]{1,0:T(8,128)S(1)}, bf16[2,8,384,384]{3,2,1,0:T(8,128)(2,1)S(1)}) custom-call(s32[4,4]{1,0:T(4,128)S(1)} %copy-done.3, bf16[8,32,384]{2,1,0:T(8,128)(2,1)S(1)} %hold.1.after.one, bf16[8,32,384]{2,1,0:T(8,128)(2,1)S(1)} %join.5.mine, bf16[8,32,384]{2,1,0:T(8,128)(2,1)S(1)} %collective-permute-done.4.mate, ...), custom_call_target="tpu_custom_call" | custom-call | flops 3623878656 | bytes 14155776 | tf_op jit(solution)/shard_map/collide_next/pallas_call | solution.py:314
  33.2 0.0 copy-start
  33.2 0.0 copy-start.1
  33.2 9.2 %collide_far.1 = f32[8,16,128]{2,1,0:T(8,128)} custom-call(s32[4,4]{1,0:T(4,128)S(1)} %copy-done.3, bf16[8,32,384]{2,1,0:T(8,128)(2,1)S(1)} %hold.1.after.one, bf16[8,32,384]{2,1,0:T(8,128)(2,1)S(1)} %collective-permute-done.5.two, bf16[4,48,384,384]{3,2,1,0:T(8,128)(2,1)} %tensors.11, bf16[4,8,384,384]{3,2,1,0:T(8,128)(2,1)S(1)} %get-tuple-element.16.shared.refs_0_, ...), custom_call_target="tpu_custom_call" | custom-call | flops 7247757312 | bytes 28311552 | tf_op jit(solution)/shard_map/collide_far/pallas_call | solution.py:370
  42.4 3.4 %all-to-all-start = ((f32[8,16,128]{2,1,0:T(8,128)}), f32[8,16,128]{2,1,0:T(8,128)S(1)}, u32[]{:S(2)}, u32[]{:S(2)}) async-start(f32[8,16,128]{2,1,0:T(8,128)} %collide_far.1), calls=%async_computation | async-start | bytes 131072 | tf_op jit(solution)/shard_map/all_to_all | solution.py:527
  45.8 0.8 %transport.1.flux = f32[40,384]{1,0:T(8,128)S(1)} custom-call(bf16[8,32,384]{2,1,0:T(8,128)(2,1)S(1)} %join.5.mine, s32[1,32]{1,0:T(1,128)S(1)} %copy-done.4, f32[1,384,384]{2,1,0:T(8,128)S(1)} %copy-done, f32[1,384,384]{2,1,0:T(8,128)S(1)} %copy-done.1), custom_call_target="tpu_custom_call" | custom-call | tf_op jit(solution)/shard_map/transport/pallas_call | solution.py:441
  46.6 6.1 %all-to-all-done.received = f32[8,16,128]{2,1,0:T(8,128)S(1)} async-done(((f32[8,16,128]{2,1,0:T(8,128)}), f32[8,16,128]{2,1,0:T(8,128)S(1)}, u32[]{:S(2)}, u32[]{:S(2)}) %all-to-all-start) | async-done | bytes 65568 | tf_op jit(solution)/shard_map/all_to_all | solution.py:527
  52.7 0.7 %finish.1 = (f32[1,32,384]{2,1,0:T(8,128)}, f32[1,32,384]{2,1,0:T(8,128)}) custom-call(f32[8,16,128]{2,1,0:T(8,128)S(1)} %all-to-all-done.received, f32[40,384]{1,0:T(8,128)S(1)} %transport.1.flux, bf16[1,32,384]{2,1,0:T(8,128)(2,1)S(1)} %copy-done.2), custom_call_target="tpu_custom_call" | custom-call | tf_op jit(solution)/shard_map/finish/pallas_call | solution.py:473
  (12 shorter events, 0.1 us)
Async XLA Ops:
  0.6 7.8 %copy-start.2 = (bf16[1,32,384]{2,1,0:T(8,128)(2,1)S(1)}, bf16[1,32,384]{2,1,0:T(8,128)(2,1)}, u32[]{:S(2)}) copy-start(bf16[1,32,384]{2,1,0:T(8,128)(2,1)} %fields.1) | copy-start | bytes 73732
  0.6 9.5 %copy-start.3 = (s32[4,4]{1,0:T(4,128)S(1)}, s32[4,4]{1,0:T(4,128)}, u32[]{:S(2)}) copy-start(s32[4,4]{1,0:T(4,128)} %table.9) | copy-start | bytes 196
  0.6 7.8 %collective-permute-start = (bf16[1,32,384]{2,1,0:T(8,128)(2,1)}, bf16[1,32,384]{2,1,0:T(8,128)(2,1)S(1)}, u32[]{:S(2)}, u32[]{:S(2)}) collective-permute-start(bf16[1,32,384]{2,1,0:T(8,128)(2,1)} %fields.1), channel_id=1, source_target_pairs={{0,16},{4,20},{8,24},{12,28},{16,0},{20,4},{24,8},{28,12},{1,17},{... | collective-permute-start | bytes 73736 | tf_op jit(solution)/shard_map/ppermute | solution.py:484
  8.5 6.0 %collective-permute-start.1 = (bf16[2,32,384]{2,1,0:T(8,128)(2,1)S(1)}, bf16[2,32,384]{2,1,0:T(8,128)(2,1)S(1)}, u32[]{:S(2)}, u32[]{:S(2)}) collective-permute-start(bf16[2,32,384]{2,1,0:T(8,128)(2,1)S(1)} %join.3.after.here), channel_id=1, source_target_pairs={{0,8},{4,12},{8,0},{12,4},{16,24},{20,28},{24,16},{28,20},{1,9},{5... | collective-permute-start | bytes 147464 | tf_op jit(solution)/shard_map/ppermute | solution.py:484
  14.6 5.9 %collective-permute-start.2 = (bf16[4,32,384]{2,1,0:T(8,128)(2,1)S(1)}, bf16[4,32,384]{2,1,0:T(8,128)(2,1)S(1)}, u32[]{:S(2)}, u32[]{:S(2)}) collective-permute-start(bf16[4,32,384]{2,1,0:T(8,128)(2,1)S(1)} %join.4.after.here), channel_id=1, source_target_pairs={{0,4},{4,0},{8,12},{12,8},{16,20},{20,16},{24,28},{28,24},{1,5},{5... | collective-permute-start | bytes 294920 | tf_op jit(solution)/shard_map/ppermute | solution.py:484
  20.5 1.7 %collective-permute-start.4 = (bf16[8,32,384]{2,1,0:T(8,128)(2,1)S(1)}, bf16[8,32,384]{2,1,0:T(8,128)(2,1)S(1)}, u32[]{:S(2)}, u32[]{:S(2)}) collective-permute-start(bf16[8,32,384]{2,1,0:T(8,128)(2,1)S(1)} %join.5.mine), channel_id=1, source_target_pairs={{0,1},{1,0},{2,3},{3,2},{4,5},{5,4},{6,7},{7,6},{8,9},{9,8},{10,11... | collective-permute-start | bytes 589832 | tf_op jit(solution)/shard_map/ppermute | solution.py:484
  20.6 7.3 %collective-permute-start.3 = (bf16[8,32,384]{2,1,0:T(8,128)(2,1)S(1)}, bf16[8,32,384]{2,1,0:T(8,128)(2,1)S(1)}, u32[]{:S(2)}, u32[]{:S(2)}) collective-permute-start(bf16[8,32,384]{2,1,0:T(8,128)(2,1)S(1)} %join.5.mine), channel_id=1, source_target_pairs={{0,2},{1,3},{2,0},{3,1},{4,6},{5,7},{6,4},{7,5},{8,10},{9,11},{10,... | collective-permute-start | bytes 589832 | tf_op jit(solution)/shard_map/ppermute | solution.py:484
  27.9 5.2 %collective-permute-start.5 = (bf16[8,32,384]{2,1,0:T(8,128)(2,1)S(1)}, bf16[8,32,384]{2,1,0:T(8,128)(2,1)S(1)}, u32[]{:S(2)}, u32[]{:S(2)}) collective-permute-start(bf16[8,32,384]{2,1,0:T(8,128)(2,1)S(1)} %hold.1.after.one), channel_id=1, source_target_pairs={{0,1},{1,0},{2,3},{3,2},{4,5},{5,4},{6,7},{7,6},{8,9},{9,8},{10,11... | collective-permute-start | bytes 589832 | tf_op jit(solution)/shard_map/ppermute | solution.py:484
  28.0 5.2 %copy-start.4 = (s32[1,32]{1,0:T(1,128)S(1)}, s32[1,32]{1,0:T(1,128)}, u32[]{:S(2)}) copy-start(s32[1,32]{1,0:T(1,128)} %limiter.1) | copy-start | bytes 388
  33.2 12.6 %copy-start = (f32[1,384,384]{2,1,0:T(8,128)S(1)}, f32[1,384,384]{2,1,0:T(8,128)}, u32[]{:S(2)}) copy-start(f32[1,384,384]{2,1,0:T(8,128)} %plus.1) | copy-start | bytes 1769476
  33.2 12.6 %copy-start.1 = (f32[1,384,384]{2,1,0:T(8,128)S(1)}, f32[1,384,384]{2,1,0:T(8,128)}, u32[]{:S(2)}) copy-start(f32[1,384,384]{2,1,0:T(8,128)} %minus.1) | copy-start | bytes 1769476
  42.4 10.2 %all-to-all-start = ((f32[8,16,128]{2,1,0:T(8,128)}), f32[8,16,128]{2,1,0:T(8,128)S(1)}, u32[]{:S(2)}, u32[]{:S(2)}) async-start(f32[8,16,128]{2,1,0:T(8,128)} %collide_far.1), calls=%async_computation | async-start | bytes 131072 | tf_op jit(solution)/shard_map/all_to_all | solution.py:527

commit v10 on v7

--- a/solution.py
+++ b/solution.py
@@ -9,7 +9,7 @@
 
 LANES = 128
 MIB = 1 << 20
-SIXTHS = 6
+TWELFTHS = 12
 
 
 def minmod_two(first, second):
@@ -241,7 +241,7 @@
     table, mine, mate, tensors, shared, two, three, total, own, far, beside, far_sems, sems
 ):
     first = shared.shape[1]
-    last = copies_of(table, tensors, (0, 1), tensors.shape[1] - first, beside, sems)
+    last = copies_of(table, tensors, (0, 1), tensors.shape[1] - beside.shape[1], beside, sems)
     later = copies_of(table, tensors, (2, 3), first, far, far_sems)
     start_all(last + later)
     own[...] = mine[...].reshape(own.shape[::-1]).astype(jnp.float32).T
@@ -255,7 +255,8 @@
 def collide_near(table, mine, mate, tensors, shared, two, three):
     groups, cells, modes = mine.shape
     out_modes = tensors.shape[1]
-    ahead = out_modes // 2
+    left = out_modes - shared.shape[1] - two.shape[1] - three.shape[1]
+    ahead = 5 * out_modes // TWELFTHS
     vmem = pl.BlockSpec(memory_space=pltpu.VMEM)
     anywhere = pl.BlockSpec(memory_space=pl.ANY)
     return pl.pallas_call(
@@ -263,7 +264,7 @@
         in_specs=[pl.BlockSpec(memory_space=pltpu.SMEM), vmem, vmem, anywhere] + [vmem] * 3,
         out_specs=(vmem, vmem, vmem),
         scratch_shapes=[
-            pltpu.VMEM((2, shared.shape[1]) + tensors.shape[2:], tensors.dtype),
+            pltpu.VMEM((2, left) + tensors.shape[2:], tensors.dtype),
             pltpu.SemaphoreType.DMA((2,)),
             pltpu.SemaphoreType.DMA((2,)),
         ],
@@ -427,13 +428,14 @@
 
 def local(fields, tensors, pair_table, plus_flux, minus_flux, face_limiter):
     groups = lax.axis_size("cell")
-    count = tensors.shape[1] // SIXTHS
+    count = tensors.shape[1] // TWELFTHS
     mine, held, token = fields, [], None
 
     def more():
         if not held:
-            return fetch_all(tensors, count)
-        return fetch_near(pair_table, mine, tensors, (2 * len(held) - 1) * count, 2 * count)
+            return fetch_all(tensors, 3 * count)
+        first = sum(part.shape[1] for part in held)
+        return fetch_near(pair_table, mine, tensors, first, (2 + len(held)) * count)
 
     bit = groups // 2
     while bit > 0:

time: 52.5 us -> 53.2 us (1.013)
    pallas_call x3, Pallas kernels: 12.4 us -> 13.2 us  [fetch(): pl.pallas_call(kernel, in_specs=specs + [pl.BlockSpec(memory_space=pl.ANY...]
  transfers between devices with their start and end apart: 7 -> 7, of which waited for: 2 -> 2; matrix products, arithmetic and copies ran while one was open for 0% -> 0% of each run, Pallas kernels for 41% -> 42%
where the time goes in v10:
time: 53.2 us; the launch traced here: 52.9 us
  Pallas kernels  32 us (60%)
  starting transfers between devices  13.7 us (26%)
  waiting for transfers between devices  6.41 us (12%)
  between operations  0.79 us (1%)
    pallas_call x3, Pallas kernels, fetch(): pl.pallas_call(kernel, in_specs=specs + [pl.BlockSpec(memory_space=pl.ANY...  13.2 us
    ppermute x6, starting transfers between devices, exchanged(): lax.ppermute(x, axis, [(i, i ^ bit) for i in range(lax.axis_size(axis))])  10.3 us
    pallas_call x1, Pallas kernels, collide_far(): pl.pallas_call(far_kernel, in_specs=[pl.BlockSpec(memory_space=pltpu.SMEM...  9.12 us
    pallas_call x1, Pallas kernels, collide_near(): pl.pallas_call(near_kernel, in_specs=[pl.BlockSpec(memory_space=pltpu.SME...  8.18 us
    all_to_all x1, waiting for transfers between devices, local(): lax.all_to_all(block, 'cell', split_axis=0, concat_axis=0, tiled=False)  6.02 us
    all_to_all x1, starting transfers between devices, local(): lax.all_to_all(block, 'cell', split_axis=0, concat_axis=0, tiled=False)  3.36 us
  transfers between devices with their start and end apart: 7, of which 2 were waited for; matrix products, arithmetic and copies ran while one was open for 0% of the time, Pallas kernels for 42%

profile of v10, /device:TPU:0, one launch (start us, length us, event | category | flops | bytes accessed | tf_op | source)
XLA Modules:
  0.0 52.9 jit_solution(11162268357633049677)
XLA Ops:
  0.6 0.0 copy-start.2
  0.6 0.0 copy-start.3
  0.6 4.1 %collective-permute-start = (bf16[1,32,384]{2,1,0:T(8,128)(2,1)}, bf16[1,32,384]{2,1,0:T(8,128)(2,1)S(1)}, u32[]{:S(2)}, u32[]{:S(2)}) collective-permute-start(bf16[1,32,384]{2,1,0:T(8,128)(2,1)} %fields.1), channel_id=1, source_target_pairs={{0,16},{4,20},{8,24},{12,28},{16,0},{20,4},{24,8},{28,12},{1,17},{... | collective-permute-start | bytes 73736 | tf_op jit(solution)/shard_map/ppermute | solution.py:426
  4.8 5.1 %fetch.3 = (bf16[4,12,384,384]{3,2,1,0:T(8,128)(2,1)S(1)}, f32[8,128]{1,0:T(8,128)S(1)}) custom-call(bf16[4,48,384,384]{3,2,1,0:T(8,128)(2,1)} %tensors.9), custom_call_target="tpu_custom_call" | custom-call | bytes 28311552 | tf_op jit(solution)/shard_map/fetch/pallas_call | solution.py:103
  9.9 0.0 collective-permute-done.came
  9.9 1.6 %collective-permute-start.1 = (bf16[2,32,384]{2,1,0:T(8,128)(2,1)S(1)}, bf16[2,32,384]{2,1,0:T(8,128)(2,1)S(1)}, u32[]{:S(2)}, u32[]{:S(2)}) collective-permute-start(bf16[2,32,384]{2,1,0:T(8,128)(2,1)S(1)} %join.3.after.here), channel_id=1, source_target_pairs={{0,8},{4,12},{8,0},{12,4},{16,24},{20,28},{24,16},{28,20},{1,9},{5... | collective-permute-start | bytes 147464 | tf_op jit(solution)/shard_map/ppermute | solution.py:426
  11.5 3.7 %fetch.4 = (bf16[2,12,384,384]{3,2,1,0:T(8,128)(2,1)S(1)}, f32[8,128]{1,0:T(8,128)S(1)}) custom-call(s32[4,4]{1,0:T(4,128)S(1)} %copy-done.3, bf16[2,32,384]{2,1,0:T(8,128)(2,1)S(1)} %join.3.after.here, bf16[4,48,384,384]{3,2,1,0:T(8,128)(2,1)} %tensors.9), custom_call_target="tpu_custom_call" | custom-call | bytes 14155776 | tf_op jit(solution)/shard_map/fetch/pallas_call | solution.py:103
  15.2 0.0 collective-permute-done.1.came
  15.3 1.6 %collective-permute-start.2 = (bf16[4,32,384]{2,1,0:T(8,128)(2,1)S(1)}, bf16[4,32,384]{2,1,0:T(8,128)(2,1)S(1)}, u32[]{:S(2)}, u32[]{:S(2)}) collective-permute-start(bf16[4,32,384]{2,1,0:T(8,128)(2,1)S(1)} %join.4.after.here), channel_id=1, source_target_pairs={{0,4},{4,0},{8,12},{12,8},{16,20},{20,16},{24,28},{28,24},{1,5},{5... | collective-permute-start | bytes 294920 | tf_op jit(solution)/shard_map/ppermute | solution.py:426
  16.8 4.4 %fetch.5 = (bf16[2,16,384,384]{3,2,1,0:T(8,128)(2,1)S(1)}, f32[8,128]{1,0:T(8,128)S(1)}) custom-call(s32[4,4]{1,0:T(4,128)S(1)} %copy-done.3, bf16[4,32,384]{2,1,0:T(8,128)(2,1)S(1)} %join.4.after.here, bf16[4,48,384,384]{3,2,1,0:T(8,128)(2,1)} %tensors.9), custom_call_target="tpu_custom_call" | custom-call | bytes 18874368 | tf_op jit(solution)/shard_map/fetch/pallas_call | solution.py:103
  21.2 0.0 collective-permute-done.2.came
  21.2 0.1 collective-permute-start.4
  21.3 1.6 %collective-permute-start.3 = (bf16[8,32,384]{2,1,0:T(8,128)(2,1)S(1)}, bf16[8,32,384]{2,1,0:T(8,128)(2,1)S(1)}, u32[]{:S(2)}, u32[]{:S(2)}) collective-permute-start(bf16[8,32,384]{2,1,0:T(8,128)(2,1)S(1)} %join.5.mine), channel_id=1, source_target_pairs={{0,2},{1,3},{2,0},{3,1},{4,6},{5,7},{6,4},{7,5},{8,10},{9,11},{10,... | collective-permute-start | bytes 589832 | tf_op jit(solution)/shard_map/ppermute | solution.py:426
  22.9 0.0 collective-permute-done.4.mate
  22.9 1.4 %collective-permute-start.5 = (bf16[8,32,384]{2,1,0:T(8,128)(2,1)S(1)}, bf16[8,32,384]{2,1,0:T(8,128)(2,1)S(1)}, u32[]{:S(2)}, u32[]{:S(2)}) collective-permute-start(bf16[8,32,384]{2,1,0:T(8,128)(2,1)S(1)} %collective-permute-done.4.mate), channel_id=1, source_target_pairs={{0,2},{1,3},{2,0},{3,1},{4,6},{5,7},{6,4},{7,5},{8,10},{9,11},{10,... | collective-permute-start | bytes 589832 | tf_op jit(solution)/shard_map/ppermute | solution.py:426
  24.3 8.2 %collide_near.1 = (f32[48,256]{1,0:T(8,128)S(1)}, f32[384,256]{1,0:T(8,128)S(1)}, bf16[2,20,384,384]{3,2,1,0:T(8,128)(2,1)S(1)}) custom-call(s32[4,4]{1,0:T(4,128)S(1)} %copy-done.3, bf16[8,32,384]{2,1,0:T(8,128)(2,1)S(1)} %join.5.mine, bf16[8,32,384]{2,1,0:T(8,128)(2,1)S(1)} %collective-permute-done.4.mate, bf16[4,48,384,384]{3,2,1,0:T(8,128)(2,1)} %tensors.9, ...), custom_call_target="tpu_custom_call" | custom-call | flops 7247757312 | bytes 28311552 | tf_op jit(solution)/shard_map/collide_near/pallas_call | solution.py:262
  32.4 0.0 collective-permute-done.3.one
  32.5 0.4 collective-permute-done.5.two
  32.9 9.1 %collide_far.1 = f32[8,16,128]{2,1,0:T(8,128)} custom-call(s32[4,4]{1,0:T(4,128)S(1)} %copy-done.3, bf16[8,32,384]{2,1,0:T(8,128)(2,1)S(1)} %collective-permute-done.3.one, bf16[8,32,384]{2,1,0:T(8,128)(2,1)S(1)} %collective-permute-done.5.two, bf16[4,48,384,384]{3,2,1,0:T(8,128)(2,1)} %tensors.9, bf16[4,12,384,384]{3,2,1,0:T(8,128)(2,1)S(1)} %get-tuple-element.14.shared, ...), custom_call_target="tpu_custom_call" | custom-call | flops 7247757312 | bytes 28311552 | tf_op jit(solution)/shard_map/collide_far/pallas_call | solution.py:314
  42.0 3.4 %all-to-all-start = ((f32[8,16,128]{2,1,0:T(8,128)}), f32[8,16,128]{2,1,0:T(8,128)S(1)}, u32[]{:S(2)}, u32[]{:S(2)}) async-start(f32[8,16,128]{2,1,0:T(8,128)} %collide_far.1), calls=%async_computation | async-start | bytes 131072 | tf_op jit(solution)/shard_map/all_to_all | solution.py:457
  45.3 0.0 copy-done
  45.4 0.8 %transport.1.flux = f32[40,384]{1,0:T(8,128)S(1)} custom-call(bf16[8,32,384]{2,1,0:T(8,128)(2,1)S(1)} %join.5.mine, s32[1,32]{1,0:T(1,128)S(1)} %copy-done.4, f32[1,384,384]{2,1,0:T(8,128)S(1)} %copy-done, f32[1,384,384]{2,1,0:T(8,128)S(1)} %copy-done.1), custom_call_target="tpu_custom_call" | custom-call | tf_op jit(solution)/shard_map/transport/pallas_call | solution.py:383
  46.2 6.0 %all-to-all-done.received = f32[8,16,128]{2,1,0:T(8,128)S(1)} async-done(((f32[8,16,128]{2,1,0:T(8,128)}), f32[8,16,128]{2,1,0:T(8,128)S(1)}, u32[]{:S(2)}, u32[]{:S(2)}) %all-to-all-start) | async-done | bytes 65568 | tf_op jit(solution)/shard_map/all_to_all | solution.py:457
  52.2 0.7 %finish.1 = (f32[1,32,384]{2,1,0:T(8,128)}, f32[1,32,384]{2,1,0:T(8,128)}) custom-call(f32[8,16,128]{2,1,0:T(8,128)S(1)} %all-to-all-done.received, f32[40,384]{1,0:T(8,128)S(1)} %transport.1.flux, bf16[1,32,384]{2,1,0:T(8,128)(2,1)S(1)} %copy-done.2), custom_call_target="tpu_custom_call" | custom-call | tf_op jit(solution)/shard_map/finish/pallas_call | solution.py:415
  (10 shorter events, 0.1 us)
Async XLA Ops:
  0.6 9.2 %copy-start.2 = (bf16[1,32,384]{2,1,0:T(8,128)(2,1)S(1)}, bf16[1,32,384]{2,1,0:T(8,128)(2,1)}, u32[]{:S(2)}) copy-start(bf16[1,32,384]{2,1,0:T(8,128)(2,1)} %fields.1) | copy-start | bytes 73732
  0.6 10.9 %copy-start.3 = (s32[4,4]{1,0:T(4,128)S(1)}, s32[4,4]{1,0:T(4,128)}, u32[]{:S(2)}) copy-start(s32[4,4]{1,0:T(4,128)} %table.7) | copy-start | bytes 196
  0.6 9.2 %collective-permute-start = (bf16[1,32,384]{2,1,0:T(8,128)(2,1)}, bf16[1,32,384]{2,1,0:T(8,128)(2,1)S(1)}, u32[]{:S(2)}, u32[]{:S(2)}) collective-permute-start(bf16[1,32,384]{2,1,0:T(8,128)(2,1)} %fields.1), channel_id=1, source_target_pairs={{0,16},{4,20},{8,24},{12,28},{16,0},{20,4},{24,8},{28,12},{1,17},{... | collective-permute-start | bytes 73736 | tf_op jit(solution)/shard_map/ppermute | solution.py:426
  9.9 5.3 %collective-permute-start.1 = (bf16[2,32,384]{2,1,0:T(8,128)(2,1)S(1)}, bf16[2,32,384]{2,1,0:T(8,128)(2,1)S(1)}, u32[]{:S(2)}, u32[]{:S(2)}) collective-permute-start(bf16[2,32,384]{2,1,0:T(8,128)(2,1)S(1)} %join.3.after.here), channel_id=1, source_target_pairs={{0,8},{4,12},{8,0},{12,4},{16,24},{20,28},{24,16},{28,20},{1,9},{5... | collective-permute-start | bytes 147464 | tf_op jit(solution)/shard_map/ppermute | solution.py:426
  15.3 5.9 %collective-permute-start.2 = (bf16[4,32,384]{2,1,0:T(8,128)(2,1)S(1)}, bf16[4,32,384]{2,1,0:T(8,128)(2,1)S(1)}, u32[]{:S(2)}, u32[]{:S(2)}) collective-permute-start(bf16[4,32,384]{2,1,0:T(8,128)(2,1)S(1)} %join.4.after.here), channel_id=1, source_target_pairs={{0,4},{4,0},{8,12},{12,8},{16,20},{20,16},{24,28},{28,24},{1,5},{5... | collective-permute-start | bytes 294920 | tf_op jit(solution)/shard_map/ppermute | solution.py:426
  21.2 1.7 %collective-permute-start.4 = (bf16[8,32,384]{2,1,0:T(8,128)(2,1)S(1)}, bf16[8,32,384]{2,1,0:T(8,128)(2,1)S(1)}, u32[]{:S(2)}, u32[]{:S(2)}) collective-permute-start(bf16[8,32,384]{2,1,0:T(8,128)(2,1)S(1)} %join.5.mine), channel_id=1, source_target_pairs={{0,1},{1,0},{2,3},{3,2},{4,5},{5,4},{6,7},{7,6},{8,9},{9,8},{10,11... | collective-permute-start | bytes 589832 | tf_op jit(solution)/shard_map/ppermute | solution.py:426
  21.3 11.1 %collective-permute-start.3 = (bf16[8,32,384]{2,1,0:T(8,128)(2,1)S(1)}, bf16[8,32,384]{2,1,0:T(8,128)(2,1)S(1)}, u32[]{:S(2)}, u32[]{:S(2)}) collective-permute-start(bf16[8,32,384]{2,1,0:T(8,128)(2,1)S(1)} %join.5.mine), channel_id=1, source_target_pairs={{0,2},{1,3},{2,0},{3,1},{4,6},{5,7},{6,4},{7,5},{8,10},{9,11},{10,... | collective-permute-start | bytes 589832 | tf_op jit(solution)/shard_map/ppermute | solution.py:426
  22.9 9.9 %collective-permute-start.5 = (bf16[8,32,384]{2,1,0:T(8,128)(2,1)S(1)}, bf16[8,32,384]{2,1,0:T(8,128)(2,1)S(1)}, u32[]{:S(2)}, u32[]{:S(2)}) collective-permute-start(bf16[8,32,384]{2,1,0:T(8,128)(2,1)S(1)} %collective-permute-done.4.mate), channel_id=1, source_target_pairs={{0,2},{1,3},{2,0},{3,1},{4,6},{5,7},{6,4},{7,5},{8,10},{9,11},{10,... | collective-permute-start | bytes 589832 | tf_op jit(solution)/shard_map/ppermute | solution.py:426
  24.3 8.6 %copy-start.4 = (s32[1,32]{1,0:T(1,128)S(1)}, s32[1,32]{1,0:T(1,128)}, u32[]{:S(2)}) copy-start(s32[1,32]{1,0:T(1,128)} %limiter.3) | copy-start | bytes 388
  32.8 12.5 %copy-start = (f32[1,384,384]{2,1,0:T(8,128)S(1)}, f32[1,384,384]{2,1,0:T(8,128)}, u32[]{:S(2)}) copy-start(f32[1,384,384]{2,1,0:T(8,128)} %plus.1) | copy-start | bytes 1769476
  32.8 12.5 %copy-start.1 = (f32[1,384,384]{2,1,0:T(8,128)S(1)}, f32[1,384,384]{2,1,0:T(8,128)}, u32[]{:S(2)}) copy-start(f32[1,384,384]{2,1,0:T(8,128)} %minus.1) | copy-start | bytes 1769476
  42.0 10.2 %all-to-all-start = ((f32[8,16,128]{2,1,0:T(8,128)}), f32[8,16,128]{2,1,0:T(8,128)S(1)}, u32[]{:S(2)}, u32[]{:S(2)}) async-start(f32[8,16,128]{2,1,0:T(8,128)} %collide_far.1), calls=%async_computation | async-start | bytes 131072 | tf_op jit(solution)/shard_map/all_to_all | solution.py:457
